TPU v7x, 32 devices: a whole 2x2x4 slice. The times are simulated.
32 devices in a mesh: wide: 8 (over y, x, core), narrow: 4 (over z).
Axes of the slice: x: 2, y: 2, z: 4, core: 2. Of those that a mesh axis runs over, the one named last changes fastest.
Arguments:
- tokens: bfloat16 [768, 24576], P('narrow', 'wide'), may hold values from -6 to 6
- lengths: int32 [192], P('wide'), may hold values from 64 to 128
- masked: int32 [192, 128], P('wide'), may hold values 0 or 1
- cotangent: bfloat16 [768, 24576], P('narrow', 'wide'), may hold values from -6 to 6
- mask_vector: float32 [768], P('narrow'), may hold values from -4 to 4
- gain_one: float32 [2, 768], P(None, 'narrow'), may hold values from 0.5 to 1.5
- in_first: bfloat16 [2, 4, 73728], P(None, 'narrow'), may hold values from -0.4375 to 0.4375
- in_second: bfloat16 [2, 4, 147456], P(None, 'narrow'), may hold values from -0.3125 to 0.3125
- short_taps: float32 [2, 3, 4, 384], P(None, None, 'narrow'), may hold values from -3.5 to 3.5
- skip_gain: float32 [2, 768], P(None, 'narrow'), may hold values from -4 to 4
- decay_rates: float32 [2, 768], P(None, 'narrow'), may hold values from 0.00390625 to 0.03125
- filter_one: float32 [2, 5, 128], replicated, may hold values from -2.5 to 2.5
- filter_bias: float32 [2, 128], replicated, may hold values from -3.140625 to 3.140625
- filter_two: float32 [2, 128, 128], replicated, may hold values from -0.5 to 0.5
- filter_three: float32 [2, 768, 128], P(None, 'narrow'), may hold values from -0.5 to 0.5
- out_first: bfloat16 [2, 4, 36864], P(None, 'narrow'), may hold values from -0.4375 to 0.4375
- out_second: bfloat16 [2, 4, 36864], P(None, 'narrow'), may hold values from -0.4375 to 0.4375
- gain_two: float32 [2, 768], P(None, 'narrow'), may hold values from 0.5 to 1.5
- up_first: bfloat16 [2, 4, 36864], P(None, 'narrow'), may hold values from -0.4375 to 0.4375
- up_second: bfloat16 [2, 4, 294912], P(None, 'narrow'), may hold values from -0.4375 to 0.4375
- down_first: bfloat16 [2, 4, 147456], P(None, 'narrow'), may hold values from -0.21875 to 0.21875
- down_second: bfloat16 [2, 4, 36864], P(None, 'narrow'), may hold values from -0.4375 to 0.4375
Outputs:
- mixed_out: bfloat16 [768, 24576], P('narrow', 'wide')
- grad_tokens: float32 [768, 24576], P('narrow', 'wide')
- grad_mask_vector: float32 [768], P('narrow')
- grad_gain_one: float32 [2, 768], P(None, 'narrow')
- grad_in_first: float32 [2, 4, 73728], P(None, 'narrow')
- grad_in_second: float32 [2, 4, 147456], P(None, 'narrow')
- grad_short_taps: float32 [2, 3, 4, 384], P(None, None, 'narrow')
- grad_skip_gain: float32 [2, 768], P(None, 'narrow')
- grad_decay_rates: float32 [2, 768], P(None, 'narrow')
- grad_filter_one: float32 [2, 5, 128], replicated
- grad_filter_bias: float32 [2, 128], replicated
- grad_filter_two: float32 [2, 128, 128], replicated
- grad_filter_three: float32 [2, 768, 128], P(None, 'narrow')
- grad_out_first: float32 [2, 4, 36864], P(None, 'narrow')
- grad_out_second: float32 [2, 4, 36864], P(None, 'narrow')
- grad_gain_two: float32 [2, 768], P(None, 'narrow')
- grad_up_first: float32 [2, 4, 36864], P(None, 'narrow')
- grad_up_second: float32 [2, 4, 294912], P(None, 'narrow')
- grad_down_first: float32 [2, 4, 147456], P(None, 'narrow')
- grad_down_second: float32 [2, 4, 36864], P(None, 'narrow')
Inputs may be any that keep to these rules, and one draw needn't show every extreme that they name: lengths[s] positions of sequence s are real tokens; the others are padding. 1 marks a masked position.
All inputs are finite; a program needn't handle non-finite values. No bound on the sum of `masked` on one device may be relied on, other than what follows from the above.
Results may differ from a plain program's by a relative error of at most 0.025.
Values may be sent and summed in bfloat16 or wider, within the bound.
No kernel may reach another device: no remote copies, remote signals or barrier semaphores. Data moves between devices by JAX's collectives and lax.ppermute only.
A program may use at most 384 MiB of HBM per device.

v0:
```python
import math

import jax
import jax.numpy as jnp
from jax import lax
from jax.sharding import PartitionSpec as P

D = 768
LENGTH = 128
LAYERS = 2
BLOCK_W = 192
FF_BLOCK = 768


epsilon = 1e-05
highest = lax.Precision.HIGHEST


def mat_mul(left_in, right_in):
    return jnp.dot(left_in, right_in, preferred_element_type=jnp.float32)


def mat_tn(left_in, right_in):
    return lax.dot_general(
        left_in, right_in, (((0,), (0,)), ((), ())), preferred_element_type=jnp.float32
    )


def mat_nt(left_in, right_in):
    return lax.dot_general(
        left_in, right_in, (((1,), (1,)), ((), ())), preferred_element_type=jnp.float32
    )


def blocks_ahead(normed, factor_one, factor_two):
    blocks = lax.axis_size("narrow")
    middle = mat_mul(normed, factor_one).astype(jnp.bfloat16)
    tok_rows, inner_width = middle.shape
    middle = middle.reshape(tok_rows, blocks, inner_width // blocks)
    arrived = lax.all_to_all(middle, "narrow", split_axis=1, concat_axis=1, tiled=True)
    flat_rows = arrived.reshape(arrived.shape[0], inner_width)
    return (flat_rows, mat_mul(flat_rows, factor_two))


def blocks_back(grad_out, normed, kept_rows, factor_one, factor_two):
    blocks = lax.axis_size("narrow")
    grad_two = mat_tn(kept_rows, grad_out)
    grad_mid = mat_nt(grad_out, factor_two).astype(jnp.bfloat16)
    tok_rows, inner_width = grad_mid.shape
    grad_mid = grad_mid.reshape(tok_rows, blocks, inner_width // blocks)
    arrived = lax.all_to_all(grad_mid, "narrow", split_axis=1, concat_axis=1, tiled=True)
    flat_rows = arrived.reshape(arrived.shape[0], inner_width)
    grad_in = mat_nt(flat_rows, factor_one)
    grad_one = mat_tn(normed, flat_rows)
    return (grad_in, grad_one, grad_two)


def norm_ahead(row_block, gain_row):
    row_sums, squares = lax.psum(
        (
            jnp.sum(row_block, axis=1, keepdims=True),
            jnp.sum(row_block * row_block, axis=1, keepdims=True),
        ),
        "narrow",
    )
    average = row_sums / D
    inv_scale = lax.rsqrt(squares / D - average * average + epsilon)
    standard = (row_block - average) * inv_scale
    return (standard, inv_scale, (standard * gain_row).astype(jnp.bfloat16))


def norm_back(grad_norm, standard, inv_scale, gain_row):
    weighted = grad_norm * gain_row
    plain_sum, cross_sum = lax.psum(
        (
            jnp.sum(weighted, axis=1, keepdims=True),
            jnp.sum(weighted * standard, axis=1, keepdims=True),
        ),
        "narrow",
    )
    grad_rows = inv_scale * (weighted - plain_sum / D - standard * cross_sum / D)
    return (grad_rows, jnp.sum(grad_norm * standard, axis=0))


def filter_table(weight_one, bias_one, weight_two, weight_three, decay_rate):
    lag_values = jnp.arange(-(LENGTH - 1), LENGTH).astype(jnp.float32)
    relative = lag_values / LENGTH
    features = jnp.stack(
        [
            relative,
            jnp.cos(math.pi * relative),
            jnp.sin(math.pi * relative),
            jnp.cos(37.0 * math.pi * relative),
            jnp.sin(37.0 * math.pi * relative),
        ],
        axis=1,
    )
    hidden_one = jnp.sin(jnp.dot(features, weight_one, precision=highest) + bias_one)
    hidden_two = jnp.sin(jnp.dot(hidden_one, weight_two, precision=highest))
    shaped = jnp.dot(hidden_two, weight_three.T, precision=highest)
    envelope = jnp.exp(-jnp.abs(lag_values)[:, None] * decay_rate[None, :])
    return shaped * envelope / math.sqrt(LENGTH)


def toeplitz_table(kernel):
    channels = kernel.shape[1]
    flipped = jnp.concatenate([kernel[::-1].T, jnp.zeros((channels, 1), kernel.dtype)], axis=1)
    repeated = jnp.tile(flipped, (1, LENGTH))
    window = repeated[:, LENGTH - 1 : LENGTH - 1 + LENGTH * (2 * LENGTH - 1)]
    return window.reshape(channels, LENGTH, 2 * LENGTH - 1)[:, :, :LENGTH]


def filter_parts(weight_one, bias_one, weight_two, weight_three, decay_rate):
    kernel = filter_table(weight_one, bias_one, weight_two, weight_three, decay_rate)
    return (toeplitz_table(kernel), kernel)


def glu_value(gate_in, up_in):
    return jax.nn.gelu(gate_in) * up_in


def layer_ahead(row_block, padding, weights, toeplitz):
    (
        gain_one,
        in_first,
        in_second,
        short_taps,
        skip_gain,
        out_first,
        out_second,
        gain_two,
        up_first,
        up_second,
        down_first,
        down_second,
    ) = weights
    seq_count = padding.shape[0]
    width_here = skip_gain.shape[0]
    ff_width = down_first.shape[0]
    std_one, inv_one, normed_one = norm_ahead(row_block, gain_one)
    kept_one, projected = blocks_ahead(normed_one, in_first, in_second)
    projected = projected.reshape(seq_count, LENGTH, 2 * width_here) * padding[:, :, None]
    padded = jnp.pad(projected, ((0, 0), (1, 1), (0, 0)))
    smoothed = (
        short_taps[0] * padded[:, :-2]
        + short_taps[1] * padded[:, 1:-1]
        + short_taps[2] * padded[:, 2:]
    )
    signal = smoothed[:, :, :width_here]
    gating = smoothed[:, :, width_here:]
    convolved = jnp.einsum("cts,nsc->ntc", toeplitz, signal, precision=highest) + skip_gain * signal
    gated_rows = (convolved * gating).reshape(-1, width_here).astype(jnp.bfloat16)
    kept_two, mixed_rows = blocks_ahead(gated_rows, out_first, out_second)
    middle = row_block + mixed_rows
    std_two, inv_two, normed_two = norm_ahead(middle, gain_two)
    kept_three, gate_up = blocks_ahead(normed_two, up_first, up_second)
    activated = glu_value(gate_up[:, :ff_width], gate_up[:, ff_width:]).astype(jnp.bfloat16)
    kept_four, down_rows = blocks_ahead(activated, down_first, down_second)
    saved_state = (
        std_one,
        inv_one,
        normed_one,
        kept_one,
        padded,
        signal,
        gating,
        convolved,
        gated_rows,
        kept_two,
        std_two,
        inv_two,
        normed_two,
        kept_three,
        gate_up,
        activated,
        kept_four,
    )
    return (middle + down_rows, saved_state)


def layer_back(grad_top, padding, weights, toeplitz, saved_state):
    (
        gain_one,
        in_first,
        in_second,
        short_taps,
        skip_gain,
        out_first,
        out_second,
        gain_two,
        up_first,
        up_second,
        down_first,
        down_second,
    ) = weights
    (
        std_one,
        inv_one,
        normed_one,
        kept_one,
        padded,
        signal,
        gating,
        convolved,
        gated_rows,
        kept_two,
        std_two,
        inv_two,
        normed_two,
        kept_three,
        gate_keep,
        activated,
        kept_four,
    ) = saved_state
    seq_count = padding.shape[0]
    width_here = skip_gain.shape[0]
    ff_width = down_first.shape[0]
    grad_act, grad_down_first, grad_down_second = blocks_back(
        grad_top.astype(jnp.bfloat16), activated, kept_four, down_first, down_second
    )
    glu_out, glu_pull = jax.vjp(glu_value, gate_keep[:, :ff_width], gate_keep[:, ff_width:])
    grad_gate, grad_up = glu_pull(grad_act)
    grad_gate_up = jnp.concatenate([grad_gate, grad_up], axis=1).astype(jnp.bfloat16)
    grad_normed_two, grad_up_first, grad_up_second = blocks_back(
        grad_gate_up, normed_two, kept_three, up_first, up_second
    )
    grad_norm_two, grad_gain_two = norm_back(grad_normed_two, std_two, inv_two, gain_two)
    grad_middle = grad_top + grad_norm_two
    grad_gated, grad_out_first, grad_out_second = blocks_back(
        grad_middle.astype(jnp.bfloat16), gated_rows, kept_two, out_first, out_second
    )
    grad_gated = grad_gated.reshape(seq_count, LENGTH, width_here)
    grad_conv = grad_gated * gating
    grad_gating = grad_gated * convolved
    grad_signal = (
        jnp.einsum("cts,ntc->nsc", toeplitz, grad_conv, precision=highest) + skip_gain * grad_conv
    )
    grad_skip = jnp.sum(grad_conv * signal, axis=(0, 1))
    grad_toeplitz = jnp.einsum("ntc,nsc->cts", grad_conv, signal, precision=highest)
    grad_smooth = jnp.concatenate([grad_signal, grad_gating], axis=2)
    shifted = jnp.pad(grad_smooth, ((0, 0), (1, 1), (0, 0)))
    grad_projected = (
        short_taps[0] * shifted[:, 2:]
        + short_taps[1] * shifted[:, 1:-1]
        + short_taps[2] * shifted[:, :-2]
    )
    grad_taps = jnp.stack(
        [
            jnp.sum(grad_smooth * padded[:, tap_at : tap_at + LENGTH], axis=(0, 1))
            for tap_at in range(3)
        ]
    )
    grad_projected = (
        (grad_projected * padding[:, :, None]).reshape(-1, 2 * width_here).astype(jnp.bfloat16)
    )
    grad_normed_one, grad_in_first, grad_in_second = blocks_back(
        grad_projected, normed_one, kept_one, in_first, in_second
    )
    grad_norm_one, grad_gain_one = norm_back(grad_normed_one, std_one, inv_one, gain_one)
    local_grads = (
        grad_gain_one,
        grad_in_first,
        grad_in_second,
        grad_taps,
        grad_skip,
        grad_out_first,
        grad_out_second,
        grad_gain_two,
        grad_up_first,
        grad_up_second,
        grad_down_first,
        grad_down_second,
    )
    return (grad_middle + grad_norm_one, grad_toeplitz, local_grads)


def pick_layer(layer_at, arrays):
    (
        gain_one,
        in_first,
        in_second,
        short_taps,
        skip_gain,
        out_first,
        out_second,
        gain_two,
        up_first,
        up_second,
        down_first,
        down_second,
    ) = arrays
    return (
        gain_one[layer_at],
        in_first[layer_at, 0].reshape(BLOCK_W, 2 * BLOCK_W),
        in_second[layer_at, 0].reshape(2 * BLOCK_W, 2 * BLOCK_W),
        short_taps[layer_at, :, 0],
        skip_gain[layer_at],
        out_first[layer_at, 0].reshape(BLOCK_W, BLOCK_W),
        out_second[layer_at, 0].reshape(BLOCK_W, BLOCK_W),
        gain_two[layer_at],
        up_first[layer_at, 0].reshape(BLOCK_W, BLOCK_W),
        up_second[layer_at, 0].reshape(BLOCK_W, 2 * FF_BLOCK),
        down_first[layer_at, 0].reshape(FF_BLOCK, BLOCK_W),
        down_second[layer_at, 0].reshape(BLOCK_W, BLOCK_W),
    )


def flatten_factor(stacked_grad):
    return stacked_grad.reshape(stacked_grad.shape[0], 1, -1)


def local(
    tokens,
    lengths,
    masked,
    cotangent,
    mask_vector,
    gain_one,
    in_first,
    in_second,
    short_taps,
    skip_gain,
    decay_rates,
    filter_one,
    filter_bias,
    filter_two,
    filter_three,
    out_first,
    out_second,
    gain_two,
    up_first,
    up_second,
    down_first,
    down_second,
):
    wide_count = lax.axis_size("wide")
    positions = jnp.arange(LENGTH, dtype=jnp.int32)
    padding = (positions[None, :] < lengths[:, None]).astype(jnp.float32)
    chosen = masked.reshape(-1, 1).astype(jnp.float32)
    penalty_coef = 4.0 * math.sqrt(chosen.shape[0] * wide_count) / wide_count
    arrays = (
        gain_one,
        in_first,
        in_second,
        short_taps,
        skip_gain,
        out_first,
        out_second,
        gain_two,
        up_first,
        up_second,
        down_first,
        down_second,
    )
    row_block = tokens.astype(jnp.float32).T * (1.0 - chosen) + chosen * mask_vector[None, :]
    pulls = []
    tables = []
    kernels = []
    states = []
    for layer_at in range(LAYERS):
        (toeplitz, kernel), pull_back = jax.vjp(
            filter_parts,
            filter_one[layer_at],
            filter_bias[layer_at],
            filter_two[layer_at],
            filter_three[layer_at],
            decay_rates[layer_at],
        )
        pulls.append(pull_back)
        tables.append(toeplitz)
        kernels.append(kernel)
        row_block, saved_state = layer_ahead(
            row_block, padding, pick_layer(layer_at, arrays), toeplitz
        )
        states.append(saved_state)
    mixed_out = row_block.T.astype(jnp.bfloat16)
    grad_rows = cotangent.astype(jnp.float32).T
    summed = [None] * LAYERS
    filter_grads = [None] * LAYERS
    mask_total = None
    for layer_at in reversed(range(LAYERS)):
        grad_rows, grad_toeplitz, local_grads = layer_back(
            grad_rows, padding, pick_layer(layer_at, arrays), tables[layer_at], states[layer_at]
        )
        grad_filt_one, grad_filt_bias, grad_filt_two, grad_filt_three, grad_rate = pulls[layer_at](
            (grad_toeplitz, penalty_coef * kernels[layer_at])
        )
        filter_grads[layer_at] = lax.psum(
            (grad_filt_one, grad_filt_bias, grad_filt_two), ("wide", "narrow")
        )
        (
            grad_gain_one,
            grad_in_first,
            grad_in_second,
            grad_taps,
            grad_skip,
            grad_out_first,
            grad_out_second,
            grad_gain_two,
            grad_up_first,
            grad_up_second,
            grad_down_first,
            grad_down_second,
        ) = local_grads
        if layer_at > 0:
            summed[layer_at] = (
                lax.psum(grad_gain_one.astype(jnp.bfloat16), "wide").astype(jnp.float32),
                lax.psum(grad_in_first.astype(jnp.bfloat16), "wide").astype(jnp.float32),
                lax.psum(grad_in_second.astype(jnp.bfloat16), "wide").astype(jnp.float32),
                lax.psum(grad_taps.astype(jnp.bfloat16), "wide").astype(jnp.float32),
                lax.psum(grad_skip.astype(jnp.bfloat16), "wide").astype(jnp.float32),
                lax.psum(grad_rate.astype(jnp.bfloat16), "wide").astype(jnp.float32),
                lax.psum(grad_filt_three.astype(jnp.bfloat16), "wide").astype(jnp.float32),
                lax.psum(grad_out_first.astype(jnp.bfloat16), "wide").astype(jnp.float32),
                lax.psum(grad_out_second.astype(jnp.bfloat16), "wide").astype(jnp.float32),
                lax.psum(grad_gain_two.astype(jnp.bfloat16), "wide").astype(jnp.float32),
                lax.psum(grad_up_first.astype(jnp.bfloat16), "wide").astype(jnp.float32),
                lax.psum(grad_up_second.astype(jnp.bfloat16), "wide").astype(jnp.float32),
                lax.psum(grad_down_first.astype(jnp.bfloat16), "wide").astype(jnp.float32),
                lax.psum(grad_down_second.astype(jnp.bfloat16), "wide").astype(jnp.float32),
            )
        else:
            mask_local = jnp.sum(chosen * grad_rows, axis=0)
            summed_low = (
                lax.psum(grad_gain_one.astype(jnp.bfloat16), "wide").astype(jnp.float32),
                lax.psum(grad_in_first.astype(jnp.bfloat16), "wide").astype(jnp.float32),
                lax.psum(grad_in_second.astype(jnp.bfloat16), "wide").astype(jnp.float32),
                lax.psum(grad_taps.astype(jnp.bfloat16), "wide").astype(jnp.float32),
                lax.psum(grad_skip.astype(jnp.bfloat16), "wide").astype(jnp.float32),
                lax.psum(grad_rate.astype(jnp.bfloat16), "wide").astype(jnp.float32),
                lax.psum(grad_filt_three.astype(jnp.bfloat16), "wide").astype(jnp.float32),
                lax.psum(grad_out_first.astype(jnp.bfloat16), "wide").astype(jnp.float32),
                lax.psum(grad_out_second.astype(jnp.bfloat16), "wide").astype(jnp.float32),
                lax.psum(grad_gain_two.astype(jnp.bfloat16), "wide").astype(jnp.float32),
                lax.psum(grad_up_first.astype(jnp.bfloat16), "wide").astype(jnp.float32),
                lax.psum(grad_up_second.astype(jnp.bfloat16), "wide").astype(jnp.float32),
                lax.psum(grad_down_first.astype(jnp.bfloat16), "wide").astype(jnp.float32),
                lax.psum(grad_down_second.astype(jnp.bfloat16), "wide").astype(jnp.float32),
                lax.psum(mask_local.astype(jnp.bfloat16), "wide").astype(jnp.float32),
            )
            summed[layer_at] = summed_low[:14]
            mask_total = summed_low[14]
    layered = [
        jnp.stack([summed[layer_at][member] for layer_at in range(LAYERS)]) for member in range(14)
    ]
    filt_stack = [
        jnp.stack([filter_grads[layer_at][member] for layer_at in range(LAYERS)])
        for member in range(3)
    ]
    grad_tokens = (grad_rows * (1.0 - chosen)).T
    return (
        mixed_out,
        grad_tokens,
        mask_total,
        layered[0],
        flatten_factor(layered[1]),
        flatten_factor(layered[2]),
        layered[3][:, :, None],
        layered[4],
        layered[5],
        filt_stack[0],
        filt_stack[1],
        filt_stack[2],
        layered[6],
        flatten_factor(layered[7]),
        flatten_factor(layered[8]),
        layered[9],
        flatten_factor(layered[10]),
        flatten_factor(layered[11]),
        flatten_factor(layered[12]),
        flatten_factor(layered[13]),
    )


def solution(mesh):
    placed = (
        P("narrow", "wide"),
        P("wide"),
        P("wide", None),
        P("narrow", "wide"),
        P("narrow"),
        P(None, "narrow"),
        P(None, "narrow", None),
        P(None, "narrow", None),
        P(None, None, "narrow", None),
        P(None, "narrow"),
        P(None, "narrow"),
        P(),
        P(),
        P(),
        P(None, "narrow", None),
        P(None, "narrow", None),
        P(None, "narrow", None),
        P(None, "narrow"),
        P(None, "narrow", None),
        P(None, "narrow", None),
        P(None, "narrow", None),
        P(None, "narrow", None),
    )
    return jax.shard_map(
        local,
        mesh=mesh,
        in_specs=placed,
        out_specs=(
            P("narrow", "wide"),
            P("narrow", "wide"),
            P("narrow"),
            P(None, "narrow"),
            P(None, "narrow", None),
            P(None, "narrow", None),
            P(None, None, "narrow", None),
            P(None, "narrow"),
            P(None, "narrow"),
            P(),
            P(),
            P(),
            P(None, "narrow", None),
            P(None, "narrow", None),
            P(None, "narrow", None),
            P(None, "narrow"),
            P(None, "narrow", None),
            P(None, "narrow", None),
            P(None, "narrow", None),
            P(None, "narrow", None),
        ),
        check_vma=False,
    )
```

profile of v0, /device:TPU:0, one launch (start us, length us, event | category | flops | bytes accessed | tf_op | source)
XLA Modules:
  0.0 1625.4 jit_solution(4461203415096790626)
XLA Ops:
  16.3 20.7 %all-reduce.19 = (f32[3072,1]{0,1:T(1,128)S(1)}, f32[3072,1]{0,1:T(1,128)S(1)}) all-reduce(f32[3072,1]{0,1:T(1,128)S(1)} %bitcast.496, f32[3072,1]{0,1:T(1,128)S(1)} %bitcast.495), channel_id=1, replica_groups=mesh['wide'=8,'narrow'=4] {'narrow'}, use_global_device_ids=true, to_apply=%region_3.0 | all-reduce | flops 6144 | bytes 49152 | tf_op jit(solution)/shard_map/psum | solution.py:59
  85.2 22.3 %copy.148 = f32[24,8,128,256]{3,1,2,0:T(8,128)S(1)} copy(f32[24,8,128,256]{3,2,1,0:T(8,128)} %bitcast.387) | data formatting | bytes 50331648
  118.4 42.0 %reshape.354 = f32[192,128,255]{2,1,0:T(8,128)} reshape(f32[192,32640]{1,0:T(8,128)} %slice.291) | data formatting | bytes 50135040 | tf_op jit(solution)/shard_map/jvp()/reshape | solution.py:110
  180.8 23.8 %fusion.6 = f32[192,24,128]{2,1,0:T(8,128)} fusion(f32[24,128,192]{1,0,2:T(8,128)S(1)} %copy.116, f32[192,128,255]{2,1,0:T(8,128)} %reshape.354), kind=kOutput, calls=%fused_computation.12 | convolution fusion | flops 905969664 | bytes 17301504 | tf_op jit(solution)/shard_map/cts,nsc->ntc/dot_general | solution.py:151
  225.9 19.6 %all-to-all-done.1 = bf16[3072,4,48]{0,2,1:T(8,128)(2,1)S(1)} async-done(((bf16[3072,4,48]{0,2,1:T(8,128)(2,1)}), bf16[3072,4,48]{0,2,1:T(8,128)(2,1)S(1)}, u32[]{:S(2)}, u32[]{:S(2)}) %all-to-all-start.1) | async-done | bytes 1179680 | tf_op jit(solution)/shard_map/all_to_all | solution.py:40
  382.8 22.1 %copy.150 = f32[24,8,128,256]{3,1,2,0:T(8,128)S(1)} copy(f32[24,8,128,256]{3,2,1,0:T(8,128)} %bitcast.388) | data formatting | bytes 50331648
  415.7 42.1 %reshape.362 = f32[192,128,255]{2,1,0:T(8,128)} reshape(f32[192,32640]{1,0:T(8,128)} %slice.297) | data formatting | bytes 50135040 | tf_op jit(solution)/shard_map/jvp()/reshape | solution.py:110
  471.3 22.9 %fusion.2 = f32[192,24,128]{2,1,0:T(8,128)} fusion(f32[24,128,192]{1,0,2:T(8,128)S(1)} %copy.120, f32[192,128,255]{2,1,0:T(8,128)} %reshape.362), kind=kOutput, calls=%fused_computation.8 | convolution fusion | flops 905969664 | bytes 17301504 | tf_op jit(solution)/shard_map/cts,nsc->ntc/dot_general | solution.py:151
  512.7 18.2 %all-to-all-done.5 = bf16[3072,4,48]{0,2,1:T(8,128)(2,1)S(1)} async-done(((bf16[3072,4,48]{0,2,1:T(8,128)(2,1)}), bf16[3072,4,48]{0,2,1:T(8,128)(2,1)S(1)}, u32[]{:S(2)}, u32[]{:S(2)}) %all-to-all-start.5) | async-done | bytes 1179680 | tf_op jit(solution)/shard_map/all_to_all | solution.py:40
  630.6 29.3 %all_to_all.80 = bf16[3072,4,48]{0,2,1:T(8,128)(2,1)S(1)} all-to-all(bf16[3072,4,48]{0,2,1:T(8,128)(2,1)S(1)} %bitcast.438), channel_id=1, replica_groups=mesh['wide'=8,'narrow'=4] {'narrow'}, dimensions={1} | all-to-all | bytes 2359296 | tf_op jit(solution)/shard_map/all_to_all | solution.py:51
  662.9 18.7 %all-reduce.15 = (f32[3072]{0:T(1024)}, f32[3072,1]{0,1:T(1,128)}) all-reduce(f32[3072]{0:T(1024)} %get-tuple-element.109, f32[3072,1]{0,1:T(1,128)} %bitcast.497), channel_id=1, replica_groups=mesh['wide'=8,'narrow'=4] {'narrow'}, use_global_device_ids=true, to_apply=%region_19.20 | all-reduce | flops 6144 | bytes 49152 | tf_op jit(solution)/shard_map/psum | solution.py:74
  695.5 20.4 %all-to-all-done.10 = bf16[3072,4,48]{0,2,1:T(8,128)(2,1)S(1)} async-done(((bf16[3072,4,48]{0,2,1:T(8,128)(2,1)}), bf16[3072,4,48]{0,2,1:T(8,128)(2,1)S(1)}, u32[]{:S(2)}, u32[]{:S(2)}) %all-to-all-start.10) | async-done | bytes 1179680 | tf_op jit(solution)/shard_map/all_to_all | solution.py:51
  796.2 22.9 %all-to-all-done.11 = bf16[3072,4,96]{0,2,1:T(8,128)(2,1)} async-done(((bf16[3072,4,96]{0,2,1:T(8,128)(2,1)}), bf16[3072,4,96]{0,2,1:T(8,128)(2,1)}, u32[]{:S(2)}, u32[]{:S(2)}) %all-to-all-start.11) | async-done | bytes 2359328 | tf_op jit(solution)/shard_map/all_to_all | solution.py:51
  827.4 32.7 %all-reduce.14 = (f32[3072]{0:T(1024)}, f32[3072,1]{0,1:T(1,128)}) all-reduce(f32[3072]{0:T(1024)} %get-tuple-element.111, f32[3072,1]{0,1:T(1,128)} %bitcast.499), channel_id=1, replica_groups=mesh['wide'=8,'narrow'=4] {'narrow'}, use_global_device_ids=true, to_apply=%region_23.24 | all-reduce | flops 6144 | bytes 49152 | tf_op jit(solution)/shard_map/psum | solution.py:74
  885.8 22.2 %fusion.152 = f32[192,128,128]{2,1,0:T(8,128)} fusion(f32[24,128,192]{1,0,2:T(8,128)S(1)} %copy-done.25, f32[24,128,192]{1,0,2:T(8,128)S(1)} %copy-done.24), kind=kOutput, calls=%fused_computation.333 | convolution fusion | flops 905969664 | bytes 17301504 | tf_op jit(solution)/shard_map/ntc,nsc->cts/dot_general | solution.py:239
  946.7 25.4 %reshape.387 = f32[192,32640]{1,0:T(8,128)} reshape(f32[192,128,255]{2,1,0:T(8,128)} %pad.33) | data formatting | bytes 50135040 | tf_op jit(solution)/shard_map/transpose(jvp())/reshape | solution.py:110
  1015.1 20.1 %all-reduce.13 = (f32[3072]{0:T(1024)S(1)}, f32[3072,1]{0,1:T(1,128)S(1)}) all-reduce(f32[3072]{0:T(1024)} %get-tuple-element.107, f32[3072,1]{0,1:T(1,128)} %bitcast.498), channel_id=1, replica_groups=mesh['wide'=8,'narrow'=4] {'narrow'}, use_global_device_ids=true, to_apply=%region_27.28 | all-reduce | flops 6144 | bytes 49152 | tf_op jit(solution)/shard_map/psum | solution.py:74
  1103.3 22.2 %fusion.151 = f32[192,128,128]{2,1,0:T(8,128)} fusion(f32[24,128,192]{1,0,2:T(8,128)S(1)} %copy-done.26, f32[24,128,192]{1,0,2:T(8,128)S(1)} %copy-done.22), kind=kOutput, calls=%fused_computation.332 | convolution fusion | flops 905969664 | bytes 17301504 | tf_op jit(solution)/shard_map/ntc,nsc->cts/dot_general | solution.py:239
  1165.1 25.4 %reshape.385 = f32[192,32640]{1,0:T(8,128)} reshape(f32[192,128,255]{2,1,0:T(8,128)} %pad.31) | data formatting | bytes 50135040 | tf_op jit(solution)/shard_map/transpose(jvp())/reshape | solution.py:110
  1231.1 41.0 %all-reduce.10 = (f32[1,5,128]{2,1,0:T(8,128)S(1)}, f32[1,5,128]{2,1,0:T(8,128)S(1)}, f32[1,128]{1,0:T(1,128)S(1)}, f32[1,128]{1,0:T(1,128)S(1)}) all-reduce(f32[1,5,128]{2,1,0:T(8,128)S(1)} %convolution_bitcast_fusion.3, f32[1,5,128]{2,1,0:T(8,128)S(1)} %convolution_bitcast_fusion.4, ...), channel_id=1, replica_groups=mesh['wide'=8,'narrow'=4] {'wide','narrow'}, use_global_device_ids=true, to_apply=%region_61.62 | all-reduce | flops 1536 | bytes 12288 | tf_op jit(solution)/shard_map/psum | solution.py:388
  1278.0 119.6 %all-reduce.26.cloned.1.call-done = (f32[1,128,128]{2,1,0:T(8,128)}, f32[1,128,128]{2,1,0:T(8,128)}) async-done(((f32[1,128,128]{2,1,0:T(8,128)}, f32[1,128,128]{2,1,0:T(8,128)}), (f32[1,128,128]{2,1,0:T(8,128)}, f32[1,128,128]{2,1,0:T(8,128)})) %all-reduce.26.cloned.1.call-update) | async-done | bytes 131088 | tf_op jit(solution)/shard_map/psum | solution.py:388
  1404.3 19.4 %all-reduce.12 = (f32[3072]{0:T(1024)}, f32[3072,1]{0,1:T(1,128)}) all-reduce(f32[3072]{0:T(1024)} %get-tuple-element.113, f32[3072,1]{0,1:T(1,128)} %bitcast.531), channel_id=1, replica_groups=mesh['wide'=8,'narrow'=4] {'narrow'}, use_global_device_ids=true, to_apply=%region_31.32 | all-reduce | flops 6144 | bytes 49152 | tf_op jit(solution)/shard_map/psum | solution.py:74
  1445.2 36.7 %all-reduce.28.cloned.1.call-done = (bf16[192]{0:T(256)(128)(2,1)}, bf16[1,192]{1,0:T(2,128)(2,1)}, bf16[1,192]{1,0:T(2,128)(2,1)}, bf16[1,3,384]{2,1,0:T(4,128)...) async-done(((bf16[192]{0:T(256)(128)(2,1)}, ...) | async-done | bytes 106384 | tf_op jit(solution)/shard_map/psum | solution.py:439
  1490.9 107.9 %all-reduce.30.cloned.1.call-done = (bf16[1,1,73728]{2,1,0:T(2,128)(2,1)}, bf16[1,1,73728]{2,1,0:T(2,128)(2,1)}, bf16[1,1,147456]{2,1,0:T(2,128)(2,1)}, bf16[1,1...) async-done(((bf16[1,1,73728]{2,1,0:T(2,128)(2,1)}, ...) | async-done | bytes 3244048 | tf_op jit(solution)/shard_map/psum | solution.py:408
  (607 shorter events, 810.6 us)
Async XLA Ops:
  8.9 237.6 %copy-start.90 = (f32[3072]{0:T(1024)}, f32[3072]{0:T(1024)S(1)}, u32[]{:S(2)}) copy-start(f32[3072]{0:T(1024)S(1)} %broadcast_subtract_fusion) | copy-start | bytes 36868
  39.5 129.0 %all-to-all-start = ((bf16[3072,4,96]{0,2,1:T(8,128)(2,1)}), bf16[3072,4,96]{0,2,1:T(8,128)(2,1)S(1)}, u32[]{:S(2)}, u32[]{:S(2)}) async-start(bf16[3072,4,96]{0,2,1:T(8,128)(2,1)} %bitcast.434), calls=%async_computation | async-start | bytes 4718592 | tf_op jit(solution)/shard_map/all_to_all | solution.py:40
  215.8 29.7 %all-to-all-start.1 = ((bf16[3072,4,48]{0,2,1:T(8,128)(2,1)}), bf16[3072,4,48]{0,2,1:T(8,128)(2,1)S(1)}, u32[]{:S(2)}, u32[]{:S(2)}) async-start(bf16[3072,4,48]{0,2,1:T(8,128)(2,1)} %bitcast.17), calls=%async_computation.1 | async-start | bytes 2359296 | tf_op jit(solution)/shard_map/all_to_all | solution.py:40
  225.9 562.7 %copy-start.133 = (f32[1,192]{1,0:T(1,128)}, f32[1,192]{1,0:T(1,128)S(1)}, u32[]{:S(2)}) copy-start(f32[1,192]{1,0:T(1,128)S(1)} %get-tuple-element.229) | copy-start | bytes 2308
  271.5 31.0 %all-to-all-start.2 = ((bf16[3072,4,48]{0,2,1:T(8,128)(2,1)}), bf16[3072,4,48]{0,2,1:T(8,128)(2,1)S(1)}, u32[]{:S(2)}, u32[]{:S(2)}) async-start(bf16[3072,4,48]{0,2,1:T(8,128)(2,1)} %bitcast.429), calls=%async_computation.2 | async-start | bytes 2359296 | tf_op jit(solution)/shard_map/all_to_all | solution.py:40
  315.8 26.5 %all-to-all-start.3 = ((bf16[3072,4,48]{0,2,1:T(8,128)(2,1)}), bf16[3072,4,48]{0,2,1:T(8,128)(2,1)S(1)}, u32[]{:S(2)}, u32[]{:S(2)}) async-start(bf16[3072,4,48]{0,2,1:T(8,128)(2,1)} %bitcast.437), calls=%async_computation.3 | async-start | bytes 2359296 | tf_op jit(solution)/shard_map/all_to_all | solution.py:40
  367.7 90.2 %all-to-all-start.4 = ((bf16[3072,4,96]{0,2,1:T(8,128)(2,1)}), bf16[3072,4,96]{0,2,1:T(8,128)(2,1)S(1)}, u32[]{:S(2)}, u32[]{:S(2)}) async-start(bf16[3072,4,96]{0,2,1:T(8,128)(2,1)} %bitcast.413), calls=%async_computation.4 | async-start | bytes 4718592 | tf_op jit(solution)/shard_map/all_to_all | solution.py:40
  504.4 26.5 %all-to-all-start.5 = ((bf16[3072,4,48]{0,2,1:T(8,128)(2,1)}), bf16[3072,4,48]{0,2,1:T(8,128)(2,1)S(1)}, u32[]{:S(2)}, u32[]{:S(2)}) async-start(bf16[3072,4,48]{0,2,1:T(8,128)(2,1)} %bitcast.430), calls=%async_computation.5 | async-start | bytes 2359296 | tf_op jit(solution)/shard_map/all_to_all | solution.py:40
  552.6 235.9 %copy-start.97 = (f32[3072,1]{0,1:T(1,128)}, f32[3072,1]{0,1:T(1,128)S(1)}, u32[]{:S(2)}) copy-start(f32[3072,1]{0,1:T(1,128)S(1)} %get-tuple-element.219) | copy-start | bytes 36868
  556.6 26.3 %all-to-all-start.6 = ((bf16[3072,4,48]{0,2,1:T(8,128)(2,1)}), bf16[3072,4,48]{0,2,1:T(8,128)(2,1)}, u32[]{:S(2)}, u32[]{:S(2)}) async-start(bf16[3072,4,48]{0,2,1:T(8,128)(2,1)} %bitcast.431), calls=%async_computation.6 | async-start | bytes 2359296 | tf_op jit(solution)/shard_map/all_to_all | solution.py:40
  582.9 28.9 %all-to-all-start.8 = ((bf16[3072,4,48]{0,2,1:T(8,128)(2,1)}), bf16[3072,4,48]{0,2,1:T(8,128)(2,1)}, u32[]{:S(2)}, u32[]{:S(2)}) async-start(bf16[3072,4,48]{0,2,1:T(8,128)(2,1)} %bitcast.428), calls=%async_computation.8 | async-start | bytes 2359296 | tf_op jit(solution)/shard_map/all_to_all | solution.py:51
  688.5 27.4 %all-to-all-start.10 = ((bf16[3072,4,48]{0,2,1:T(8,128)(2,1)}), bf16[3072,4,48]{0,2,1:T(8,128)(2,1)S(1)}, u32[]{:S(2)}, u32[]{:S(2)}) async-start(bf16[3072,4,48]{0,2,1:T(8,128)(2,1)} %bitcast.66), calls=%async_computation.10 | async-start | bytes 2359296 | tf_op jit(solution)/shard_map/all_to_all | solution.py:51
  762.9 56.2 %all-to-all-start.11 = ((bf16[3072,4,96]{0,2,1:T(8,128)(2,1)}), bf16[3072,4,96]{0,2,1:T(8,128)(2,1)}, u32[]{:S(2)}, u32[]{:S(2)}) async-start(bf16[3072,4,96]{0,2,1:T(8,128)(2,1)} %bitcast.394), calls=%async_computation.11 | async-start | bytes 4718592 | tf_op jit(solution)/shard_map/all_to_all | solution.py:51
  819.1 47.9 %all-to-all-start.7 = ((bf16[3072,4,48]{0,2,1:T(8,128)(2,1)}), bf16[3072,4,48]{0,2,1:T(8,128)(2,1)S(1)}, u32[]{:S(2)}, u32[]{:S(2)}) async-start(bf16[3072,4,48]{0,2,1:T(8,128)(2,1)} %bitcast.436), calls=%async_computation.7 | async-start | bytes 2359296 | tf_op jit(solution)/shard_map/all_to_all | solution.py:40
  868.1 39.9 %all-to-all-start.12 = ((bf16[3072,4,48]{0,2,1:T(8,128)(2,1)}), bf16[3072,4,48]{0,2,1:T(8,128)(2,1)}, u32[]{:S(2)}, u32[]{:S(2)}) async-start(bf16[3072,4,48]{0,2,1:T(8,128)(2,1)} %bitcast.425), calls=%async_computation.12 | async-start | bytes 2359296 | tf_op jit(solution)/shard_map/all_to_all | solution.py:51
  923.5 87.8 %all-to-all-start.13 = ((bf16[3072,4,48]{0,2,1:T(8,128)(2,1)}), bf16[3072,4,48]{0,2,1:T(8,128)(2,1)S(1)}, u32[]{:S(2)}, u32[]{:S(2)}) async-start(bf16[3072,4,48]{0,2,1:T(8,128)(2,1)} %bitcast.435), calls=%async_computation.13 | async-start | bytes 2359296 | tf_op jit(solution)/shard_map/all_to_all | solution.py:51
  1042.0 36.0 %all-to-all-start.14 = ((bf16[3072,4,48]{0,2,1:T(8,128)(2,1)}), bf16[3072,4,48]{0,2,1:T(8,128)(2,1)}, u32[]{:S(2)}, u32[]{:S(2)}) async-start(bf16[3072,4,48]{0,2,1:T(8,128)(2,1)} %bitcast.424), calls=%async_computation.14 | async-start | bytes 2359296 | tf_op jit(solution)/shard_map/all_to_all | solution.py:51
  1145.5 253.6 %all-to-all-start.15 = ((bf16[3072,4,96]{0,2,1:T(8,128)(2,1)}), bf16[3072,4,96]{0,2,1:T(8,128)(2,1)}, u32[]{:S(2)}, u32[]{:S(2)}) async-start(bf16[3072,4,96]{0,2,1:T(8,128)(2,1)} %bitcast.84), calls=%async_computation.15 | async-start | bytes 4718592 | tf_op jit(solution)/shard_map/all_to_all | solution.py:51
  1150.6 247.0 %all-reduce.26.cloned.1.call-start = ((), (), s32[]{:S(2)}) async-start(), calls=%async_computation.16 | async-start | bytes 262144 | tf_op jit(solution)/shard_map/psum | solution.py:388
  1225.7 173.5 %copy-start.16 = (bf16[192,3072]{1,0:T(8,128)(2,1)S(1)}, bf16[192,3072]{1,0:T(8,128)(2,1)}, u32[]{:S(2)}) copy-start(bf16[192,3072]{1,0:T(8,128)(2,1)} %param.22) | copy-start | bytes 3538948
  1225.7 173.5 %copy-start.92 = (f32[3072]{0:T(1024)S(1)}, f32[3072]{0:T(1024)}, u32[]{:S(2)}) copy-start(f32[3072]{0:T(1024)} %copy-done.90) | copy-start | bytes 36868
  1225.7 173.5 %copy-start.143 = (f32[192]{0:T(256)S(1)}, f32[192]{0:T(256)}, u32[]{:S(2)}) copy-start(f32[192]{0:T(256)} %param.26) | copy-start | bytes 2308
  1274.8 207.1 %all-reduce.28.cloned.1.call-start = ((), (), s32[]{:S(2)}) async-start(), calls=%async_computation.17 | async-start | bytes 226304 | tf_op jit(solution)/shard_map/psum | solution.py:439
  1429.3 169.5 %all-reduce.30.cloned.1.call-start = ((), (), s32[]{:S(2)}) async-start(), calls=%async_computation.18 | async-start | bytes 12976128 | tf_op jit(solution)/shard_map/psum | solution.py:408
  (167 other events, 1507.0 us)
Sparse Core Ops, SparseCore 0:
  1274.9 122.6 all-reduce.25
Sparse Core Ops, SparseCore 1:
  1429.4 52.4 all-reduce.27
  1489.1 109.6 all-reduce.29
where the time goes:
time: 1630 us
  local copies, waits for them, and re-layouts  469 us (29%)
  waiting for transfers between devices  389 us (24%)
  matrix products  329 us (20%)
  blocking collectives  234 us (14%)
  other arithmetic  121 us (7%)
  starting transfers between devices  66.6 us (4%)
  between operations  17.5 us (1%)
    reshape x4, local copies, waits for them, and re-layouts, toeplitz_table(): return window.reshape(channels, LENGTH, 2 * LENGTH - 1)[:, :, :LENGTH]  135 us
    psum x1, waiting for transfers between devices, local(): lax.psum((grad_filt_one, grad_filt_bias, grad_filt_two), ('wide', 'narrow'))  120 us
    psum x1, waiting for transfers between devices, local(): lax.psum(grad_in_first.astype(jnp.bfloat16), 'wide').astype(jnp.float32)  108 us
    unnamed x360, local copies, waits for them, and re-layouts  106 us
    psum x4, blocking collectives, norm_back(): lax.psum((jnp.sum(weighted, axis=1, keepdims=True), jnp.sum(weighted * st...  90.9 us
    dot_general x16, matrix products, mat_nt(): lax.dot_general(left_in, right_in, (((1,), (1,)), ((), ())), preferred_el...  76.9 us
    psum x4, blocking collectives, norm_ahead(): lax.psum((jnp.sum(row_block, axis=1, keepdims=True), jnp.sum(row_block *...  72.7 us
    all_to_all x8, waiting for transfers between devices, blocks_ahead(): lax.all_to_all(middle, 'narrow', split_axis=1, concat_axis=1, tiled=True)  71.5 us
  transfers between devices with their start and end apart: 18, of which 10 were waited for; matrix products, arithmetic and copies ran while one was open for 35% of the time, Pallas kernels for 0%

commit v1 on v0

v1 whole, which is shorter than its diff:
```python
import math
import functools
import numpy as np
import jax
import jax.numpy as jnp
from jax import lax
from jax.experimental import pallas as pl
from jax.experimental.pallas import tpu as pltpu
from jax.sharding import PartitionSpec as P

F32 = jnp.float32
BF16 = jnp.bfloat16
D = 768
LENGTH = 128
LAYERS = 2
BLOCK_W = 192
FF_BLOCK = 768
BLOCKS = 4
EPSILON = 1e-05
HIGHEST = lax.Precision.HIGHEST
GAIN_ONE, GAIN_TWO, SKIP, TAP_X, TAP_G, MASK, DECAY = 0, 1, 2, 3, 6, 9, 10
IN_ONE, IN_TWO, OUT_ROWS, PARAM_ROWS = 0, 192, 576, 768
UP_ONE, UP_TWO, DOWN_ONE = 0, 192, 960
MIX_ROWS, FF_USED, FF_ROWS, IN_GRAD_ROWS = 1024, 1344, 1408, 640
PIECE_ROWS = {"ff": 176, "conv": 48, "in": 80}
FINISH_ORDER = (("ff", "conv", "in"),) * LAYERS


def nn(a, b):
    return lax.dot_general(a, b, (((1,), (0,)), ((), ())), preferred_element_type=F32)


def nt(a, b):
    return lax.dot_general(a, b, (((1,), (1,)), ((), ())), preferred_element_type=F32)


def tn(a, b):
    return lax.dot_general(a, b, (((0,), (0,)), ((), ())), preferred_element_type=F32)


def spectrum_tables():
    time = np.arange(2 * LENGTH)
    freq = np.arange(LENGTH)
    angle = 2.0 * np.pi * np.outer(time, freq) / (2 * LENGTH)
    ahead = np.concatenate([np.cos(angle), -np.sin(angle)], axis=1)
    ahead[:, LENGTH] = np.cos(np.pi * time)
    scale = np.full((2 * LENGTH,), 2.0 / (2 * LENGTH))
    scale[0] = scale[LENGTH] = 1.0 / (2 * LENGTH)
    return ahead.astype(np.float32), (ahead * scale[None, :]).T.astype(np.float32)


def lanes_of(shape):
    return lax.broadcasted_iota(jnp.int32, shape, 1)


def later(v, lane):
    return jnp.where(lane == 0, 0.0, pltpu.roll(v, 1, 1))


def earlier(v, lane):
    return jnp.where(lane == LENGTH - 1, 0.0, pltpu.roll(v, LENGTH - 1, 1))


def norm_rows(parts):
    total = sum(jnp.sum(p, axis=0, keepdims=True) for p in parts)
    squares = sum(jnp.sum(p * p, axis=0, keepdims=True) for p in parts)
    mean = total / D
    inv = lax.rsqrt(squares / D - mean * mean + EPSILON)
    return mean, inv


def block(ref, b, width=BLOCK_W):
    return ref[pl.ds(b * width, width), :]


def fwd_mix_kernel(first, seqs, *refs):
    idx, own, rel_a, rel_b, *refs = refs
    if first:
        *parts, chosen_ref = refs[: BLOCKS + 1]
        refs = refs[BLOCKS + 1 :]
    else:
        h_ref, *refs = refs
    pad, hidden, ahead_full, ahead, back, *refs = refs
    if first:
        h_ref, *refs = refs
    q1, proj, conv, gated, q2, middle, stats, cols, kspec, w, normed, xs, gs, sem = refs
    fetch_table(idx, own, rel_a, rel_b, w, sem)
    make_params(w, hidden, ahead_full, cols, kspec)
    if first:
        keep = chosen_ref[0:1, :]
        for k, part in enumerate(parts):
            rows = pl.ds(pl.multiple_of(block_of(idx, k) * BLOCK_W, BLOCK_W), BLOCK_W)
            h_ref[rows, :] = part[...].astype(F32) * (1.0 - keep) + keep * cols[rows, MASK : MASK + 1]
    mean, inv = norm_rows([block(h_ref, b) for b in range(BLOCKS)])
    stats[0:1, :] = mean
    stats[1:2, :] = inv
    for b in range(BLOCKS):
        rows = pl.ds(b * BLOCK_W, BLOCK_W)
        normed[rows, :] = ((h_ref[rows, :] - mean) * inv * cols[rows, GAIN_ONE : GAIN_ONE + 1]).astype(BF16)
    for b in range(BLOCKS):
        inner = tn(w[b, IN_ONE : IN_ONE + 192, :], block(normed, b)).astype(BF16)
        for c in range(BLOCKS):
            q1[c, 96 * b : 96 * b + 96, :] = inner[96 * c : 96 * c + 96]
    lane = lanes_of((BLOCK_W, LENGTH))
    row_lane = lanes_of((BLOCK_W, LENGTH))
    for c in range(BLOCKS):
        rows = pl.ds(c * BLOCK_W, BLOCK_W)
        value = tn(w[c, IN_TWO : IN_TWO + 384, :], q1[c]) * pad[0:1, :]
        proj[c] = value.astype(BF16)
        for s in range(seqs):
            here = slice(s * LENGTH, (s + 1) * LENGTH)
            for part, tap, out in ((0, TAP_X, xs), (192, TAP_G, gs)):
                v = value[part : part + 192, here]
                out[:, here] = (
                    cols[rows, tap : tap + 1] * later(v, lane)
                    + cols[rows, tap + 1 : tap + 2] * v
                    + cols[rows, tap + 2 : tap + 3] * earlier(v, lane)
                )
        signal = jnp.concatenate([xs[:, s * LENGTH : (s + 1) * LENGTH] for s in range(seqs)], axis=0)
        spec = nn(signal.astype(BF16), ahead[...])
        k_re = kspec[rows, 0:LENGTH]
        k_im = kspec[rows, LENGTH : 2 * LENGTH]
        k_off = jnp.where(row_lane == 0, 0.0, k_im)
        k_im = jnp.where(row_lane == 0, k_im, k_re)
        made = []
        for s in range(seqs):
            re = spec[s * 192 : s * 192 + 192, 0:LENGTH]
            im = spec[s * 192 : s * 192 + 192, LENGTH : 2 * LENGTH]
            made.append(
                jnp.concatenate([re * k_re - im * k_off, re * k_off + im * k_im], axis=1).astype(BF16)
            )
        y = nn(jnp.concatenate(made, axis=0), back[...])
        for s in range(seqs):
            here = slice(s * LENGTH, (s + 1) * LENGTH)
            value = y[s * 192 : s * 192 + 192] + cols[rows, SKIP : SKIP + 1] * xs[:, here]
            conv[rows, here] = value.astype(BF16)
            gated[rows, here] = (value * gs[:, here]).astype(BF16)
    for b in range(BLOCKS):
        inner = tn(w[b, OUT_ROWS : OUT_ROWS + 192, 0:192], block(gated, b)).astype(BF16)
        for c in range(BLOCKS):
            q2[c, 48 * b : 48 * b + 48, :] = inner[48 * c : 48 * c + 48]
    for c in range(BLOCKS):
        rows = pl.ds(c * BLOCK_W, BLOCK_W)
        middle[rows, :] = h_ref[rows, :] + tn(w[c, OUT_ROWS : OUT_ROWS + 192, 192:384], q2[c])


def gelu_parts(v):
    inner = math.sqrt(2.0 / math.pi) * (v + 0.044715 * (v * v * v))
    return jnp.tanh(inner)


def fwd_ff_kernel(last, idx, own, rel_a, rel_b, middle, cols, q3, gate_up, q4, h_next, stats, w, normed, act, sem):
    fetch_table(idx, own, rel_a, rel_b, w, sem)
    mean, inv = norm_rows([block(middle, b) for b in range(BLOCKS)])
    stats[0:1, :] = mean
    stats[1:2, :] = inv
    for b in range(BLOCKS):
        rows = pl.ds(b * BLOCK_W, BLOCK_W)
        normed[rows, :] = ((middle[rows, :] - mean) * inv * cols[rows, GAIN_TWO : GAIN_TWO + 1]).astype(BF16)
    for b in range(BLOCKS):
        inner = tn(w[b, UP_ONE : UP_ONE + 192, 0:192], block(normed, b)).astype(BF16)
        for c in range(BLOCKS):
            q3[c, 48 * b : 48 * b + 48, :] = inner[48 * c : 48 * c + 48]
    for c in range(BLOCKS):
        for half in range(2):
            ups = []
            for piece in (half, half + 2):
                ups.append(tn(w[c, UP_TWO + 192 * piece : UP_TWO + 192 * piece + 192, :], q3[c]))
            gate, up = ups
            gate_up[c, 384 * half : 384 * half + 384, :] = gate.astype(BF16)
            gate_up[c, 768 + 384 * half : 768 + 384 * half + 384, :] = up.astype(BF16)
            act[384 * half : 384 * half + 384, :] = (
                0.5 * gate * (1.0 + gelu_parts(gate)) * up
            ).astype(BF16)
        inner = (
            tn(w[c, DOWN_ONE : DOWN_ONE + 384, 0:192], act[0:384, :])
            + tn(w[c, DOWN_ONE : DOWN_ONE + 384, 192:384], act[384:768, :])
        ).astype(BF16)
        for to in range(BLOCKS):
            q4[to, 48 * c : 48 * c + 48, :] = inner[48 * to : 48 * to + 48]
    for c in range(BLOCKS):
        rows = pl.ds(c * BLOCK_W, BLOCK_W)
        value = middle[rows, :] + tn(w[c, UP_ONE : UP_ONE + 192, 192:384], q4[c])
        if last:
            h_next[(c - idx[0]) & (BLOCKS - 1)] = value.astype(BF16)
        else:
            h_next[rows, :] = value


def bwd_ff_kernel(last, idx, own, rel_a, rel_b, *refs):
    parts = refs[: BLOCKS if last else 1]
    q4, gate_up, q3, middle, stats, cols, g_mid, g_out, small, w, g_w, g_low, gi4, gi3, g_gu, g_n, sem = refs[len(parts) :]
    fetch_table(idx, own, rel_a, rel_b, w, sem)
    mean = stats[0:1, :]
    inv = stats[1:2, :]
    if last:
        for k, part in enumerate(parts):
            g_low[pl.ds(pl.multiple_of(block_of(idx, k) * BLOCK_W, BLOCK_W), BLOCK_W), :] = part[...]
        g_top = g_low
    else:
        (g_top,) = parts
        for c in range(BLOCKS):
            g_low[c * 192 : c * 192 + 192, :] = block(g_top, c).astype(BF16)
    for b in range(BLOCKS):
        g_w[b, FF_USED:FF_ROWS, :] = jnp.zeros((FF_ROWS - FF_USED, 384), BF16)
    for c in range(BLOCKS):
        gt = block(g_low, c)
        g_w[c, UP_ONE : UP_ONE + 192, 192:384] = nt(q4[c], gt).astype(BF16)
        gq = nn(w[c, UP_ONE : UP_ONE + 192, 192:384], gt).astype(BF16)
        for b in range(BLOCKS):
            gi4[b, 48 * c : 48 * c + 48, :] = gq[48 * b : 48 * b + 48]
    rate = math.sqrt(2.0 / math.pi)
    for b in range(BLOCKS):
        for half in range(2):
            span = slice(192 * half, 192 * half + 192)
            gate = gate_up[b, 384 * half : 384 * half + 384, :].astype(F32)
            up = gate_up[b, 768 + 384 * half : 768 + 384 * half + 384, :].astype(F32)
            ga = nn(w[b, DOWN_ONE : DOWN_ONE + 384, span], gi4[b])
            square = gate * gate
            t = jnp.tanh(rate * gate * (1.0 + 0.044715 * square))
            rise = 0.5 * (1.0 + t)
            gelu = gate * rise
            slope = rise + 0.5 * gelu_slope(gate, square, t, rate)
            act = (gelu * up).astype(BF16)
            g_w[b, DOWN_ONE : DOWN_ONE + 384, span] = nt(act, gi4[b]).astype(BF16)
            g_gu[384 * half : 384 * half + 384, :] = (ga * up * slope).astype(BF16)
            g_gu[768 + 384 * half : 768 + 384 * half + 384, :] = (ga * gelu).astype(BF16)
        gq = None
        for piece in range(4):
            rows = slice(UP_TWO + 192 * piece, UP_TWO + 192 * piece + 192)
            gg = g_gu[384 * piece : 384 * piece + 384, :]
            g_w[b, rows, :] = nt(q3[b], gg).astype(BF16)
            term = nn(w[b, rows, :], gg)
            gq = term if gq is None else gq + term
        gq = gq.astype(BF16)
        for to in range(BLOCKS):
            gi3[to, 48 * b : 48 * b + 48, :] = gq[48 * to : 48 * to + 48]
    norm_back(
        middle, mean, inv, cols, GAIN_TWO, w, slice(UP_ONE, UP_ONE + 192), slice(0, 192), gi3, g_n, g_w, small, 1, g_top, g_mid
    )
    send_pieces(g_w, g_out, idx, sem)


def gelu_slope(gate, square, t, rate):
    return gate * (1.0 - t * t) * (rate * (1.0 + 3.0 * 0.044715 * square))


def row_sums(place, values):
    lanes = values.shape[1]
    part = values[:, 0:LENGTH]
    for at in range(LENGTH, lanes, LENGTH):
        part = part + values[:, at : at + LENGTH]
    high = part.astype(BF16)
    low = (part - high.astype(F32)).astype(BF16)
    pick = (lax.broadcasted_iota(jnp.int32, (16, LENGTH), 0) == place).astype(F32).astype(BF16)
    return nt(pick, high) + nt(pick, low)


def norm_back(h, mean, inv, cols, gain_at, w, w_rows, w_lanes, gi, g_n, g_w, small, place, g_in, g_out):
    plain = cross = 0.0
    for b in range(BLOCKS):
        rows = pl.ds(b * 192, 192)
        gain = cols[rows, gain_at : gain_at + 1]
        xh = (h[rows, :] - mean) * inv
        gn = nn(w[b, w_rows, w_lanes], gi[b])
        g_w[b, w_rows, w_lanes] = nt((xh * gain).astype(BF16), gi[b]).astype(BF16)
        gx = gn * xh
        small[b] = row_sums(place, gx)
        g_n[rows, :] = gn * gain
        plain = plain + jnp.sum(gn * gain, axis=0, keepdims=True)
        cross = cross + jnp.sum(gx * gain, axis=0, keepdims=True)
    plain = plain / D
    cross = cross / D
    for b in range(BLOCKS):
        rows = pl.ds(b * 192, 192)
        xh = (h[rows, :] - mean) * inv
        g_out[rows, :] = g_in[rows, :].astype(F32) + inv * (g_n[rows, :] - plain - xh * cross)


def bwd_conv_kernel(
    seqs, idx, own, rel_a, rel_b, g_mid, q2, gated, conv, proj, pad, cols, kspec, ahead, back, small_ff, gv, g_out, w, g_w, gi2, gcs, xs, sem
):
    fetch_table(idx, own, rel_a, rel_b, w, sem)
    for c in range(BLOCKS):
        gt = block(g_mid, c).astype(BF16)
        g_w[c, 0:192, 192:384] = nt(q2[c], gt).astype(BF16)
        gq = nn(w[c, OUT_ROWS : OUT_ROWS + 192, 192:384], gt).astype(BF16)
        for b in range(BLOCKS):
            gi2[b, 48 * c : 48 * c + 48, :] = gq[48 * b : 48 * b + 48]
    lane = lanes_of((BLOCK_W, LENGTH))
    first_lane = lane == 0
    for b in range(BLOCKS):
        rows = pl.ds(b * 192, 192)
        g_gated = nn(w[b, OUT_ROWS : OUT_ROWS + 192, 0:192], gi2[b])
        g_w[b, 0:192, 0:192] = nt(block(gated, b), gi2[b]).astype(BF16)
        sums = [0.0] * 7
        for s in range(seqs):
            here = slice(s * LENGTH, (s + 1) * LENGTH)
            v = proj[b, 0:192, here].astype(F32)
            xs[:, here] = (
                cols[rows, TAP_X : TAP_X + 1] * later(v, lane)
                + cols[rows, TAP_X + 1 : TAP_X + 2] * v
                + cols[rows, TAP_X + 2 : TAP_X + 3] * earlier(v, lane)
            )
            v = proj[b, 192:384, here].astype(F32)
            after, before = later(v, lane), earlier(v, lane)
            gate = (
                cols[rows, TAP_G : TAP_G + 1] * after
                + cols[rows, TAP_G + 1 : TAP_G + 2] * v
                + cols[rows, TAP_G + 2 : TAP_G + 3] * before
            )
            gg = g_gated[:, here]
            gcs[:, here] = gg * gate
            z = gg * conv[rows, here].astype(F32)
            sums[4] = sums[4] + z * after
            sums[5] = sums[5] + z * v
            sums[6] = sums[6] + z * before
            gv[b, 192:384, here] = (
                (
                    cols[rows, TAP_G : TAP_G + 1] * earlier(z, lane)
                    + cols[rows, TAP_G + 1 : TAP_G + 2] * z
                    + cols[rows, TAP_G + 2 : TAP_G + 3] * later(z, lane)
                )
                * pad[0:1, here]
            ).astype(BF16)
            sums[0] = sums[0] + gcs[:, here] * xs[:, here]
        stacked = jnp.concatenate(
            [ref[:, s * LENGTH : (s + 1) * LENGTH] for ref in (xs, gcs) for s in range(seqs)], axis=0
        )
        spec = nn(stacked.astype(BF16), ahead[...])
        k_re = kspec[rows, 0:LENGTH]
        k_im = kspec[rows, LENGTH : 2 * LENGTH]
        k_off = jnp.where(first_lane, 0.0, k_im)
        k_im = jnp.where(first_lane, k_im, k_re)
        made = []
        p_re = p_im = p_off = 0.0
        for s in range(seqs):
            x_re = spec[s * 192 : s * 192 + 192, 0:LENGTH]
            x_im = spec[s * 192 : s * 192 + 192, LENGTH : 2 * LENGTH]
            at = (seqs + s) * 192
            g_re = spec[at : at + 192, 0:LENGTH]
            g_im = spec[at : at + 192, LENGTH : 2 * LENGTH]
            p_re = p_re + g_re * x_re
            p_im = p_im + g_im * x_im
            p_off = p_off + (g_im * x_re - g_re * x_im)
            made.append(
                jnp.concatenate([g_re * k_re + g_im * k_off, g_im * k_im - g_re * k_off], axis=1).astype(BF16)
            )
        g_w[b, 192:384, 0:128] = jnp.where(first_lane, p_re, p_re + p_im).astype(BF16)
        g_w[b, 192:384, 128:256] = jnp.where(first_lane, p_im, p_off).astype(BF16)
        y = nn(jnp.concatenate(made, axis=0), back[...])
        for s in range(seqs):
            here = slice(s * LENGTH, (s + 1) * LENGTH)
            z = y[s * 192 : s * 192 + 192] + cols[rows, SKIP : SKIP + 1] * gcs[:, here]
            v = proj[b, 0:192, here].astype(F32)
            sums[1] = sums[1] + z * later(v, lane)
            sums[2] = sums[2] + z * v
            sums[3] = sums[3] + z * earlier(v, lane)
            gv[b, 0:192, here] = (
                (
                    cols[rows, TAP_X : TAP_X + 1] * earlier(z, lane)
                    + cols[rows, TAP_X + 1 : TAP_X + 2] * z
                    + cols[rows, TAP_X + 2 : TAP_X + 3] * later(z, lane)
                )
                * pad[0:1, here]
            ).astype(BF16)
        table = small_ff[b]
        for at, value in enumerate(sums):
            table = table + row_sums(2 + at, value)
        table = table.astype(BF16)
        g_w[b, 192:208, 256:384] = table[:, 0:128]
        g_w[b, 208:224, 256:320] = table[:, 128:192]
        g_w[b, 208:224, 320:384] = jnp.zeros((16, 64), BF16)
        g_w[b, 224:384, 256:384] = jnp.zeros((160, 128), BF16)
    send_pieces(g_w, g_out, idx, sem)


def bwd_in_kernel(first, *refs):
    refs = list(refs)
    idx, own, rel_a, rel_b, gv, g_mid, q1, h, stats, cols = refs[:10]
    refs = refs[10:]
    chosen = refs.pop(0) if first else None
    g_out, g_send, w, g_w, gi1, g_n, small, sem = refs[:8]
    g_h = refs[8] if first else g_out
    fetch_table(idx, own, rel_a, rel_b, w, sem)
    mean = stats[0:1, :]
    inv = stats[1:2, :]
    for c in range(BLOCKS):
        g_w[c, IN_TWO : IN_TWO + 384, :] = nt(q1[c], gv[c]).astype(BF16)
        gq = nn(w[c, IN_TWO : IN_TWO + 384, :], gv[c]).astype(BF16)
        for b in range(BLOCKS):
            gi1[b, 96 * c : 96 * c + 96, :] = gq[96 * b : 96 * b + 96]
    norm_back(
        h, mean, inv, cols, GAIN_ONE, w, slice(IN_ONE, IN_ONE + 192), slice(0, 384), gi1, g_n, g_w, small, 0, g_mid, g_h
    )
    for b in range(BLOCKS):
        rows = pl.ds(b * 192, 192)
        table = small[b]
        if first:
            value = g_h[rows, :]
            masked = value * chosen[0:1, :]
            table = table + row_sums(1, masked)
            g_out[(b - idx[0]) & (BLOCKS - 1)] = (value - masked).astype(BF16)
        g_w[b, 576:592, 0:192] = table.astype(BF16)
        g_w[b, 576:592, 192:384] = jnp.zeros((16, 192), BF16)
        g_w[b, 592:640, :] = jnp.zeros((48, 384), BF16)
    send_pieces(g_w, g_send, idx, sem)


def piece_rows(idx, core, chip, rows):
    return pl.ds(pl.multiple_of((idx[1] ^ (2 * chip + core)) * rows, 16), rows)


def block_of(idx, k):
    return (idx[0] - k) & (BLOCKS - 1)


def run_copies(pairs, sem):
    copies = [pltpu.make_async_copy(source, target, sem.at[at]) for at, (source, target) in enumerate(pairs)]
    for copy in copies:
        copy.start()
    for copy in copies:
        copy.wait()


def send_pieces(table, out, idx, sem):
    rows = out.shape[3]
    run_copies(
        [
            (table.at[block_of(idx, k), piece_rows(idx, core, chip, rows), :], out.at[core, chip, k])
            for core in range(2)
            for chip in range(4)
            for k in range(BLOCKS)
        ],
        sem,
    )


def fetch_table(idx, own, rel_a, rel_b, table, sem):
    rows = rel_a.shape[2]
    run_copies(
        [(own, table.at[idx[0]])]
        + [
            (rel.at[chip, k - 1], table.at[block_of(idx, k), piece_rows(idx, core, chip, rows), :])
            for core, rel in enumerate((rel_a, rel_b))
            for chip in range(4)
            for k in range(1, BLOCKS)
        ],
        sem,
    )


def make_params(w, hidden, ahead_full, cols, kspec):
    place = lanes_of((BLOCK_W, 2 * LENGTH))
    lag = jnp.where(place < LENGTH, place, 2 * LENGTH - place).astype(F32)
    for b in range(BLOCKS):
        rows = pl.ds(b * BLOCK_W, BLOCK_W)
        packed = w[b, PARAM_ROWS : PARAM_ROWS + BLOCK_W, :].astype(F32)
        three = packed[:, 256:384]
        cols[rows, :] = three + pltpu.roll(three, 128 - 16, 1) + pltpu.roll(three, 128 - 32, 1)
        shaped_rows = lax.dot_general(
            packed[:, 0:128] + packed[:, 128:256],
            hidden[...],
            (((1,), (1,)), ((), ())),
            precision=HIGHEST,
            preferred_element_type=F32,
        )
        envelope = jnp.exp(-lag * cols[rows, DECAY : DECAY + 1])
        table = jnp.where(place == LENGTH, 0.0, shaped_rows * envelope * (1.0 / math.sqrt(LENGTH)))
        kspec[rows, :] = lax.dot_general(
            table, ahead_full[...], (((1,), (0,)), ((), ())), precision=HIGHEST, preferred_element_type=F32
        )


def fold_back(lines, wide, count):
    low = lanes_of((count // 2, 128)) < 64
    one, two, three = (lines[pl.ds(j, count // 2, stride=3), :] for j in range(3))
    three = pltpu.roll(three, 64, 1)
    wide[0, pl.ds(0, count // 2, stride=2), :] = one
    wide[1, pl.ds(0, count // 2, stride=2), :] = two
    wide[0, pl.ds(1, count // 2, stride=2), :] = jnp.where(low, pltpu.roll(two, 64, 1), three)
    wide[1, pl.ds(1, count // 2, stride=2), :] = three


def fold_out(wide, out, count):
    low = lanes_of((count // 2, 128)) < 64
    half = count // 2
    even_a = wide[0, pl.ds(0, half, stride=2), :]
    even_b = wide[1, pl.ds(0, half, stride=2), :]
    odd_a = pltpu.roll(wide[0, pl.ds(1, half, stride=2), :], 64, 1)
    odd_b = pltpu.roll(wide[1, pl.ds(1, half, stride=2), :], 64, 1)
    out[pl.ds(0, half, stride=3), :] = even_a
    out[pl.ds(1, half, stride=3), :] = jnp.where(low, even_b, odd_a)
    out[pl.ds(2, half, stride=3), :] = jnp.where(low, odd_a, odd_b)


def spread_lines(flat, layer, count, lanes, lines):
    rows = flat.shape[1]
    lines[0:rows, :] = flat[layer].astype(F32)
    return [lines[pl.ds(j, count, stride=lanes), :] for j in range(lanes)]


def narrow_lines(flat, layer, count, lines, wide):
    rows = flat.shape[1]
    lines[0:rows, :] = flat[layer].astype(F32)
    fold_back(lines, wide, count)
    return jnp.concatenate([wide[0, 0:count, :], wide[1, 0:count, 0:64]], axis=1).astype(BF16)


def own_piece(idx, table, out, layer):
    rows = out.shape[1]
    out[layer] = table[layer, pl.ds(pl.multiple_of(idx[1] * rows, 16), rows), :]


def pack_mix_kernel(idx, in_one, in_two, out_one, out_two, params, table, out, lines, wide):
    for layer in range(LAYERS):
        for flat, start, count in ((in_one, IN_ONE, 192), (in_two, IN_TWO, 384)):
            for j, part in enumerate(spread_lines(flat, layer, count, 3, lines)):
                table[layer, start : start + count, 128 * j : 128 * j + 128] = part.astype(BF16)
        table[layer, OUT_ROWS : OUT_ROWS + 192, 0:192] = narrow_lines(out_one, layer, 192, lines, wide)
        table[layer, OUT_ROWS : OUT_ROWS + 192, 192:384] = narrow_lines(out_two, layer, 192, lines, wide)
        last = params[layer, :, 128:256]
        high = last.astype(BF16)
        rows = slice(PARAM_ROWS, PARAM_ROWS + BLOCK_W)
        table[layer, rows, 0:128] = high
        table[layer, rows, 128:256] = (last - high.astype(F32)).astype(BF16)
        left = params[layer, :, 0:128]
        terms = jnp.zeros((BLOCK_W, 128), F32)
        for at in range(3):
            part = left.astype(BF16).astype(F32)
            left = left - part
            terms = terms + (pltpu.roll(part, 16 * at, 1) if at else part)
        table[layer, rows, 256:384] = terms.astype(BF16)
        table[layer, PARAM_ROWS + BLOCK_W : MIX_ROWS, :] = jnp.zeros((MIX_ROWS - PARAM_ROWS - BLOCK_W, 384), BF16)
        own_piece(idx, table, out, layer)


def pack_ff_kernel(idx, up_one, up_two, down_one, down_two, table, out, lines, wide):
    for layer in range(LAYERS):
        table[layer, UP_ONE : UP_ONE + 192, 0:192] = narrow_lines(up_one, layer, 192, lines, wide)
        table[layer, UP_ONE : UP_ONE + 192, 192:384] = narrow_lines(down_two, layer, 192, lines, wide)
        for j, part in enumerate(spread_lines(up_two, layer, 192, 12, lines)):
            at = UP_TWO + 192 * (j // 3)
            table[layer, at : at + 192, 128 * (j % 3) : 128 * (j % 3) + 128] = part.astype(BF16)
        down = narrow_lines(down_one, layer, 768, lines, wide)
        table[layer, DOWN_ONE : DOWN_ONE + 384, 0:192] = down[0:384]
        table[layer, DOWN_ONE : DOWN_ONE + 384, 192:384] = down[384:768]
        table[layer, FF_USED:FF_ROWS, :] = jnp.zeros((FF_ROWS - FF_USED, 384), BF16)
        own_piece(idx, table, out, layer)


def finish_kernel(idx, *refs):
    pieces = refs[: 2 * len(FINISH_ORDER)]
    refs = refs[2 * len(FINISH_ORDER) :]
    in_one, in_two, out_one, out_two, up_one, up_two, down_one, down_two, small = refs[:9]
    ff, conv, inp, wide, sem = refs[9:]
    tables = {"ff": ff, "conv": conv, "in": inp}
    pairs = []
    for at, group in enumerate(FINISH_ORDER):
        for core in range(2):
            rel = pieces[2 * at + core]
            first = 0
            for name in group:
                rows = PIECE_ROWS[name]
                for chip in range(4):
                    pairs.append(
                        (
                            rel.at[chip, pl.ds(first, rows), :],
                            tables[name].at[at, piece_rows(idx, core, chip, rows), :],
                        )
                    )
                first += rows
    run_copies(pairs, sem)

    def spread(out, layer, values, lanes, first):
        count = values.shape[0]
        for j in range(3):
            out[layer, pl.ds(first + j, count, stride=lanes), :] = values[:, 128 * j : 128 * j + 128].astype(F32)

    def narrow_of(out, layer, values):
        count = values.shape[0]
        wide[0, 0:count, :] = values[:, 0:128].astype(F32)
        wide[1, 0:count, 0:64] = values[:, 128:192].astype(F32)
        fold_out(wide, out.at[layer], count)

    for layer in range(LAYERS):
        spread(in_one, layer, inp[layer, IN_ONE : IN_ONE + 192, :], 3, 0)
        spread(in_two, layer, inp[layer, IN_TWO : IN_TWO + 384, :], 3, 0)
        for q in range(4):
            at = UP_TWO + 192 * q
            spread(up_two, layer, ff[layer, at : at + 192, :], 12, 3 * q)
        narrow_of(out_one, layer, conv[layer, 0:192, 0:192])
        narrow_of(out_two, layer, conv[layer, 0:192, 192:384])
        narrow_of(up_one, layer, ff[layer, UP_ONE : UP_ONE + 192, 0:192])
        narrow_of(down_two, layer, ff[layer, UP_ONE : UP_ONE + 192, 192:384])
        narrow_of(
            down_one,
            layer,
            jnp.concatenate(
                [ff[layer, DOWN_ONE : DOWN_ONE + 384, 0:192], ff[layer, DOWN_ONE : DOWN_ONE + 384, 192:384]], axis=0
            ),
        )
        small[layer, 0:16, 0:128] = conv[layer, 192:208, 256:384].astype(F32)
        small[layer, 0:16, 128:256] = conv[layer, 208:224, 256:384].astype(F32)
        small[layer, 16:32, 0:256] = inp[layer, 576:592, 0:256].astype(F32)


def join_kernel(first, idx, rel_a, rel_b, out, sem):
    rows = PIECE_ROWS["conv"]
    run_copies(
        [
            (rel.at[chip, pl.ds(first, rows), :], out.at[piece_rows(idx, core, chip, rows), :])
            for core, rel in enumerate((rel_a, rel_b))
            for chip in range(4)
        ],
        sem,
    )


ANY = pl.BlockSpec(memory_space=pl.ANY)
SCALARS = pl.BlockSpec(memory_space=pltpu.SMEM)
WHOLE = pl.BlockSpec(memory_space=pltpu.VMEM)


def shaped(dtype, *shape):
    return jax.ShapeDtypeStruct(shape, dtype)


def call(kernel, outs, scratch, in_specs, out_specs, micros, deps=()):
    count = len(in_specs)

    def body(*refs):
        kernel(*refs[:count], *refs[count + len(deps) :])

    made = pl.pallas_call(
        body,
        out_shape=outs,
        in_specs=list(in_specs) + [ANY] * len(deps),
        out_specs=out_specs,
        scratch_shapes=scratch,
        compiler_params=pltpu.CompilerParams(vmem_limit_bytes=56 << 20),
        cost_estimate=pl.CostEstimate(flops=int(micros * 1e9), bytes_accessed=1 << 20, transcendentals=0),
    )
    return lambda *arrays: made(*arrays, *deps)


def place_parts_kernel(idx, *refs):
    parts, out = refs[:BLOCKS], refs[BLOCKS]
    span = parts[0].shape[1]
    for k, part in enumerate(parts):
        out[:, pl.ds(pl.multiple_of(block_of(idx, k) * span, 128), span)] = part[...].astype(out.dtype)


def wide_shift(x, mask):
    return lax.ppermute(x, "wide", [(i, i ^ mask) for i in range(lax.axis_size("wide"))])


def narrow_shift(x, by):
    narrow = lax.axis_size("narrow")
    return lax.ppermute(x, "narrow", [(i, (i + by) % narrow) for i in range(narrow)])


def added(parts):
    return sum(p.astype(F32) for p in parts).astype(parts[0].dtype)


def after(x, *deps):
    return lax.optimization_barrier((x, deps))[0]


def exchange(parts):
    return [parts[0]] + [narrow_shift(parts[k], k) for k in range(1, BLOCKS)]


def over_blocks(piece):
    return jnp.stack([narrow_shift(piece, k) for k in range(1, BLOCKS)])


def over_chips(x):
    return jnp.stack([x] + [wide_shift(x, 2 * m) for m in range(1, 4)])


def reduce_core(table):
    return added([table[0], wide_shift(table[1], 1)])


def reduce_chips(half):
    total = added([half[0]] + [wide_shift(half[m], 2 * m) for m in range(1, 4)])
    groups = lax.axis_size("wide") // 8
    if groups > 1:
        total = added([total] + [wide_shift(total, 8 * g) for g in range(1, groups)])
    return total


def reduce_blocks(total):
    return added([total[0]] + [narrow_shift(total[k], -k) for k in range(1, BLOCKS)])


def join_rows(*tables):
    return jnp.concatenate(tables, axis=-2)


def filter_lags():
    place = jnp.arange(2 * LENGTH)
    return place, jnp.where(place < LENGTH, place, place - 2 * LENGTH).astype(F32)


def filter_hidden(weight_one, bias_one, weight_two):
    relative = filter_lags()[1] / LENGTH
    features = jnp.stack(
        [
            relative,
            jnp.cos(math.pi * relative),
            jnp.sin(math.pi * relative),
            jnp.cos(37.0 * math.pi * relative),
            jnp.sin(37.0 * math.pi * relative),
        ],
        axis=1,
    )
    hidden_one = jnp.sin(jnp.dot(features, weight_one, precision=HIGHEST) + bias_one)
    return jnp.sin(jnp.dot(hidden_one, weight_two, precision=HIGHEST))


def filter_table(weight_one, bias_one, weight_two, weight_three, decay_rate):
    place, lag = filter_lags()
    hidden_two = filter_hidden(weight_one, bias_one, weight_two)
    shaped_rows = lax.dot_general(
        weight_three, hidden_two, (((1,), (1,)), ((), ())), precision=HIGHEST, preferred_element_type=F32
    )
    envelope = jnp.exp(-jnp.abs(lag)[None, :] * decay_rate[:, None])
    return jnp.where(place[None, :] == LENGTH, 0.0, shaped_rows * envelope / math.sqrt(LENGTH))


def local(
    tokens,
    lengths,
    masked,
    cotangent,
    mask_vector,
    gain_one,
    in_first,
    in_second,
    short_taps,
    skip_gain,
    decay_rates,
    filter_one,
    filter_bias,
    filter_two,
    filter_three,
    out_first,
    out_second,
    gain_two,
    up_first,
    up_second,
    down_first,
    down_second,
):
    wide_count = lax.axis_size("wide")
    me = lax.axis_index("narrow")
    place = lax.axis_index("wide") & 7
    idx = jnp.stack([me, place]).astype(jnp.int32)
    seqs = lengths.shape[0] // BLOCKS
    span = seqs * LENGTH
    all_tokens = tokens.shape[1] * wide_count

    def token_parts(table):
        return [lax.dynamic_slice_in_dim(table, ((me + k) % BLOCKS) * span, span, 1) for k in range(BLOCKS)]

    def flat_lines(weight):
        return weight.reshape(LAYERS, weight.shape[2] // 128, 128)

    factors = [in_first, in_second, out_first, out_second, up_first, up_second, down_first, down_second]
    lines = [flat_lines(weight) for weight in factors]
    tokens_here = exchange(token_parts(tokens))

    columns = jnp.concatenate(
        [
            gain_one[:, None],
            gain_two[:, None],
            skip_gain[:, None],
            short_taps[:, :, 0, :BLOCK_W],
            short_taps[:, :, 0, BLOCK_W:],
            jnp.broadcast_to(mask_vector, (LAYERS, 1, BLOCK_W)),
            decay_rates[:, None],
            jnp.zeros((LAYERS, 5, BLOCK_W), F32),
        ],
        axis=1,
    )
    columns = jnp.pad(columns.transpose(0, 2, 1), ((0, 0), (0, 0), (0, 112)))
    params = jnp.concatenate([columns, filter_three], axis=2)

    def pack(kernel, count, rows, arrays, micros):
        return call(
            kernel,
            [shaped(BF16, LAYERS, rows, 384), shaped(BF16, LAYERS, rows // 8, 384)],
            [pltpu.VMEM((2304, 128), F32), pltpu.VMEM((2, 768, 128), F32)],
            [SCALARS] + [WHOLE] * count,
            [WHOLE] * 2,
            micros,
        )(idx, *arrays)

    mix, mix_piece = pack(pack_mix_kernel, 5, MIX_ROWS, lines[:4] + [params], 3)
    ff, ff_piece = pack(pack_ff_kernel, 4, FF_ROWS, lines[4:], 4)

    weights_mix, weights_ff = [None] * LAYERS, [None] * LAYERS
    previous = ()
    for layer in range(LAYERS):
        for own, piece, made in ((mix, mix_piece, weights_mix), (ff, ff_piece, weights_ff)):
            others = over_blocks(after(piece[layer], *previous))
            previous = (others,)
            chips = over_chips(others)
            made[layer] = (own[layer], chips, wide_shift(chips, 1))
    cotangent_here = exchange(token_parts(after(cotangent, *previous)))

    own_lengths = lax.dynamic_slice_in_dim(lengths, me * seqs, seqs, 0)
    own_masked = lax.dynamic_slice_in_dim(masked, me * seqs, seqs, 0)
    positions = jnp.arange(LENGTH, dtype=jnp.int32)
    pad = (positions[None, :] < own_lengths[:, None]).astype(F32).reshape(1, span)
    pad = jnp.broadcast_to(pad, (8, span))
    chosen = jnp.broadcast_to(own_masked.astype(F32).reshape(1, span), (8, span))

    ahead, back = spectrum_tables()
    ahead_low = jnp.asarray(ahead[:LENGTH]).astype(BF16)
    back_low = jnp.asarray(back[:, :LENGTH]).astype(BF16)
    ahead_full = jnp.asarray(ahead)
    hidden = [filter_hidden(filter_one[layer], filter_bias[layer], filter_two[layer]) for layer in range(LAYERS)]
    pulls = [
        jax.vjp(
            filter_table,
            filter_one[layer],
            filter_bias[layer],
            filter_two[layer],
            filter_three[layer],
            decay_rates[layer],
        )
        for layer in range(LAYERS)
    ]
    mix_scratch = pltpu.VMEM((BLOCKS, MIX_ROWS, 384), BF16)
    ff_scratch = pltpu.VMEM((BLOCKS, FF_ROWS, 384), BF16)
    fetched = pltpu.SemaphoreType.DMA((25,))
    sent = pltpu.SemaphoreType.DMA((32,))
    table_specs = [SCALARS, ANY, ANY, ANY]

    h = None
    saved = []
    for layer in range(LAYERS):
        first, last = layer == 0, layer == LAYERS - 1
        made = call(
            functools.partial(fwd_mix_kernel, first, seqs),
            ([shaped(F32, D, span)] if first else [])
            + [
                shaped(BF16, BLOCKS, 384, span),
                shaped(BF16, BLOCKS, 384, span),
                shaped(BF16, D, span),
                shaped(BF16, D, span),
                shaped(BF16, BLOCKS, 192, span),
                shaped(F32, D, span),
                shaped(F32, 8, span),
                shaped(F32, D, 128),
                shaped(F32, D, 256),
            ],
            [
                mix_scratch,
                pltpu.VMEM((D, span), BF16),
                pltpu.VMEM((BLOCK_W, span), F32),
                pltpu.VMEM((BLOCK_W, span), F32),
                fetched,
            ],
            table_specs + [WHOLE] * (BLOCKS + 1 if first else 1) + [WHOLE] * 5,
            [WHOLE] * (10 if first else 9),
            18,
        )(
            idx,
            *weights_mix[layer],
            *([*tokens_here, chosen] if first else [h]),
            pad,
            hidden[layer],
            ahead_full,
            ahead_low,
            back_low,
        )
        if first:
            h, *made = made
        q1, proj, conv, gated, q2, middle, stats_one, cols, kspec = made
        q3, gate_up, q4, h_next, stats_two = call(
            functools.partial(fwd_ff_kernel, last),
            [
                shaped(BF16, BLOCKS, 192, span),
                shaped(BF16, BLOCKS, 1536, span),
                shaped(BF16, BLOCKS, 192, span),
                shaped(BF16, BLOCKS, BLOCK_W, span) if last else shaped(F32, D, span),
                shaped(F32, 8, span),
            ],
            [ff_scratch, pltpu.VMEM((D, span), BF16), pltpu.VMEM((FF_BLOCK, span), BF16), fetched],
            table_specs + [WHOLE] * 2,
            [WHOLE] * 5,
            15,
        )(idx, *weights_ff[layer], middle, cols)
        saved.append((h, q1, proj, conv, gated, q2, middle, stats_one, cols, kspec, q3, gate_up, q4, stats_two))
        h = h_next

    def collect(parts, dtype):
        return call(
            place_parts_kernel,
            shaped(dtype, BLOCK_W, BLOCKS * span),
            [],
            [SCALARS] + [WHOLE] * BLOCKS,
            WHOLE,
            2,
        )(idx, *exchange([parts[k] for k in range(BLOCKS)]))

    mixed_out = collect(h, BF16)

    def back_ff(layer, g_top, deps):
        last = layer == LAYERS - 1
        h, q1, proj, conv, gated, q2, middle, stats_one, cols, kspec, q3, gate_up, q4, stats_two = saved[layer]
        return call(
            functools.partial(bwd_ff_kernel, last),
            [shaped(F32, D, span), shaped(BF16, 2, 4, BLOCKS, FF_ROWS // 8, 384), shaped(F32, BLOCKS, 16, BLOCK_W)],
            [
                ff_scratch,
                pltpu.VMEM((BLOCKS, FF_ROWS, 384), BF16),
                pltpu.VMEM((D, span), BF16),
                pltpu.VMEM((BLOCKS, 192, span), BF16),
                pltpu.VMEM((BLOCKS, 192, span), BF16),
                pltpu.VMEM((2 * FF_BLOCK, span), BF16),
                pltpu.VMEM((D, span), F32),
                sent,
            ],
            table_specs + [WHOLE] * (BLOCKS if last else 1) + [WHOLE] * 6,
            [WHOLE, ANY, WHOLE],
            27,
            deps,
        )(idx, *weights_ff[layer], *(g_top if last else [g_top]), q4, gate_up, q3, middle, stats_two, cols)

    def back_conv(layer, g_mid, small_ff, deps):
        h, q1, proj, conv, gated, q2, middle, stats_one, cols, kspec, q3, gate_up, q4, stats_two = saved[layer]
        return call(
            functools.partial(bwd_conv_kernel, seqs),
            [shaped(BF16, BLOCKS, 384, span), shaped(BF16, 2, 4, BLOCKS, 48, 384)],
            [
                mix_scratch,
                pltpu.VMEM((BLOCKS, 384, 384), BF16),
                pltpu.VMEM((BLOCKS, 192, span), BF16),
                pltpu.VMEM((BLOCK_W, span), F32),
                pltpu.VMEM((BLOCK_W, span), F32),
                sent,
            ],
            table_specs + [WHOLE] * 11,
            [WHOLE, ANY],
            23,
            deps,
        )(
            idx,
            *weights_mix[layer],
            g_mid,
            q2,
            gated,
            conv,
            proj,
            pad,
            cols,
            kspec,
            ahead_low,
            back_low,
            small_ff,
        )

    def back_in(layer, gv, g_mid, deps):
        first = layer == 0
        h, q1, proj, conv, gated, q2, middle, stats_one, cols, kspec, q3, gate_up, q4, stats_two = saved[layer]
        return call(
            functools.partial(bwd_in_kernel, first),
            [
                shaped(BF16, BLOCKS, BLOCK_W, span) if first else shaped(F32, D, span),
                shaped(BF16, 2, 4, BLOCKS, IN_GRAD_ROWS // 8, 384),
            ],
            [
                mix_scratch,
                pltpu.VMEM((BLOCKS, IN_GRAD_ROWS, 384), BF16),
                pltpu.VMEM((BLOCKS, 384, span), BF16),
                pltpu.VMEM((D, span), F32),
                pltpu.VMEM((BLOCKS, 16, BLOCK_W), F32),
                sent,
            ]
            + ([pltpu.VMEM((D, span), F32)] if first else []),
            table_specs + [WHOLE] * (7 if first else 6),
            [WHOLE, ANY],
            12,
            deps,
        )(idx, *weights_mix[layer], gv, g_mid, q1, h, stats_one, cols, *([chosen] if first else []))

    def spread(*tables):
        chips = over_chips(join_rows(*tables))
        return chips, wide_shift(chips, 1)

    g_mid, g_ff, small_ff = back_ff(1, cotangent_here, ())
    ff_one = reduce_core(g_ff)
    gv, g_conv = back_conv(1, g_mid, small_ff, ())
    conv_one = reduce_core(g_conv)
    g_top, g_in = back_in(1, gv, g_mid, (ff_one,))
    ff_one = reduce_chips(ff_one)
    in_one = reduce_core(g_in)

    g_mid, g_ff, small_ff = back_ff(0, g_top, (conv_one,))
    mix_one = join_rows(conv_one, in_one)
    ff_zero = reduce_core(g_ff)
    gv, g_conv = back_conv(0, g_mid, small_ff, (ff_one, mix_one))
    mix_one = reduce_chips(mix_one)
    ff_one = reduce_blocks(ff_one)
    conv_zero = reduce_core(g_conv)
    g_top, g_in = back_in(0, gv, g_mid, (ff_one, mix_one, ff_zero))
    grad_tokens = collect(g_top, F32)
    mix_one = reduce_blocks(mix_one)
    ff_zero = reduce_blocks(reduce_chips(ff_zero))
    mix_zero = reduce_blocks(reduce_chips(join_rows(conv_zero, reduce_core(g_in))))
    groups = [spread(ff_zero, mix_zero), spread(ff_one, mix_one)]

    filter_grads = []
    for layer in range(LAYERS):
        joined = call(
            functools.partial(join_kernel, PIECE_ROWS["ff"]),
            shaped(BF16, 384, 384),
            [pltpu.SemaphoreType.DMA((8,))],
            [SCALARS, ANY, ANY],
            WHOLE,
            2,
        )(idx, *groups[layer])
        g_kernel = jnp.dot(joined[192:384, 0:256].astype(F32), jnp.asarray(back), precision=HIGHEST)
        kernel, pull = pulls[layer]
        grads = pull(g_kernel + 4.0 * math.sqrt(all_tokens) * kernel)
        shared = jnp.concatenate([grads[2], grads[0], grads[1][None], jnp.zeros((2, 128), F32)], axis=0)
        shared = added([shared] + [narrow_shift(shared, k) for k in range(1, BLOCKS)])
        filter_grads.append((shared[128:133], shared[133], shared[0:128], grads[3], grads[4]))

    sizes = [weight.shape[2] // 128 for weight in factors]
    flat = call(
        finish_kernel,
        [shaped(F32, LAYERS, size, 128) for size in sizes] + [shaped(F32, LAYERS, 32, 256)],
        [
            pltpu.VMEM((LAYERS, FF_ROWS, 384), BF16),
            pltpu.VMEM((LAYERS, 384, 384), BF16),
            pltpu.VMEM((LAYERS, IN_GRAD_ROWS, 384), BF16),
            pltpu.VMEM((2, 768, 128), F32),
            pltpu.SemaphoreType.DMA((24 * LAYERS,)),
        ],
        [SCALARS] + [ANY] * (2 * LAYERS),
        [WHOLE] * 9,
        8,
    )(idx, *(part for group in groups for part in group))
    grads = [table.reshape(LAYERS, 1, table.shape[1] * 128) for table in flat[:8]]
    small = flat[8][:, :, :BLOCK_W]
    filt = [jnp.stack([filter_grads[layer][at] for layer in range(LAYERS)]) for at in range(5)]
    return (
        mixed_out,
        grad_tokens,
        small[0, 17],
        small[:, 16],
        grads[0],
        grads[1],
        jnp.concatenate([small[:, 3:6], small[:, 6:9]], axis=2)[:, :, None],
        small[:, 2],
        filt[4],
        filt[0],
        filt[1],
        filt[2],
        filt[3],
        grads[2],
        grads[3],
        small[:, 1],
        grads[4],
        grads[5],
        grads[6],
        grads[7],
    )


def solution(mesh):
    placed = (
        P("narrow", "wide"),
        P("wide"),
        P("wide", None),
        P("narrow", "wide"),
        P("narrow"),
        P(None, "narrow"),
        P(None, "narrow", None),
        P(None, "narrow", None),
        P(None, None, "narrow", None),
        P(None, "narrow"),
        P(None, "narrow"),
        P(),
        P(),
        P(),
        P(None, "narrow", None),
        P(None, "narrow", None),
        P(None, "narrow", None),
        P(None, "narrow"),
        P(None, "narrow", None),
        P(None, "narrow", None),
        P(None, "narrow", None),
        P(None, "narrow", None),
    )
    return jax.shard_map(
        local,
        mesh=mesh,
        in_specs=placed,
        out_specs=(
            P("narrow", "wide"),
            P("narrow", "wide"),
            P("narrow"),
            P(None, "narrow"),
            P(None, "narrow", None),
            P(None, "narrow", None),
            P(None, None, "narrow", None),
            P(None, "narrow"),
            P(None, "narrow"),
            P(),
            P(),
            P(),
            P(None, "narrow", None),
            P(None, "narrow", None),
            P(None, "narrow", None),
            P(None, "narrow"),
            P(None, "narrow", None),
            P(None, "narrow", None),
            P(None, "narrow", None),
            P(None, "narrow", None),
        ),
        check_vma=False,
    )
```

time: 1630 us -> 578 us (0.35)
  local copies, waits for them, and re-layouts: 469 us -> 46.9 us
  matrix products: 329 us -> 14.4 us
  waiting for transfers between devices: 389 us -> 138 us
  blocking collectives: 234 us -> 0 us
  Pallas kernels: 0 us -> 222 us
  other arithmetic: 121 us -> 23.9 us
  starting transfers between devices: 66.6 us -> 121 us
    dot_general x70 -> x18, matrix products: 329 us -> 14.4 us  [the longest x6 4.59 us: filter_hidden(): return jnp.sin(jnp.dot(hidden_one, weight_two, precision=HIGHEST))]
    psum x3 -> x0, waiting for transfers between devices: 264 us -> none  [the longest x1 120 us: local(): lax.psum((grad_filt_one, grad_filt_bias, grad_filt_two), ('wide', 'narrow'))]
    pallas_call x0 -> x17, Pallas kernels: none -> 222 us  [call(): return lambda *arrays: made(*arrays, *deps)]
    psum x9 -> x0, blocking collectives: 205 us -> none  [the longest x4 90.9 us: norm_back(): lax.psum((jnp.sum(weighted, axis=1, keepdims=True), jnp.sum(weighted * st...]
    ppermute x0 -> x84, waiting for transfers between devices: none -> 138 us  [the longest x42 80.4 us: narrow_shift(): lax.ppermute(x, 'narrow', [(i, (i + by) % narrow) for i in range(narrow)])]
    reshape x4 -> x2, local copies, waits for them, and re-layouts: 135 us -> 1.5 us  [flat_lines(): return weight.reshape(LAYERS, weight.shape[2] // 128, 128)]
    all_to_all x15 -> x0, waiting for transfers between devices: 124 us -> none  [the longest x8 71.5 us: blocks_ahead(): lax.all_to_all(middle, 'narrow', split_axis=1, concat_axis=1, tiled=True)]
    ppermute x0 -> x84, starting transfers between devices: none -> 121 us  [the longest x42 82.1 us: narrow_shift(): lax.ppermute(x, 'narrow', [(i, (i + by) % narrow) for i in range(narrow)])]
  transfers between devices with their start and end apart: 18 -> 84, of which waited for: 10 -> 33; matrix products, arithmetic and copies ran while one was open for 35% -> 10% of each run, Pallas kernels for 0% -> 32%
where the time goes in v1:
time: 578 us; the launch traced here: 568 us
  Pallas kernels  222 us (38%)
  waiting for transfers between devices  138 us (24%)
  starting transfers between devices  121 us (21%)
  local copies, waits for them, and re-layouts  46.9 us (8%)
  other arithmetic  23.9 us (4%)
  matrix products  14.4 us (2%)
    pallas_call x17, Pallas kernels, call(): return lambda *arrays: made(*arrays, *deps)  222 us
    ppermute x42, starting transfers between devices, narrow_shift(): lax.ppermute(x, 'narrow', [(i, (i + by) % narrow) for i in range(narrow)])  82.1 us
    ppermute x42, waiting for transfers between devices, narrow_shift(): lax.ppermute(x, 'narrow', [(i, (i + by) % narrow) for i in range(narrow)])  80.4 us
    ppermute x42, waiting for transfers between devices, wide_shift(): lax.ppermute(x, 'wide', [(i, i ^ mask) for i in range(lax.axis_size('wide...  57.1 us
    ppermute x42, starting transfers between devices, wide_shift(): lax.ppermute(x, 'wide', [(i, i ^ mask) for i in range(lax.axis_size('wide...  38.7 us
    unnamed x181, local copies, waits for them, and re-layouts  17 us
  transfers between devices with their start and end apart: 84, of which 33 were waited for; matrix products, arithmetic and copies ran while one was open for 10% of the time, Pallas kernels for 32%

profile of v1, /device:TPU:0, one launch (start us, length us, event | category | flops | bytes accessed | tf_op | source)
XLA Modules:
  0.0 568.5 jit_solution(14328970186241194912)
XLA Ops:
  12.4 5.1 collective-permute-start.2
  41.9 8.2 %collective-permute-done.4 = bf16[176,384]{1,0:T(8,128)(2,1)S(1)} collective-permute-done((bf16[176,384]{1,0:T(8,128)(2,1)S(1)}, bf16[176,384]{1,0:T(8,128)(2,1)S(1)}, u32[]{:S(2)}, u32[]{:S(2)}) %collective-permute-start.4) | collective-permute-done | bytes 135200 | tf_op jit(solution)/shard_map/ppermute | solution.py:660
  102.1 8.2 %collective-permute-done.14 = bf16[3,176,384]{2,1,0:T(8,128)(2,1)S(1)} collective-permute-done((bf16[3,176,384]{2,1,0:T(8,128)(2,1)S(1)}, bf16[3,176,384]{2,1,0:T(8,128)(2,1)S(1)}, u32[]{:S(2)}, u32[]{:S(2)}) %collective-permute-start.14) | collective-permute-done | bytes 405536 | tf_op jit(solution)/shard_map/ppermute | solution.py:655
  122.2 15.6 %collective-permute-done.29.refs_6_ = bf16[192,768]{1,0:T(8,128)(2,1)S(1)} collective-permute-done((bf16[192,768]{1,0:T(8,128)(2,1)S(1)}, bf16[192,768]{1,0:T(8,128)(2,1)S(1)}, u32[]{:S(2)}, u32[]{:S(2)}) %collective-permute-start.29) | collective-permute-done | bytes 294944 | tf_op jit(solution)/shard_map/ppermute | solution.py:660
  139.9 18.5 %shard_map.403 = (f32[768,768]{1,0:T(8,128)}, bf16[4,384,768]{2,1,0:T(8,128)(2,1)}, bf16[4,384,768]{2,1,0:T(8,128)(2,1)}, bf16[768,768]{1,0:T(8,128)(2,1)}, bf16...) custom-call(s32[2]{0:T(128)} %pad_add_fusion.refs_0_, ...), custom_call_target="tpu_custom_call" | custom-call | flops 17999998976 | bytes 1048576 | tf_op jit(solution)/shard_map/pallas_call | solution.py:644
  159.7 14.9 %shard_map.404 = (bf16[4,192,768]{2,1,0:T(8,128)(2,1)}, bf16[4,1536,768]{2,1,0:T(8,128)(2,1)}, bf16[4,192,768]{2,1,0:T(8,128)(2,1)}, f32[768,768]{1,0:T(8,128)}, f32[8,768]{1,0:T(8,128)}) custom-call(s32[2]{0:T(128)} %pad_add_fusion.refs_0_, bf16[1408,384]{1,0:T(8,128)(2,1)} %get-tuple-element.228.refs_1_, bf16[4,3,176,384]{3,2,1,0:T(8,128)(2,1)} %copy-done.7, ...), custom_call_target="tpu_custom_call" | custom-call | flops 15000000512 | bytes 1048576 | tf_op jit(solution)/shard_map/pallas_call | solution.py:644
  174.6 17.4 %shard_map.405 = (bf16[4,384,768]{2,1,0:T(8,128)(2,1)}, bf16[4,384,768]{2,1,0:T(8,128)(2,1)}, bf16[768,768]{1,0:T(8,128)(2,1)}, bf16[768,768]{1,0:T(8,128)(2,1)}...) custom-call(s32[2]{0:T(128)} %pad_add_fusion.refs_0_, ...), custom_call_target="tpu_custom_call" | custom-call | flops 17999998976 | bytes 1048576 | tf_op jit(solution)/shard_map/pallas_call | solution.py:644
  193.1 15.0 %shard_map.406 = (bf16[4,192,768]{2,1,0:T(8,128)(2,1)}, bf16[4,1536,768]{2,1,0:T(8,128)(2,1)}, bf16[4,192,768]{2,1,0:T(8,128)(2,1)}, bf16[4,192,768]{2,1,0:T(8,128)(2,1)}, f32[8,768]{1,0:T(8,128)}) custom-call(s32[2]{0:T(128)} %pad_add_fusion.refs_0_, bf16[1408,384]{1,0:T(8,128)(2,1)} %get-tuple-element.229.refs_1_, bf16[4,3,176,384]{3,2,1,0:T(8,128)(2,1)} %copy-done.8, ...), custom_call_target="tpu_custom_call" | custom-call | flops 15000000512 | bytes 1048576 | tf_op jit(solution)/shard_map/pallas_call | solution.py:644
  209.0 27.6 %shard_map.408 = (f32[768,768]{1,0:T(8,128)}, bf16[2,4,4,176,384]{4,3,2,1,0:T(8,128)(2,1)}, f32[4,16,192]{2,1,0:T(8,128)}) custom-call(s32[2]{0:T(128)} %pad_add_fusion.refs_0_, bf16[1408,384]{1,0:T(8,128)(2,1)} %get-tuple-element.229.refs_1_, bf16[4,3,176,384]{3,2,1,0:T(8,128)(2,1)} %copy-done.8, bf16[4,3,176,384]{3,2,1,0:T(8,128)(2,1)} %copy-done.67, ...), custom_call_target="tpu_custom_call" | custom-call | flops 27000000512 | bytes 1048576 | tf_op jit(solution)/shard_map/pallas_call | solution.py:644
  238.9 24.5 %shard_map.409 = (bf16[4,384,768]{2,1,0:T(8,128)(2,1)}, bf16[2,4,4,48,384]{4,3,2,1,0:T(8,128)(2,1)}) custom-call(s32[2]{0:T(128)} %pad_add_fusion.refs_0_, bf16[1024,384]{1,0:T(8,128)(2,1)} %get-tuple-element.237.refs_1_, bf16[4,3,128,384]{3,2,1,0:T(8,128)(2,1)} %copy-done.23, bf16[4,3,128,384]{3,2,1,0:T(8,128)(2,1)} %collective-permute-done.19.refs_3_, ...), custom_call_target="tpu_custom_call" | custom-call | flops 23000000512 | bytes 1048576 | tf_op jit(solution)/shard_map/pallas_call | solution.py:644
  266.4 7.2 %collective-permute-start.31 = (bf16[192,768]{1,0:T(8,128)(2,1)S(1)}, bf16[192,768]{1,0:T(8,128)(2,1)S(1)}, u32[]{:S(2)}, u32[]{:S(2)}) collective-permute-start(bf16[192,768]{1,0:T(8,128)(2,1)S(1)} %get-tuple-element.248), channel_id=1, source_target_pairs={{0,1},{1,2},{2,3},{3,0},{4,5},{5,6},{6,7},{7,4},{8,9},{9,10},{10,1... | collective-permute-start | bytes 884744 | tf_op jit(solution)/shard_map/ppermute | solution.py:660
  280.9 9.4 %collective-permute-done.32.refs_3_ = bf16[192,768]{1,0:T(8,128)(2,1)S(1)} collective-permute-done((bf16[192,768]{1,0:T(8,128)(2,1)S(1)}, bf16[192,768]{1,0:T(8,128)(2,1)S(1)}, u32[]{:S(2)}, u32[]{:S(2)}) %collective-permute-start.32) | collective-permute-done | bytes 294944 | tf_op jit(solution)/shard_map/ppermute | solution.py:660
  305.4 13.6 %shard_map.410 = (f32[768,768]{1,0:T(8,128)}, bf16[2,4,4,80,384]{4,3,2,1,0:T(8,128)(2,1)}) custom-call(s32[2]{0:T(128)} %pad_add_fusion.refs_0_, bf16[1024,384]{1,0:T(8,128)(2,1)} %get-tuple-element.237.refs_1_, bf16[4,3,128,384]{3,2,1,0:T(8,128)(2,1)} %copy-done.23, bf16[4,3,128,384]{3,2,1,0:T(8,128)(2,1)} %collective-permute-done.19.refs_3_, ...), custom_call_target="tpu_custom_call" | custom-call | flops 12000000000 | bytes 1048576 | tf_op jit(solution)/shard_map/pallas_call | solution.py:644
  320.4 27.8 %shard_map.411 = (f32[768,768]{1,0:T(8,128)}, bf16[2,4,4,176,384]{4,3,2,1,0:T(8,128)(2,1)}, f32[4,16,192]{2,1,0:T(8,128)}) custom-call(s32[2]{0:T(128)} %pad_add_fusion.refs_0_, bf16[1408,384]{1,0:T(8,128)(2,1)} %get-tuple-element.228.refs_1_, bf16[4,3,176,384]{3,2,1,0:T(8,128)(2,1)} %copy-done.7, bf16[4,3,176,384]{3,2,1,0:T(8,128)(2,1)} %copy-done.66, ...), custom_call_target="tpu_custom_call" | custom-call | flops 27000000512 | bytes 1048576 | tf_op jit(solution)/shard_map/pallas_call | solution.py:644
  353.0 7.3 %collective-permute-start.45 = (bf16[176,384]{1,0:T(8,128)(2,1)S(1)}, bf16[176,384]{1,0:T(8,128)(2,1)S(1)}, u32[]{:S(2)}, u32[]{:S(2)}) collective-permute-start(bf16[176,384]{1,0:T(8,128)(2,1)S(1)} %get-tuple-element.258), channel_id=1, source_target_pairs={{0,1},{1,2},{2,3},{3,0},{4,5},{5,6},{6,7},{7,4},{8,9},{9,10},{10,1... | collective-permute-start | bytes 405512 | tf_op jit(solution)/shard_map/ppermute | solution.py:660
  377.1 7.3 %collective-permute-done.47 = bf16[4,128,384]{2,1,0:T(8,128)(2,1)S(1)} collective-permute-done((bf16[4,128,384]{2,1,0:T(8,128)(2,1)S(1)}, bf16[4,128,384]{2,1,0:T(8,128)(2,1)S(1)}, u32[]{:S(2)}, u32[]{:S(2)}) %collective-permute-start.47) | collective-permute-done | bytes 393248 | tf_op jit(solution)/shard_map/ppermute | solution.py:655
  389.4 25.0 %shard_map.412 = (bf16[4,384,768]{2,1,0:T(8,128)(2,1)}, bf16[2,4,4,48,384]{4,3,2,1,0:T(8,128)(2,1)}) custom-call(s32[2]{0:T(128)} %pad_add_fusion.refs_0_, bf16[1024,384]{1,0:T(8,128)(2,1)} %get-tuple-element.236.refs_1_, bf16[4,3,128,384]{3,2,1,0:T(8,128)(2,1)} %copy-done.22, bf16[4,3,128,384]{3,2,1,0:T(8,128)(2,1)} %collective-permute-done.27.refs_3_, ...), custom_call_target="tpu_custom_call" | custom-call | flops 23000000512 | bytes 1048576 | tf_op jit(solution)/shard_map/pallas_call | solution.py:644
  419.0 5.2 collective-permute-done.76
  429.5 14.0 %shard_map.413 = (bf16[4,192,768]{2,1,0:T(8,128)(2,1)}, bf16[2,4,4,80,384]{4,3,2,1,0:T(8,128)(2,1)}) custom-call(s32[2]{0:T(128)} %pad_add_fusion.refs_0_, bf16[1024,384]{1,0:T(8,128)(2,1)} %get-tuple-element.236.refs_1_, bf16[4,3,128,384]{3,2,1,0:T(8,128)(2,1)} %copy-done.22, bf16[4,3,128,384]{3,2,1,0:T(8,128)(2,1)} %collective-permute-done.27.refs_3_, ...), custom_call_target="tpu_custom_call" | custom-call | flops 12000000000 | bytes 1048576 | tf_op jit(solution)/shard_map/pallas_call | solution.py:644
  459.7 10.1 %collective-permute-done.51.refs_3_ = bf16[192,768]{1,0:T(8,128)(2,1)S(1)} collective-permute-done((bf16[192,768]{1,0:T(8,128)(2,1)S(1)}, bf16[192,768]{1,0:T(8,128)(2,1)S(1)}, u32[]{:S(2)}, u32[]{:S(2)}) %collective-permute-start.51) | collective-permute-done | bytes 294944 | tf_op jit(solution)/shard_map/ppermute | solution.py:660
  481.4 10.9 %collective-permute-done.54 = bf16[4,176,384]{2,1,0:T(8,128)(2,1)} collective-permute-done((bf16[4,176,384]{2,1,0:T(8,128)(2,1)}, bf16[4,176,384]{2,1,0:T(8,128)(2,1)}, u32[]{:S(2)}, u32[]{:S(2)}) %collective-permute-start.54) | collective-permute-done | bytes 540704 | tf_op jit(solution)/shard_map/ppermute | solution.py:655
  494.1 7.2 %collective-permute-start.57 = (bf16[176,384]{1,0:T(8,128)(2,1)S(1)}, bf16[176,384]{1,0:T(8,128)(2,1)S(1)}, u32[]{:S(2)}, u32[]{:S(2)}) collective-permute-start(bf16[176,384]{1,0:T(8,128)(2,1)S(1)} %get-tuple-element.256), channel_id=1, source_target_pairs={{0,2},{1,3},{2,0},{3,1},{4,6},{5,7},{6,4},{7,5},{8,10},{9,11},{10,... | collective-permute-start | bytes 405512 | tf_op jit(solution)/shard_map/ppermute | solution.py:660
  502.2 5.3 collective-permute-start.66
  531.9 6.8 %shard_map.415 = (f32[2,576,128]{2,1,0:T(8,128)}, f32[2,1152,128]{2,1,0:T(8,128)}, f32[2,288,128]{2,1,0:T(8,128)}, f32[2,288,128]{2,1,0:T(8,128)}, f32[2,288,128...) custom-call(s32[2]{0:T(128)} %pad_add_fusion.refs_0_, ...), custom_call_target="tpu_custom_call" | custom-call | flops 8000000000 | bytes 1048576 | tf_op jit(solution)/shard_map/pallas_call | solution.py:644
  (457 shorter events, 253.7 us)
Async XLA Ops:
  63.8 27.3 %collective-permute-start.22 = (bf16[3,176,384]{2,1,0:T(8,128)(2,1)}, bf16[3,176,384]{2,1,0:T(8,128)(2,1)}, u32[]{:S(2)}, u32[]{:S(2)}) collective-permute-start(bf16[3,176,384]{2,1,0:T(8,128)(2,1)} %get-tuple-element.261), channel_id=1, source_target_pairs={{0,24},{4,28},{8,16},{12,20},{16,8},{20,12},{24,0},{28,4},{1,25},{... | collective-permute-start | bytes 1216520 | tf_op jit(solution)/shard_map/ppermute | solution.py:655
  79.6 59.1 %collective-permute-start.27 = (bf16[4,3,128,384]{3,2,1,0:T(8,128)(2,1)S(1)}, bf16[4,3,128,384]{3,2,1,0:T(8,128)(2,1)}, u32[]{:S(2)}, u32[]{:S(2)}) collective-permute-start(bf16[4,3,128,384]{3,2,1,0:T(8,128)(2,1)S(1)} %pad_maximum_fusion.4.refs_2_), channel_id=1, source_target_pairs={{0,4},{4,0},{8,12},{12,8},{16,20},{20,16},{24,28},{28,24},{1,5},{5... | collective-permute-start | bytes 3538952 | tf_op jit(solution)/shard_map/ppermute | solution.py:655
  110.3 27.4 %collective-permute-start.29 = (bf16[192,768]{1,0:T(8,128)(2,1)S(1)}, bf16[192,768]{1,0:T(8,128)(2,1)S(1)}, u32[]{:S(2)}, u32[]{:S(2)}) collective-permute-start(bf16[192,768]{1,0:T(8,128)(2,1)S(1)} %get-tuple-element.253), channel_id=1, source_target_pairs={{0,2},{1,3},{2,0},{3,1},{4,6},{5,7},{6,4},{7,5},{8,10},{9,11},{10,... | collective-permute-start | bytes 884744 | tf_op jit(solution)/shard_map/ppermute | solution.py:660
  114.1 23.8 %collective-permute-start.30 = (bf16[192,768]{1,0:T(8,128)(2,1)S(1)}, bf16[192,768]{1,0:T(8,128)(2,1)S(1)}, u32[]{:S(2)}, u32[]{:S(2)}) collective-permute-start(bf16[192,768]{1,0:T(8,128)(2,1)S(1)} %get-tuple-element.250), channel_id=1, source_target_pairs={{0,3},{1,0},{2,1},{3,2},{4,7},{5,4},{6,5},{7,6},{8,11},{9,8},{10,9... | collective-permute-start | bytes 884744 | tf_op jit(solution)/shard_map/ppermute | solution.py:660
  118.9 89.3 %collective-permute-start.34 = (bf16[192,768]{1,0:T(8,128)(2,1)S(1)}, bf16[192,768]{1,0:T(8,128)(2,1)S(1)}, u32[]{:S(2)}, u32[]{:S(2)}) collective-permute-start(bf16[192,768]{1,0:T(8,128)(2,1)S(1)} %get-tuple-element.244), channel_id=1, source_target_pairs={{0,1},{1,2},{2,3},{3,0},{4,5},{5,6},{6,7},{7,4},{8,9},{9,10},{10,1... | collective-permute-start | bytes 884744 | tf_op jit(solution)/shard_map/ppermute | solution.py:660
  120.2 88.0 %collective-permute-start.35 = (bf16[192,768]{1,0:T(8,128)(2,1)S(1)}, bf16[192,768]{1,0:T(8,128)(2,1)S(1)}, u32[]{:S(2)}, u32[]{:S(2)}) collective-permute-start(bf16[192,768]{1,0:T(8,128)(2,1)S(1)} %get-tuple-element.243), channel_id=1, source_target_pairs={{0,2},{1,3},{2,0},{3,1},{4,6},{5,7},{6,4},{7,5},{8,10},{9,11},{10,... | collective-permute-start | bytes 884744 | tf_op jit(solution)/shard_map/ppermute | solution.py:660
  137.8 70.4 %collective-permute-start.36 = (bf16[192,768]{1,0:T(8,128)(2,1)S(1)}, bf16[192,768]{1,0:T(8,128)(2,1)}, u32[]{:S(2)}, u32[]{:S(2)}) collective-permute-start(bf16[192,768]{1,0:T(8,128)(2,1)S(1)} %get-tuple-element.242), channel_id=1, source_target_pairs={{0,3},{1,0},{2,1},{3,2},{4,7},{5,4},{6,5},{7,6},{8,11},{9,8},{10,9... | collective-permute-start | bytes 884744 | tf_op jit(solution)/shard_map/ppermute | solution.py:660
  138.0 36.6 %collective-permute-start.19 = (bf16[4,3,128,384]{3,2,1,0:T(8,128)(2,1)S(1)}, bf16[4,3,128,384]{3,2,1,0:T(8,128)(2,1)}, u32[]{:S(2)}, u32[]{:S(2)}) collective-permute-start(bf16[4,3,128,384]{3,2,1,0:T(8,128)(2,1)S(1)} %pad_maximum_fusion.3.refs_2_), channel_id=1, source_target_pairs={{0,4},{4,0},{8,12},{12,8},{16,20},{20,16},{24,28},{28,24},{1,5},{5... | collective-permute-start | bytes 3538952 | tf_op jit(solution)/shard_map/ppermute | solution.py:655
  158.5 33.5 %collective-permute-start.15 = (bf16[4,3,176,384]{3,2,1,0:T(8,128)(2,1)S(1)}, bf16[4,3,176,384]{3,2,1,0:T(8,128)(2,1)S(1)}, u32[]{:S(2)}, u32[]{:S(2)}) collective-permute-start(bf16[4,3,176,384]{3,2,1,0:T(8,128)(2,1)S(1)} %pad_maximum_fusion.1.refs_2_), channel_id=1, source_target_pairs={{0,4},{4,0},{8,12},{12,8},{16,20},{20,16},{24,28},{28,24},{1,5},{5... | collective-permute-start | bytes 4866056 | tf_op jit(solution)/shard_map/ppermute | solution.py:655
  238.4 60.0 %collective-permute-start.37 = (bf16[4,4,176,384]{3,2,1,0:T(8,128)(2,1)S(1)}, bf16[4,4,176,384]{3,2,1,0:T(8,128)(2,1)}, u32[]{:S(2)}, u32[]{:S(2)}) collective-permute-start(bf16[4,4,176,384]{3,2,1,0:T(8,128)(2,1)S(1)} %slice_bitcast_fusion.1), channel_id=1, source_target_pairs={{0,4},{4,0},{8,12},{12,8},{16,20},{20,16},{24,28},{28,24},{1,5},{5... | collective-permute-start | bytes 6488072 | tf_op jit(solution)/shard_map/ppermute | solution.py:655
  265.6 30.8 %collective-permute-start.38 = (bf16[4,4,48,384]{3,2,1,0:T(8,128)(2,1)}, bf16[4,4,48,384]{3,2,1,0:T(8,128)(2,1)}, u32[]{:S(2)}, u32[]{:S(2)}) collective-permute-start(bf16[4,4,48,384]{3,2,1,0:T(8,128)(2,1)} %slice_bitcast_fusion.9), channel_id=1, source_target_pairs={{0,4},{4,0},{8,12},{12,8},{16,20},{20,16},{24,28},{28,24},{1,5},{5... | collective-permute-start | bytes 1769480 | tf_op jit(solution)/shard_map/ppermute | solution.py:655
  301.9 49.5 %collective-permute-start.41 = (bf16[4,176,384]{2,1,0:T(8,128)(2,1)S(1)}, bf16[4,176,384]{2,1,0:T(8,128)(2,1)S(1)}, u32[]{:S(2)}, u32[]{:S(2)}) collective-permute-start(bf16[4,176,384]{2,1,0:T(8,128)(2,1)S(1)} %get-tuple-element.226), channel_id=1, source_target_pairs={{0,24},{4,28},{8,16},{12,20},{16,8},{20,12},{24,0},{28,4},{1,25},{... | collective-permute-start | bytes 1622024 | tf_op jit(solution)/shard_map/ppermute | solution.py:655
  303.6 47.8 %collective-permute-start.40 = (bf16[4,176,384]{2,1,0:T(8,128)(2,1)S(1)}, bf16[4,176,384]{2,1,0:T(8,128)(2,1)S(1)}, u32[]{:S(2)}, u32[]{:S(2)}) collective-permute-start(bf16[4,176,384]{2,1,0:T(8,128)(2,1)S(1)} %get-tuple-element.227), channel_id=1, source_target_pairs={{0,16},{4,20},{8,24},{12,28},{16,0},{20,4},{24,8},{28,12},{1,17},{... | collective-permute-start | bytes 1622024 | tf_op jit(solution)/shard_map/ppermute | solution.py:655
  304.9 46.5 %collective-permute-start.39 = (bf16[4,176,384]{2,1,0:T(8,128)(2,1)S(1)}, bf16[4,176,384]{2,1,0:T(8,128)(2,1)S(1)}, u32[]{:S(2)}, u32[]{:S(2)}) collective-permute-start(bf16[4,176,384]{2,1,0:T(8,128)(2,1)S(1)} %get-tuple-element.225), channel_id=1, source_target_pairs={{0,8},{4,12},{8,0},{12,4},{16,24},{20,28},{24,16},{28,20},{1,9},{5... | collective-permute-start | bytes 1622024 | tf_op jit(solution)/shard_map/ppermute | solution.py:655
  320.3 43.4 %collective-permute-start.42 = (bf16[4,4,80,384]{3,2,1,0:T(8,128)(2,1)S(1)}, bf16[4,4,80,384]{3,2,1,0:T(8,128)(2,1)S(1)}, u32[]{:S(2)}, u32[]{:S(2)}) collective-permute-start(bf16[4,4,80,384]{3,2,1,0:T(8,128)(2,1)S(1)} %slice_bitcast_fusion.5), channel_id=1, source_target_pairs={{0,4},{4,0},{8,12},{12,8},{16,20},{20,16},{24,28},{28,24},{1,5},{5... | collective-permute-start | bytes 2949128 | tf_op jit(solution)/shard_map/ppermute | solution.py:655
  373.2 54.4 %collective-permute-start.49 = (bf16[4,4,176,384]{3,2,1,0:T(8,128)(2,1)}, bf16[4,4,176,384]{3,2,1,0:T(8,128)(2,1)S(1)}, u32[]{:S(2)}, u32[]{:S(2)}) collective-permute-start(bf16[4,4,176,384]{3,2,1,0:T(8,128)(2,1)} %slice_bitcast_fusion), channel_id=1, source_target_pairs={{0,4},{4,0},{8,12},{12,8},{16,20},{20,16},{24,28},{28,24},{1,5},{5... | collective-permute-start | bytes 6488072 | tf_op jit(solution)/shard_map/ppermute | solution.py:655
  384.7 29.7 %collective-permute-start.73 = (bf16[128,384]{1,0:T(8,128)(2,1)S(1)}, bf16[128,384]{1,0:T(8,128)(2,1)S(1)}, u32[]{:S(2)}, u32[]{:S(2)}) collective-permute-start(bf16[128,384]{1,0:T(8,128)(2,1)S(1)} %get-tuple-element.265), channel_id=1, source_target_pairs={{0,1},{1,2},{2,3},{3,0},{4,5},{5,6},{6,7},{7,4},{8,9},{9,10},{10,1... | collective-permute-start | bytes 294920 | tf_op jit(solution)/shard_map/ppermute | solution.py:660
  386.5 27.9 %collective-permute-start.72 = (bf16[128,384]{1,0:T(8,128)(2,1)S(1)}, bf16[128,384]{1,0:T(8,128)(2,1)S(1)}, u32[]{:S(2)}, u32[]{:S(2)}) collective-permute-start(bf16[128,384]{1,0:T(8,128)(2,1)S(1)} %get-tuple-element.266), channel_id=1, source_target_pairs={{0,2},{1,3},{2,0},{3,1},{4,6},{5,7},{6,4},{7,5},{8,10},{9,11},{10,... | collective-permute-start | bytes 294920 | tf_op jit(solution)/shard_map/ppermute | solution.py:660
  386.8 27.6 %collective-permute-start.71 = (bf16[128,384]{1,0:T(8,128)(2,1)S(1)}, bf16[128,384]{1,0:T(8,128)(2,1)S(1)}, u32[]{:S(2)}, u32[]{:S(2)}) collective-permute-start(bf16[128,384]{1,0:T(8,128)(2,1)S(1)} %get-tuple-element.264), channel_id=1, source_target_pairs={{0,3},{1,0},{2,1},{3,2},{4,7},{5,4},{6,5},{7,6},{8,11},{9,8},{10,9... | collective-permute-start | bytes 294920 | tf_op jit(solution)/shard_map/ppermute | solution.py:660
  419.0 29.5 %collective-permute-start.59 = (bf16[4,4,48,384]{3,2,1,0:T(8,128)(2,1)}, bf16[4,4,48,384]{3,2,1,0:T(8,128)(2,1)}, u32[]{:S(2)}, u32[]{:S(2)}) collective-permute-start(bf16[4,4,48,384]{3,2,1,0:T(8,128)(2,1)} %slice_bitcast_fusion.8), channel_id=1, source_target_pairs={{0,4},{4,0},{8,12},{12,8},{16,20},{20,16},{24,28},{28,24},{1,5},{5... | collective-permute-start | bytes 1769480 | tf_op jit(solution)/shard_map/ppermute | solution.py:655
  427.5 47.4 %collective-permute-start.77 = (bf16[4,304,384]{2,1,0:T(8,128)(2,1)S(1)}, bf16[4,304,384]{2,1,0:T(8,128)(2,1)}, u32[]{:S(2)}, u32[]{:S(2)}) collective-permute-start(bf16[4,304,384]{2,1,0:T(8,128)(2,1)S(1)} %pad_maximum_fusion.6.refs_3_.refs_1_), channel_id=1, source_target_pairs={{0,4},{4,0},{8,12},{12,8},{16,20},{20,16},{24,28},{28,24},{1,5},{5... | collective-permute-start | bytes 2801672 | tf_op jit(solution)/shard_map/ppermute | solution.py:655
  444.9 32.5 %collective-permute-start.60 = (bf16[4,4,80,384]{3,2,1,0:T(8,128)(2,1)S(1)}, bf16[4,4,80,384]{3,2,1,0:T(8,128)(2,1)S(1)}, u32[]{:S(2)}, u32[]{:S(2)}) collective-permute-start(bf16[4,4,80,384]{3,2,1,0:T(8,128)(2,1)S(1)} %slice_bitcast_fusion.4), channel_id=1, source_target_pairs={{0,4},{4,0},{8,12},{12,8},{16,20},{20,16},{24,28},{28,24},{1,5},{5... | collective-permute-start | bytes 2949128 | tf_op jit(solution)/shard_map/ppermute | solution.py:655
  446.5 23.4 %collective-permute-start.51 = (bf16[192,768]{1,0:T(8,128)(2,1)S(1)}, bf16[192,768]{1,0:T(8,128)(2,1)S(1)}, u32[]{:S(2)}, u32[]{:S(2)}) collective-permute-start(bf16[192,768]{1,0:T(8,128)(2,1)S(1)} %get-tuple-element.239), channel_id=1, source_target_pairs={{0,2},{1,3},{2,0},{3,1},{4,6},{5,7},{6,4},{7,5},{8,10},{9,11},{10,... | collective-permute-start | bytes 884744 | tf_op jit(solution)/shard_map/ppermute | solution.py:660
  477.8 23.5 %collective-permute-start.63 = (bf16[4,128,384]{2,1,0:T(8,128)(2,1)S(1)}, bf16[4,128,384]{2,1,0:T(8,128)(2,1)S(1)}, u32[]{:S(2)}, u32[]{:S(2)}) collective-permute-start(bf16[4,128,384]{2,1,0:T(8,128)(2,1)S(1)} %get-tuple-element.231), channel_id=1, source_target_pairs={{0,24},{4,28},{8,16},{12,20},{16,8},{20,12},{24,0},{28,4},{1,25},{... | collective-permute-start | bytes 1179656 | tf_op jit(solution)/shard_map/ppermute | solution.py:655
  (145 other events, 1588.7 us)

commit v2 on v1

--- a/solution.py
+++ b/solution.py
@@ -22,8 +22,8 @@
 IN_ONE, IN_TWO, OUT_ROWS, PARAM_ROWS = 0, 192, 576, 768
 UP_ONE, UP_TWO, DOWN_ONE = 0, 192, 960
 MIX_ROWS, FF_USED, FF_ROWS, IN_GRAD_ROWS = 1024, 1344, 1408, 640
+HIDDEN_ONE, HIDDEN_TWO, SLOPE_ONE, SLOPE_TWO = 0, 1, 2, 3
 PIECE_ROWS = {"ff": 176, "conv": 48, "in": 80}
-FINISH_ORDER = (("ff", "conv", "in"),) * LAYERS
 
 
 def nn(a, b):
@@ -182,14 +182,14 @@
         rows = pl.ds(c * BLOCK_W, BLOCK_W)
         value = middle[rows, :] + tn(w[c, UP_ONE : UP_ONE + 192, 192:384], q4[c])
         if last:
-            h_next[(c - idx[0]) & (BLOCKS - 1)] = value.astype(BF16)
+            h_next[c] = value.astype(BF16)
         else:
             h_next[rows, :] = value
 
 
 def bwd_ff_kernel(last, idx, own, rel_a, rel_b, *refs):
     parts = refs[: BLOCKS if last else 1]
-    q4, gate_up, q3, middle, stats, cols, g_mid, g_out, small, w, g_w, g_low, gi4, gi3, g_gu, g_n, sem = refs[len(parts) :]
+    q4, gate_up, q3, middle, stats, cols, g_mid, g_near, g_far, small, w, g_w, g_low, gi4, gi3, g_gu, g_n, sem = refs[len(parts) :]
     fetch_table(idx, own, rel_a, rel_b, w, sem)
     mean = stats[0:1, :]
     inv = stats[1:2, :]
@@ -238,7 +238,7 @@
     norm_back(
         middle, mean, inv, cols, GAIN_TWO, w, slice(UP_ONE, UP_ONE + 192), slice(0, 192), gi3, g_n, g_w, small, 1, g_top, g_mid
     )
-    send_pieces(g_w, g_out, idx, sem)
+    send_pieces(g_w, (g_near, g_far), idx, sem)
 
 
 def gelu_slope(gate, square, t, rate):
@@ -278,7 +278,8 @@
 
 
 def bwd_conv_kernel(
-    seqs, idx, own, rel_a, rel_b, g_mid, q2, gated, conv, proj, pad, cols, kspec, ahead, back, small_ff, gv, g_out, w, g_w, gi2, gcs, xs, sem
+    seqs, penalty, idx, own, rel_a, rel_b, g_mid, q2, gated, conv, proj, pad, cols, kspec, ahead, back, small_ff,
+    filt, weight_two, features, back_full, gv, g_near, g_far, w, g_w, gi2, gcs, xs, sem
 ):
     fetch_table(idx, own, rel_a, rel_b, w, sem)
     for c in range(BLOCKS):
@@ -346,8 +347,21 @@
             made.append(
                 jnp.concatenate([g_re * k_re + g_im * k_off, g_im * k_im - g_re * k_off], axis=1).astype(BF16)
             )
-        g_w[b, 192:384, 0:128] = jnp.where(first_lane, p_re, p_re + p_im).astype(BF16)
-        g_w[b, 192:384, 128:256] = jnp.where(first_lane, p_im, p_off).astype(BF16)
+        g_table = exact(
+            jnp.concatenate(
+                [jnp.where(first_lane, p_re, p_re + p_im), jnp.where(first_lane, p_im, p_off)], axis=1
+            ),
+            back_full[...],
+            1,
+            0,
+        )
+        last, envelope, table = filter_values(w, b, cols, filt[HIDDEN_TWO])
+        g_table = g_table + penalty * table
+        g_decay = -(g_table * table * filter_lag())
+        g_shape = g_table * envelope
+        g_w[b, 192:384, 0:128] = exact(g_shape, filt[HIDDEN_TWO], 1, 0).astype(BF16)
+        term = exact(g_shape, last, 0, 0)
+        g_hidden = term if b == 0 else g_hidden + term
         y = nn(jnp.concatenate(made, axis=0), back[...])
         for s in range(seqs):
             here = slice(s * LENGTH, (s + 1) * LENGTH)
@@ -365,14 +379,22 @@
                 * pad[0:1, here]
             ).astype(BF16)
         table = small_ff[b]
-        for at, value in enumerate(sums):
+        for at, value in enumerate(sums + [g_decay]):
             table = table + row_sums(2 + at, value)
         table = table.astype(BF16)
         g_w[b, 192:208, 256:384] = table[:, 0:128]
         g_w[b, 208:224, 256:320] = table[:, 128:192]
         g_w[b, 208:224, 320:384] = jnp.zeros((16, 64), BF16)
         g_w[b, 224:384, 256:384] = jnp.zeros((160, 128), BF16)
-    send_pieces(g_w, g_out, idx, sem)
+    g_two = g_hidden * filt[SLOPE_TWO]
+    g_one = exact(g_two, weight_two[...], 1, 1) * filt[SLOPE_ONE]
+    g_weight_two = exact(filt[HIDDEN_ONE], g_two, 0, 0).astype(BF16)
+    g_weight_one = exact(features[...], g_one, 0, 0)[0:16, :].astype(BF16)
+    for b in range(BLOCKS):
+        g_w[b, 192:320, 128:256] = g_weight_two
+        g_w[b, 320:336, 128:256] = g_weight_one
+        g_w[b, 336:384, 128:256] = jnp.zeros((48, 128), BF16)
+    send_pieces(g_w, (g_near, g_far), idx, sem)
 
 
 def bwd_in_kernel(first, *refs):
@@ -380,8 +402,8 @@
     idx, own, rel_a, rel_b, gv, g_mid, q1, h, stats, cols = refs[:10]
     refs = refs[10:]
     chosen = refs.pop(0) if first else None
-    g_out, g_send, w, g_w, gi1, g_n, small, sem = refs[:8]
-    g_h = refs[8] if first else g_out
+    g_out, g_near, g_far, w, g_w, gi1, g_n, small, sem = refs[:9]
+    g_h = refs[9] if first else g_out
     fetch_table(idx, own, rel_a, rel_b, w, sem)
     mean = stats[0:1, :]
     inv = stats[1:2, :]
@@ -400,11 +422,11 @@
             value = g_h[rows, :]
             masked = value * chosen[0:1, :]
             table = table + row_sums(1, masked)
-            g_out[(b - idx[0]) & (BLOCKS - 1)] = (value - masked).astype(BF16)
+            g_out[b] = (value - masked).astype(BF16)
         g_w[b, 576:592, 0:192] = table.astype(BF16)
         g_w[b, 576:592, 192:384] = jnp.zeros((16, 192), BF16)
         g_w[b, 592:640, :] = jnp.zeros((48, 384), BF16)
-    send_pieces(g_w, g_send, idx, sem)
+    send_pieces(g_w, (g_near, g_far), idx, sem)
 
 
 def piece_rows(idx, core, chip, rows):
@@ -423,11 +445,11 @@
         copy.wait()
 
 
-def send_pieces(table, out, idx, sem):
-    rows = out.shape[3]
+def send_pieces(table, outs, idx, sem):
+    rows = outs[0].shape[2]
     run_copies(
         [
-            (table.at[block_of(idx, k), piece_rows(idx, core, chip, rows), :], out.at[core, chip, k])
+            (table.at[block_of(idx, k), piece_rows(idx, core, chip, rows), :], outs[core].at[chip, k])
             for core in range(2)
             for chip in range(4)
             for k in range(BLOCKS)
@@ -450,26 +472,32 @@
     )
 
 
+def exact(a, b, left, right):
+    return lax.dot_general(
+        a, b, (((left,), (right,)), ((), ())), precision=HIGHEST, preferred_element_type=F32
+    )
+
+
+def filter_lag():
+    place = lanes_of((BLOCK_W, 2 * LENGTH))
+    return jnp.where(place < LENGTH, place, 2 * LENGTH - place).astype(F32)
+
+
+def filter_values(w, b, cols, hidden):
+    packed = w[b, PARAM_ROWS : PARAM_ROWS + BLOCK_W, 0:256].astype(F32)
+    last = packed[:, 0:128] + packed[:, 128:256]
+    lag = filter_lag()
+    envelope = jnp.exp(-lag * cols[b * BLOCK_W : (b + 1) * BLOCK_W, DECAY : DECAY + 1]) * (1.0 / math.sqrt(LENGTH))
+    envelope = jnp.where(lag == LENGTH, 0.0, envelope)
+    return last, envelope, exact(last, hidden, 1, 1) * envelope
+
+
 def make_params(w, hidden, ahead_full, cols, kspec):
-    place = lanes_of((BLOCK_W, 2 * LENGTH))
-    lag = jnp.where(place < LENGTH, place, 2 * LENGTH - place).astype(F32)
     for b in range(BLOCKS):
         rows = pl.ds(b * BLOCK_W, BLOCK_W)
-        packed = w[b, PARAM_ROWS : PARAM_ROWS + BLOCK_W, :].astype(F32)
-        three = packed[:, 256:384]
+        three = w[b, PARAM_ROWS : PARAM_ROWS + BLOCK_W, 256:384].astype(F32)
         cols[rows, :] = three + pltpu.roll(three, 128 - 16, 1) + pltpu.roll(three, 128 - 32, 1)
-        shaped_rows = lax.dot_general(
-            packed[:, 0:128] + packed[:, 128:256],
-            hidden[...],
-            (((1,), (1,)), ((), ())),
-            precision=HIGHEST,
-            preferred_element_type=F32,
-        )
-        envelope = jnp.exp(-lag * cols[rows, DECAY : DECAY + 1])
-        table = jnp.where(place == LENGTH, 0.0, shaped_rows * envelope * (1.0 / math.sqrt(LENGTH)))
-        kspec[rows, :] = lax.dot_general(
-            table, ahead_full[...], (((1,), (0,)), ((), ())), precision=HIGHEST, preferred_element_type=F32
-        )
+        kspec[rows, :] = exact(filter_values(w, b, cols, hidden[HIDDEN_TWO])[2], ahead_full[...], 1, 0)
 
 
 def fold_back(lines, wide, count):
@@ -507,114 +535,132 @@
     return jnp.concatenate([wide[0, 0:count, :], wide[1, 0:count, 0:64]], axis=1).astype(BF16)
 
 
-def own_piece(idx, table, out, layer):
-    rows = out.shape[1]
-    out[layer] = table[layer, pl.ds(pl.multiple_of(idx[1] * rows, 16), rows), :]
-
-
-def pack_mix_kernel(idx, in_one, in_two, out_one, out_two, params, table, out, lines, wide):
+def own_piece(idx, table, out):
+    rows = out.shape[0]
+    out[...] = table[pl.ds(pl.multiple_of(idx[1] * rows, 16), rows), :]
+
+
+def pack_mix_kernel(
+    idx, in_one, in_two, out_one, out_two, gain_one, gain_two, skip, taps, mask, decay, filter_three,
+    table_a, table_b, piece_a, piece_b, lines, wide, cols,
+):
+    tables, pieces = (table_a, table_b), (piece_a, piece_b)
+    eye = (
+        lax.broadcasted_iota(jnp.int32, (16, 128), 0) == lax.broadcasted_iota(jnp.int32, (16, 128), 1)
+    ).astype(F32)
+    cols[...] = jnp.zeros((16, BLOCK_W), F32)
     for layer in range(LAYERS):
+        table = tables[layer]
         for flat, start, count in ((in_one, IN_ONE, 192), (in_two, IN_TWO, 384)):
             for j, part in enumerate(spread_lines(flat, layer, count, 3, lines)):
-                table[layer, start : start + count, 128 * j : 128 * j + 128] = part.astype(BF16)
-        table[layer, OUT_ROWS : OUT_ROWS + 192, 0:192] = narrow_lines(out_one, layer, 192, lines, wide)
-        table[layer, OUT_ROWS : OUT_ROWS + 192, 192:384] = narrow_lines(out_two, layer, 192, lines, wide)
-        last = params[layer, :, 128:256]
+                table[start : start + count, 128 * j : 128 * j + 128] = part.astype(BF16)
+        table[OUT_ROWS : OUT_ROWS + 192, 0:192] = narrow_lines(out_one, layer, 192, lines, wide)
+        table[OUT_ROWS : OUT_ROWS + 192, 192:384] = narrow_lines(out_two, layer, 192, lines, wide)
+        last = filter_three[layer]
         high = last.astype(BF16)
         rows = slice(PARAM_ROWS, PARAM_ROWS + BLOCK_W)
-        table[layer, rows, 0:128] = high
-        table[layer, rows, 128:256] = (last - high.astype(F32)).astype(BF16)
-        left = params[layer, :, 0:128]
+        table[rows, 0:128] = high
+        table[rows, 128:256] = (last - high.astype(F32)).astype(BF16)
+        for at, source in ((GAIN_ONE, gain_one), (GAIN_TWO, gain_two), (SKIP, skip), (DECAY, decay)):
+            cols[at : at + 1, :] = source[layer : layer + 1, :]
+        cols[TAP_X : TAP_X + 3, :] = taps[layer, :, 0:BLOCK_W]
+        cols[TAP_G : TAP_G + 3, :] = taps[layer, :, BLOCK_W : 2 * BLOCK_W]
+        cols[MASK : MASK + 1, :] = mask[...]
+        left = lax.dot_general(
+            cols[...], eye, (((0,), (0,)), ((), ())), precision=HIGHEST, preferred_element_type=F32
+        )
         terms = jnp.zeros((BLOCK_W, 128), F32)
         for at in range(3):
             part = left.astype(BF16).astype(F32)
             left = left - part
             terms = terms + (pltpu.roll(part, 16 * at, 1) if at else part)
-        table[layer, rows, 256:384] = terms.astype(BF16)
-        table[layer, PARAM_ROWS + BLOCK_W : MIX_ROWS, :] = jnp.zeros((MIX_ROWS - PARAM_ROWS - BLOCK_W, 384), BF16)
-        own_piece(idx, table, out, layer)
-
-
-def pack_ff_kernel(idx, up_one, up_two, down_one, down_two, table, out, lines, wide):
+        table[rows, 256:384] = terms.astype(BF16)
+        table[PARAM_ROWS + BLOCK_W : MIX_ROWS, :] = jnp.zeros((MIX_ROWS - PARAM_ROWS - BLOCK_W, 384), BF16)
+        own_piece(idx, table, pieces[layer])
+
+
+def pack_ff_kernel(idx, up_one, up_two, down_one, down_two, table_a, table_b, piece_a, piece_b, lines, wide):
+    tables, pieces = (table_a, table_b), (piece_a, piece_b)
     for layer in range(LAYERS):
-        table[layer, UP_ONE : UP_ONE + 192, 0:192] = narrow_lines(up_one, layer, 192, lines, wide)
-        table[layer, UP_ONE : UP_ONE + 192, 192:384] = narrow_lines(down_two, layer, 192, lines, wide)
+        table = tables[layer]
+        table[UP_ONE : UP_ONE + 192, 0:192] = narrow_lines(up_one, layer, 192, lines, wide)
+        table[UP_ONE : UP_ONE + 192, 192:384] = narrow_lines(down_two, layer, 192, lines, wide)
         for j, part in enumerate(spread_lines(up_two, layer, 192, 12, lines)):
             at = UP_TWO + 192 * (j // 3)
-            table[layer, at : at + 192, 128 * (j % 3) : 128 * (j % 3) + 128] = part.astype(BF16)
+            table[at : at + 192, 128 * (j % 3) : 128 * (j % 3) + 128] = part.astype(BF16)
         down = narrow_lines(down_one, layer, 768, lines, wide)
-        table[layer, DOWN_ONE : DOWN_ONE + 384, 0:192] = down[0:384]
-        table[layer, DOWN_ONE : DOWN_ONE + 384, 192:384] = down[384:768]
-        table[layer, FF_USED:FF_ROWS, :] = jnp.zeros((FF_ROWS - FF_USED, 384), BF16)
-        own_piece(idx, table, out, layer)
-
-
-def finish_kernel(idx, *refs):
-    pieces = refs[: 2 * len(FINISH_ORDER)]
-    refs = refs[2 * len(FINISH_ORDER) :]
-    in_one, in_two, out_one, out_two, up_one, up_two, down_one, down_two, small = refs[:9]
-    ff, conv, inp, wide, sem = refs[9:]
-    tables = {"ff": ff, "conv": conv, "in": inp}
+        table[DOWN_ONE : DOWN_ONE + 384, 0:192] = down[0:384]
+        table[DOWN_ONE : DOWN_ONE + 384, 192:384] = down[384:768]
+        table[FF_USED:FF_ROWS, :] = jnp.zeros((FF_ROWS - FF_USED, 384), BF16)
+        own_piece(idx, table, pieces[layer])
+
+
+def finish_kernel(layer, idx, *refs):
+    pieces, refs = refs[:2], refs[2:]
+    if layer == 0:
+        other, refs = refs[9], refs[10:]
+    in_one, in_two, out_one, out_two, up_one, up_two, down_one, down_two, three = refs[:9]
+    rest, (ff, conv, inp, wide, sem) = refs[9:-5], refs[-5:]
     pairs = []
-    for at, group in enumerate(FINISH_ORDER):
-        for core in range(2):
-            rel = pieces[2 * at + core]
-            first = 0
-            for name in group:
-                rows = PIECE_ROWS[name]
-                for chip in range(4):
-                    pairs.append(
-                        (
-                            rel.at[chip, pl.ds(first, rows), :],
-                            tables[name].at[at, piece_rows(idx, core, chip, rows), :],
-                        )
-                    )
-                first += rows
+    for core, rel in enumerate(pieces):
+        first = 0
+        for name, table in (("ff", ff), ("conv", conv), ("in", inp)):
+            rows = PIECE_ROWS[name]
+            for chip in range(4):
+                pairs.append((rel.at[chip, pl.ds(first, rows), :], table.at[piece_rows(idx, core, chip, rows), :]))
+            first += rows
     run_copies(pairs, sem)
 
-    def spread(out, layer, values, lanes, first):
+    def spread(out, values, lanes, first):
         count = values.shape[0]
         for j in range(3):
-            out[layer, pl.ds(first + j, count, stride=lanes), :] = values[:, 128 * j : 128 * j + 128].astype(F32)
-
-    def narrow_of(out, layer, values):
+            out[pl.ds(first + j, count, stride=lanes), :] = values[:, 128 * j : 128 * j + 128].astype(F32)
+
+    def narrow_of(out, values):
         count = values.shape[0]
         wide[0, 0:count, :] = values[:, 0:128].astype(F32)
         wide[1, 0:count, 0:64] = values[:, 128:192].astype(F32)
-        fold_out(wide, out.at[layer], count)
-
-    for layer in range(LAYERS):
-        spread(in_one, layer, inp[layer, IN_ONE : IN_ONE + 192, :], 3, 0)
-        spread(in_two, layer, inp[layer, IN_TWO : IN_TWO + 384, :], 3, 0)
-        for q in range(4):
-            at = UP_TWO + 192 * q
-            spread(up_two, layer, ff[layer, at : at + 192, :], 12, 3 * q)
-        narrow_of(out_one, layer, conv[layer, 0:192, 0:192])
-        narrow_of(out_two, layer, conv[layer, 0:192, 192:384])
-        narrow_of(up_one, layer, ff[layer, UP_ONE : UP_ONE + 192, 0:192])
-        narrow_of(down_two, layer, ff[layer, UP_ONE : UP_ONE + 192, 192:384])
-        narrow_of(
-            down_one,
-            layer,
-            jnp.concatenate(
-                [ff[layer, DOWN_ONE : DOWN_ONE + 384, 0:192], ff[layer, DOWN_ONE : DOWN_ONE + 384, 192:384]], axis=0
-            ),
-        )
-        small[layer, 0:16, 0:128] = conv[layer, 192:208, 256:384].astype(F32)
-        small[layer, 0:16, 128:256] = conv[layer, 208:224, 256:384].astype(F32)
-        small[layer, 16:32, 0:256] = inp[layer, 576:592, 0:256].astype(F32)
-
-
-def join_kernel(first, idx, rel_a, rel_b, out, sem):
-    rows = PIECE_ROWS["conv"]
-    run_copies(
-        [
-            (rel.at[chip, pl.ds(first, rows), :], out.at[piece_rows(idx, core, chip, rows), :])
-            for core, rel in enumerate((rel_a, rel_b))
-            for chip in range(4)
-        ],
-        sem,
+        fold_out(wide, out, count)
+
+    spread(in_one, inp[IN_ONE : IN_ONE + 192, :], 3, 0)
+    spread(in_two, inp[IN_TWO : IN_TWO + 384, :], 3, 0)
+    for q in range(4):
+        at = UP_TWO + 192 * q
+        spread(up_two, ff[at : at + 192, :], 12, 3 * q)
+    narrow_of(out_one, conv[0:192, 0:192])
+    narrow_of(out_two, conv[0:192, 192:384])
+    narrow_of(up_one, ff[UP_ONE : UP_ONE + 192, 0:192])
+    narrow_of(down_two, ff[UP_ONE : UP_ONE + 192, 192:384])
+    narrow_of(
+        down_one,
+        jnp.concatenate([ff[DOWN_ONE : DOWN_ONE + 384, 0:192], ff[DOWN_ONE : DOWN_ONE + 384, 192:384]], axis=0),
     )
+    three[...] = conv[192:384, 0:128].astype(F32)
+    if layer > 0:
+        rest[0][0:192, :] = conv[192:384, 128:384].astype(F32)
+        rest[0][192:208, :] = inp[576:592, 0:256].astype(F32)
+        return
+    g_gain_one, g_gain_two, g_skip, g_taps, g_decay, g_mask, g_one, g_bias, g_two = rest
+    for at in range(LAYERS):
+        if at:
+            shared, small, last = other[0:192, 0:128], other[0:32, 128:256], other[192:208, 0:192]
+        else:
+            shared = conv[192:384, 128:256].astype(F32)
+            small = conv[192:224, 256:384].astype(F32)
+            last = inp[576:592, 0:192].astype(F32)
+        small = jnp.concatenate([small[0:16], small[16:32, 0:64]], axis=1)
+        here = slice(at, at + 1)
+        g_gain_one[here, :] = last[0:1]
+        g_gain_two[here, :] = small[1:2]
+        g_skip[here, :] = small[2:3]
+        g_taps[at, :, 0:192] = small[3:6]
+        g_taps[at, :, 192:384] = small[6:9]
+        g_decay[here, :] = small[9:10]
+        g_two[at] = shared[0:128]
+        g_one[at] = shared[128:133]
+        g_bias[here, :] = shared[133:134]
+        if at == 0:
+            g_mask[...] = last[1:2]
 
 
 ANY = pl.BlockSpec(memory_space=pl.ANY)
@@ -626,7 +672,7 @@
     return jax.ShapeDtypeStruct(shape, dtype)
 
 
-def call(kernel, outs, scratch, in_specs, out_specs, micros, deps=()):
+def call(kernel, outs, scratch, in_specs, out_specs, micros, deps=(), aliases=None):
     count = len(in_specs)
 
     def body(*refs):
@@ -638,17 +684,17 @@
         in_specs=list(in_specs) + [ANY] * len(deps),
         out_specs=out_specs,
         scratch_shapes=scratch,
+        input_output_aliases=aliases or {},
         compiler_params=pltpu.CompilerParams(vmem_limit_bytes=56 << 20),
         cost_estimate=pl.CostEstimate(flops=int(micros * 1e9), bytes_accessed=1 << 20, transcendentals=0),
     )
     return lambda *arrays: made(*arrays, *deps)
 
 
-def place_parts_kernel(idx, *refs):
-    parts, out = refs[:BLOCKS], refs[BLOCKS]
-    span = parts[0].shape[1]
-    for k, part in enumerate(parts):
-        out[:, pl.ds(pl.multiple_of(block_of(idx, k) * span, 128), span)] = part[...].astype(out.dtype)
+def place_parts_kernel(table, out):
+    span = table.shape[2]
+    for b in range(BLOCKS):
+        out[:, b * span : (b + 1) * span] = table[b].astype(out.dtype)
 
 
 def wide_shift(x, mask):
@@ -668,6 +714,10 @@
     return lax.optimization_barrier((x, deps))[0]
 
 
+def settle(*trees):
+    return lax.optimization_barrier(trees)
+
+
 def exchange(parts):
     return [parts[0]] + [narrow_shift(parts[k], k) for k in range(1, BLOCKS)]
 
@@ -676,19 +726,29 @@
     return jnp.stack([narrow_shift(piece, k) for k in range(1, BLOCKS)])
 
 
+def others_at_once(piece, me):
+    moved = lax.all_to_all(jnp.stack([piece] * BLOCKS), "narrow", split_axis=0, concat_axis=0, tiled=True)
+    return jnp.stack([lax.dynamic_index_in_dim(moved, (me - k) % BLOCKS, 0, keepdims=False) for k in range(1, BLOCKS)])
+
+
 def over_chips(x):
     return jnp.stack([x] + [wide_shift(x, 2 * m) for m in range(1, 4)])
 
 
-def reduce_core(table):
-    return added([table[0], wide_shift(table[1], 1)])
-
-
-def reduce_chips(half):
-    total = added([half[0]] + [wide_shift(half[m], 2 * m) for m in range(1, 4)])
+def reduce_core(near, far):
+    moved = wide_shift(far, 1)
+    return [added([near[m], moved[m]]) for m in range(4)]
+
+
+def move_chips(half):
+    return [half[0]] + [wide_shift(half[m], 2 * m) for m in range(1, 4)]
+
+
+def add_chips(parts):
+    total = [added([part[k] for part in parts]) for k in range(BLOCKS)]
     groups = lax.axis_size("wide") // 8
     if groups > 1:
-        total = added([total] + [wide_shift(total, 8 * g) for g in range(1, groups)])
+        total = [added([t] + [wide_shift(t, 8 * g) for g in range(1, groups)]) for t in total]
     return total
 
 
@@ -696,39 +756,40 @@
     return added([total[0]] + [narrow_shift(total[k], -k) for k in range(1, BLOCKS)])
 
 
+def blocks_at_once(total, me):
+    table = jnp.stack(total)
+    table = jnp.stack([lax.dynamic_index_in_dim(table, (me - b) % BLOCKS, 0, keepdims=False) for b in range(BLOCKS)])
+    moved = lax.all_to_all(table, "narrow", split_axis=0, concat_axis=0, tiled=True)
+    return [moved[b] for b in range(BLOCKS)]
+
+
 def join_rows(*tables):
-    return jnp.concatenate(tables, axis=-2)
-
-
-def filter_lags():
-    place = jnp.arange(2 * LENGTH)
-    return place, jnp.where(place < LENGTH, place, place - 2 * LENGTH).astype(F32)
-
-
-def filter_hidden(weight_one, bias_one, weight_two):
-    relative = filter_lags()[1] / LENGTH
-    features = jnp.stack(
-        [
+    return [jnp.concatenate(parts, axis=-2) for parts in zip(*tables)]
+
+
+def filter_features():
+    place = np.arange(2 * LENGTH)
+    relative = np.where(place < LENGTH, place, place - 2 * LENGTH) / LENGTH
+    table = np.zeros((2 * LENGTH, 128))
+    for at, value in enumerate(
+        (
             relative,
-            jnp.cos(math.pi * relative),
-            jnp.sin(math.pi * relative),
-            jnp.cos(37.0 * math.pi * relative),
-            jnp.sin(37.0 * math.pi * relative),
-        ],
-        axis=1,
-    )
-    hidden_one = jnp.sin(jnp.dot(features, weight_one, precision=HIGHEST) + bias_one)
-    return jnp.sin(jnp.dot(hidden_one, weight_two, precision=HIGHEST))
-
-
-def filter_table(weight_one, bias_one, weight_two, weight_three, decay_rate):
-    place, lag = filter_lags()
-    hidden_two = filter_hidden(weight_one, bias_one, weight_two)
-    shaped_rows = lax.dot_general(
-        weight_three, hidden_two, (((1,), (1,)), ((), ())), precision=HIGHEST, preferred_element_type=F32
-    )
-    envelope = jnp.exp(-jnp.abs(lag)[None, :] * decay_rate[:, None])
-    return jnp.where(place[None, :] == LENGTH, 0.0, shaped_rows * envelope / math.sqrt(LENGTH))
+            np.cos(np.pi * relative),
+            np.sin(np.pi * relative),
+            np.cos(37.0 * np.pi * relative),
+            np.sin(37.0 * np.pi * relative),
+            np.ones_like(relative),
+        )
+    ):
+        table[:, at] = value
+    return jnp.asarray(table.astype(np.float32))
+
+
+def filter_hidden(features, weight_one, bias_one, weight_two):
+    one = jnp.dot(features[:, :5], weight_one, precision=HIGHEST) + bias_one
+    hidden_one = jnp.sin(one)
+    two = jnp.dot(hidden_one, weight_two, precision=HIGHEST)
+    return jnp.stack([hidden_one, jnp.sin(two), jnp.cos(one), jnp.cos(two)])
 
 
 def local(
@@ -773,44 +834,34 @@
     lines = [flat_lines(weight) for weight in factors]
     tokens_here = exchange(token_parts(tokens))
 
-    columns = jnp.concatenate(
-        [
-            gain_one[:, None],
-            gain_two[:, None],
-            skip_gain[:, None],
-            short_taps[:, :, 0, :BLOCK_W],
-            short_taps[:, :, 0, BLOCK_W:],
-            jnp.broadcast_to(mask_vector, (LAYERS, 1, BLOCK_W)),
-            decay_rates[:, None],
-            jnp.zeros((LAYERS, 5, BLOCK_W), F32),
-        ],
-        axis=1,
-    )
-    columns = jnp.pad(columns.transpose(0, 2, 1), ((0, 0), (0, 0), (0, 112)))
-    params = jnp.concatenate([columns, filter_three], axis=2)
-
-    def pack(kernel, count, rows, arrays, micros):
+    def pack(kernel, rows, arrays, deps=(), scratch=()):
         return call(
             kernel,
-            [shaped(BF16, LAYERS, rows, 384), shaped(BF16, LAYERS, rows // 8, 384)],
-            [pltpu.VMEM((2304, 128), F32), pltpu.VMEM((2, 768, 128), F32)],
-            [SCALARS] + [WHOLE] * count,
-            [WHOLE] * 2,
-            micros,
+            [shaped(BF16, rows, 384)] * LAYERS + [shaped(BF16, rows // 8, 384)] * LAYERS,
+            [pltpu.VMEM((2304, 128), F32), pltpu.VMEM((2, 768, 128), F32)] + list(scratch),
+            [SCALARS] + [WHOLE] * len(arrays),
+            [WHOLE] * (2 * LAYERS),
+            3,
+            deps,
         )(idx, *arrays)
 
-    mix, mix_piece = pack(pack_mix_kernel, 5, MIX_ROWS, lines[:4] + [params], 3)
-    ff, ff_piece = pack(pack_ff_kernel, 4, FF_ROWS, lines[4:], 4)
-
-    weights_mix, weights_ff = [None] * LAYERS, [None] * LAYERS
-    previous = ()
-    for layer in range(LAYERS):
-        for own, piece, made in ((mix, mix_piece, weights_mix), (ff, ff_piece, weights_ff)):
-            others = over_blocks(after(piece[layer], *previous))
-            previous = (others,)
-            chips = over_chips(others)
-            made[layer] = (own[layer], chips, wide_shift(chips, 1))
-    cotangent_here = exchange(token_parts(after(cotangent, *previous)))
+    per_feature = [gain_one, gain_two, skip_gain, short_taps[:, :, 0], mask_vector[None], decay_rates, filter_three]
+    *mix, mix_zero, mix_one = pack(
+        pack_mix_kernel, MIX_ROWS, lines[:4] + per_feature, scratch=[pltpu.VMEM((16, BLOCK_W), F32)]
+    )
+    *ff, ff_zero, ff_one = pack(pack_ff_kernel, FF_ROWS, lines[4:], (mix_zero,))
+
+    parts = token_parts(tokens)
+    near, across, far = (narrow_shift(parts[k], k) for k in range(1, BLOCKS))
+    mix_zero = over_blocks(mix_zero)
+    ff_zero = over_blocks(after(ff_zero, mix_zero))
+    mix_chips = over_chips(after(mix_zero, near))
+    mix_chips, ff_zero, across, far = settle(mix_chips, ff_zero, across, far)
+    mix_zero = (mix[0], mix_chips, wide_shift(mix_chips, 1))
+    tokens_here = [parts[0], near, across, far]
+    mix_zero, tokens_here, ff_zero, mix_one = settle(mix_zero, tokens_here, ff_zero, mix_one)
+    ff_chips = over_chips(ff_zero)
+    mix_one = others_at_once(mix_one, me)
 
     own_lengths = lax.dynamic_slice_in_dim(lengths, me * seqs, seqs, 0)
     own_masked = lax.dynamic_slice_in_dim(masked, me * seqs, seqs, 0)
@@ -823,29 +874,21 @@
     ahead_low = jnp.asarray(ahead[:LENGTH]).astype(BF16)
     back_low = jnp.asarray(back[:, :LENGTH]).astype(BF16)
     ahead_full = jnp.asarray(ahead)
-    hidden = [filter_hidden(filter_one[layer], filter_bias[layer], filter_two[layer]) for layer in range(LAYERS)]
-    pulls = [
-        jax.vjp(
-            filter_table,
-            filter_one[layer],
-            filter_bias[layer],
-            filter_two[layer],
-            filter_three[layer],
-            decay_rates[layer],
-        )
-        for layer in range(LAYERS)
+    features = filter_features()
+    back_full = jnp.asarray(back)
+    hidden = [
+        filter_hidden(features, filter_one[layer], filter_bias[layer], filter_two[layer]) for layer in range(LAYERS)
     ]
+    penalty = 4.0 * math.sqrt(all_tokens) / (wide_count * BLOCKS)
     mix_scratch = pltpu.VMEM((BLOCKS, MIX_ROWS, 384), BF16)
     ff_scratch = pltpu.VMEM((BLOCKS, FF_ROWS, 384), BF16)
     fetched = pltpu.SemaphoreType.DMA((25,))
     sent = pltpu.SemaphoreType.DMA((32,))
     table_specs = [SCALARS, ANY, ANY, ANY]
 
-    h = None
-    saved = []
-    for layer in range(LAYERS):
-        first, last = layer == 0, layer == LAYERS - 1
-        made = call(
+    def ahead_mix(layer, table, h, deps=()):
+        first = layer == 0
+        return call(
             functools.partial(fwd_mix_kernel, first, seqs),
             ([shaped(F32, D, span)] if first else [])
             + [
@@ -869,20 +912,12 @@
             table_specs + [WHOLE] * (BLOCKS + 1 if first else 1) + [WHOLE] * 5,
             [WHOLE] * (10 if first else 9),
             18,
-        )(
-            idx,
-            *weights_mix[layer],
-            *([*tokens_here, chosen] if first else [h]),
-            pad,
-            hidden[layer],
-            ahead_full,
-            ahead_low,
-            back_low,
-        )
-        if first:
-            h, *made = made
-        q1, proj, conv, gated, q2, middle, stats_one, cols, kspec = made
-        q3, gate_up, q4, h_next, stats_two = call(
+            deps,
+        )(idx, *table, *([*h, chosen] if first else [h]), pad, hidden[layer], ahead_full, ahead_low, back_low)
+
+    def ahead_ff(layer, table, middle, cols, deps=()):
+        last = layer == LAYERS - 1
+        return call(
             functools.partial(fwd_ff_kernel, last),
             [
                 shaped(BF16, BLOCKS, 192, span),
@@ -895,28 +930,78 @@
             table_specs + [WHOLE] * 2,
             [WHOLE] * 5,
             15,
-        )(idx, *weights_ff[layer], middle, cols)
-        saved.append((h, q1, proj, conv, gated, q2, middle, stats_one, cols, kspec, q3, gate_up, q4, stats_two))
-        h = h_next
-
-    def collect(parts, dtype):
-        return call(
-            place_parts_kernel,
-            shaped(dtype, BLOCK_W, BLOCKS * span),
-            [],
-            [SCALARS] + [WHOLE] * BLOCKS,
-            WHOLE,
-            2,
-        )(idx, *exchange([parts[k] for k in range(BLOCKS)]))
-
-    mixed_out = collect(h, BF16)
+            deps,
+        )(idx, *table, middle, cols)
+
+    saved = []
+    h, q1, proj, conv, gated, q2, middle, stats_one, cols, kspec = ahead_mix(0, mix_zero, tokens_here)
+    parts = token_parts(cotangent)
+    middle, ff_chips, mix_one, ff_one = settle(middle, ff_chips, mix_one, ff_one)
+    ff_zero = (ff[0], ff_chips, wide_shift(ff_chips, 1))
+    middle, ff_zero, mix_one, ff_one = settle(middle, ff_zero, mix_one, ff_one)
+    mix_chips = over_chips(mix_one)
+    ff_one = others_at_once(ff_one, me)
+    q3, gate_up, q4, h_next, stats_two = ahead_ff(0, ff_zero, middle, cols)
+    saved.append((h, q1, proj, conv, gated, q2, middle, stats_one, cols, kspec, q3, gate_up, q4, stats_two))
+    h, mix_chips, ff_one = settle(h_next, mix_chips, ff_one)
+    mix_one = (mix[1], mix_chips, wide_shift(mix_chips, 1))
+    h, mix_one, ff_one, parts = settle(h, mix_one, ff_one, parts)
+    ff_chips = over_chips(ff_one)
+    near, far = narrow_shift(parts[1], 1), narrow_shift(parts[3], 3)
+    q1, proj, conv, gated, q2, middle, stats_one, cols, kspec = ahead_mix(1, mix_one, h)
+    middle, ff_chips, near, far = settle(middle, ff_chips, near, far)
+    ff_one = (ff[1], ff_chips, wide_shift(ff_chips, 1))
+    middle, ff_one, across = settle(middle, ff_one, parts[2])
+    across = narrow_shift(across, 2)
+    cotangent_here = [parts[0], near, across, far]
+    q3, gate_up, q4, h_last, stats_two = ahead_ff(1, ff_one, middle, cols)
+    saved.append((h, q1, proj, conv, gated, q2, middle, stats_one, cols, kspec, q3, gate_up, q4, stats_two))
+    weights_mix, weights_ff = (mix_zero, mix_one), (ff_zero, ff_one)
+
+    sizes = [weight.shape[2] // 128 for weight in factors]
+
+    def finish(layer, group, earlier):
+        shapes = [(LAYERS, size, 128) for size in sizes] + [(LAYERS, BLOCK_W, 128)]
+        specs = [pl.BlockSpec((None, *shape[1:]), lambda _: (layer, 0, 0)) for shape in shapes]
+        if layer:
+            rest = [(208, 256)]
+        else:
+            rest = [(LAYERS, BLOCK_W)] * 3 + [(LAYERS, 3, 384), (LAYERS, BLOCK_W), (1, BLOCK_W)]
+            rest += [(LAYERS, 5, 128), (LAYERS, 128), (LAYERS, 128, 128)]
+        specs += [pl.BlockSpec(shape, lambda _, n=len(shape): (0,) * n) for shape in rest]
+        inputs = [SCALARS] + [ANY] * (2 + len(earlier))
+        if earlier:
+            inputs[-1] = pl.BlockSpec(earlier[-1].shape, lambda _: (0, 0))
+        return pl.pallas_call(
+            functools.partial(finish_kernel, layer),
+            grid=(1,),
+            out_shape=[shaped(F32, *shape) for shape in shapes + rest],
+            in_specs=inputs,
+            out_specs=specs,
+            scratch_shapes=[
+                pltpu.VMEM((FF_ROWS, 384), BF16),
+                pltpu.VMEM((384, 384), BF16),
+                pltpu.VMEM((IN_GRAD_ROWS, 384), BF16),
+                pltpu.VMEM((2, 768, 128), F32),
+                pltpu.SemaphoreType.DMA((24,)),
+            ],
+            input_output_aliases={3 + at: at for at in range(9)} if earlier else {},
+            compiler_params=pltpu.CompilerParams(vmem_limit_bytes=56 << 20),
+            cost_estimate=pl.CostEstimate(flops=4 * 10**9, bytes_accessed=1 << 20, transcendentals=0),
+        )(idx, *group, *earlier)
+
+    def collect(table, dtype):
+        return call(place_parts_kernel, shaped(dtype, BLOCK_W, BLOCKS * span), [], [WHOLE], WHOLE, 2)(table)
+
+    def to_blocks(table):
+        return lax.all_to_all(table, "narrow", split_axis=0, concat_axis=0, tiled=True)
 
     def back_ff(layer, g_top, deps):
         last = layer == LAYERS - 1
         h, q1, proj, conv, gated, q2, middle, stats_one, cols, kspec, q3, gate_up, q4, stats_two = saved[layer]
         return call(
             functools.partial(bwd_ff_kernel, last),
-            [shaped(F32, D, span), shaped(BF16, 2, 4, BLOCKS, FF_ROWS // 8, 384), shaped(F32, BLOCKS, 16, BLOCK_W)],
+            [shaped(F32, D, span), *[shaped(BF16, 4, BLOCKS, FF_ROWS // 8, 384)] * 2, shaped(F32, BLOCKS, 16, BLOCK_W)],
             [
                 ff_scratch,
                 pltpu.VMEM((BLOCKS, FF_ROWS, 384), BF16),
@@ -928,7 +1013,7 @@
                 sent,
             ],
             table_specs + [WHOLE] * (BLOCKS if last else 1) + [WHOLE] * 6,
-            [WHOLE, ANY, WHOLE],
+            [WHOLE, ANY, ANY, WHOLE],
             27,
             deps,
         )(idx, *weights_ff[layer], *(g_top if last else [g_top]), q4, gate_up, q3, middle, stats_two, cols)
@@ -936,8 +1021,8 @@
     def back_conv(layer, g_mid, small_ff, deps):
         h, q1, proj, conv, gated, q2, middle, stats_one, cols, kspec, q3, gate_up, q4, stats_two = saved[layer]
         return call(
-            functools.partial(bwd_conv_kernel, seqs),
-            [shaped(BF16, BLOCKS, 384, span), shaped(BF16, 2, 4, BLOCKS, 48, 384)],
+            functools.partial(bwd_conv_kernel, seqs, penalty),
+            [shaped(BF16, BLOCKS, 384, span), *[shaped(BF16, 4, BLOCKS, 48, 384)] * 2],
             [
                 mix_scratch,
                 pltpu.VMEM((BLOCKS, 384, 384), BF16),
@@ -946,8 +1031,8 @@
                 pltpu.VMEM((BLOCK_W, span), F32),
                 sent,
             ],
-            table_specs + [WHOLE] * 11,
-            [WHOLE, ANY],
+            table_specs + [WHOLE] * 15,
+            [WHOLE, ANY, ANY],
             23,
             deps,
         )(
@@ -964,6 +1049,10 @@
             ahead_low,
             back_low,
             small_ff,
+            hidden[layer],
+            filter_two[layer],
+            features,
+            back_full,
         )
 
     def back_in(layer, gv, g_mid, deps):
@@ -973,7 +1062,7 @@
             functools.partial(bwd_in_kernel, first),
             [
                 shaped(BF16, BLOCKS, BLOCK_W, span) if first else shaped(F32, D, span),
-                shaped(BF16, 2, 4, BLOCKS, IN_GRAD_ROWS // 8, 384),
+                *[shaped(BF16, 4, BLOCKS, IN_GRAD_ROWS // 8, 384)] * 2,
             ],
             [
                 mix_scratch,
@@ -985,89 +1074,78 @@
             ]
             + ([pltpu.VMEM((D, span), F32)] if first else []),
             table_specs + [WHOLE] * (7 if first else 6),
-            [WHOLE, ANY],
+            [WHOLE, ANY, ANY],
             12,
             deps,
         )(idx, *weights_mix[layer], gv, g_mid, q1, h, stats_one, cols, *([chosen] if first else []))
 
-    def spread(*tables):
-        chips = over_chips(join_rows(*tables))
+    def spread(piece):
+        chips = over_chips(piece)
         return chips, wide_shift(chips, 1)
 
-    g_mid, g_ff, small_ff = back_ff(1, cotangent_here, ())
-    ff_one = reduce_core(g_ff)
-    gv, g_conv = back_conv(1, g_mid, small_ff, ())
-    conv_one = reduce_core(g_conv)
-    g_top, g_in = back_in(1, gv, g_mid, (ff_one,))
-    ff_one = reduce_chips(ff_one)
-    in_one = reduce_core(g_in)
-
-    g_mid, g_ff, small_ff = back_ff(0, g_top, (conv_one,))
-    mix_one = join_rows(conv_one, in_one)
-    ff_zero = reduce_core(g_ff)
-    gv, g_conv = back_conv(0, g_mid, small_ff, (ff_one, mix_one))
-    mix_one = reduce_chips(mix_one)
-    ff_one = reduce_blocks(ff_one)
-    conv_zero = reduce_core(g_conv)
-    g_top, g_in = back_in(0, gv, g_mid, (ff_one, mix_one, ff_zero))
-    grad_tokens = collect(g_top, F32)
-    mix_one = reduce_blocks(mix_one)
-    ff_zero = reduce_blocks(reduce_chips(ff_zero))
-    mix_zero = reduce_blocks(reduce_chips(join_rows(conv_zero, reduce_core(g_in))))
-    groups = [spread(ff_zero, mix_zero), spread(ff_one, mix_one)]
-
-    filter_grads = []
-    for layer in range(LAYERS):
-        joined = call(
-            functools.partial(join_kernel, PIECE_ROWS["ff"]),
-            shaped(BF16, 384, 384),
-            [pltpu.SemaphoreType.DMA((8,))],
-            [SCALARS, ANY, ANY],
-            WHOLE,
-            2,
-        )(idx, *groups[layer])
-        g_kernel = jnp.dot(joined[192:384, 0:256].astype(F32), jnp.asarray(back), precision=HIGHEST)
-        kernel, pull = pulls[layer]
-        grads = pull(g_kernel + 4.0 * math.sqrt(all_tokens) * kernel)
-        shared = jnp.concatenate([grads[2], grads[0], grads[1][None], jnp.zeros((2, 128), F32)], axis=0)
-        shared = added([shared] + [narrow_shift(shared, k) for k in range(1, BLOCKS)])
-        filter_grads.append((shared[128:133], shared[133], shared[0:128], grads[3], grads[4]))
-
-    sizes = [weight.shape[2] // 128 for weight in factors]
-    flat = call(
-        finish_kernel,
-        [shaped(F32, LAYERS, size, 128) for size in sizes] + [shaped(F32, LAYERS, 32, 256)],
-        [
-            pltpu.VMEM((LAYERS, FF_ROWS, 384), BF16),
-            pltpu.VMEM((LAYERS, 384, 384), BF16),
-            pltpu.VMEM((LAYERS, IN_GRAD_ROWS, 384), BF16),
-            pltpu.VMEM((2, 768, 128), F32),
-            pltpu.SemaphoreType.DMA((24 * LAYERS,)),
-        ],
-        [SCALARS] + [ANY] * (2 * LAYERS),
-        [WHOLE] * 9,
-        8,
-    )(idx, *(part for group in groups for part in group))
+    def each_after(arrays, *deps):
+        return [after(x, *deps) for x in arrays]
+
+    h_last, cotangent_here = settle(h_last, cotangent_here)
+    mixed_parts = to_blocks(h_last)
+    g_mid, near, far, small_ff = back_ff(1, cotangent_here, ())
+    g_mid, near, far, mixed_parts = settle(g_mid, near, far, mixed_parts)
+    mixed_out = collect(mixed_parts, BF16)
+    ff_one = reduce_core(near, far)
+    gv, near, far = back_conv(1, g_mid, small_ff, (mixed_out,))
+    gv, near, far, ff_one = settle(gv, near, far, ff_one)
+    conv_one = reduce_core(near, far)
+    ff_parts = [ff_one[0], wide_shift(ff_one[1], 2), wide_shift(ff_one[2], 4)]
+    g_top, near, far = back_in(1, gv, g_mid, ())
+    g_top, near, far, conv_one, ff_parts, last = settle(g_top, near, far, conv_one, ff_parts, ff_one[3])
+    near, far = settle(near, reduce_core(near, far))
+    mix_parts, g_top = settle(join_rows(conv_one, far), g_top)
+    ff_parts = ff_parts + [wide_shift(last, 6)]
+    mix_parts = move_chips(mix_parts)
+    g_mid, near, far, small_ff = back_ff(0, g_top, ())
+    g_mid, near, far, mix_parts, ff_parts = settle(g_mid, near, far, mix_parts, ff_parts)
+    all_one, ff_zero = settle(join_rows(add_chips(ff_parts), add_chips(mix_parts)), reduce_core(near, far))
+    all_parts = blocks_at_once(all_one, me)
+    ff_parts = move_chips(ff_zero)
+    gv, near, far = back_conv(0, g_mid, small_ff, ff_zero)
+    gv, near, far, all_parts, ff_parts = settle(gv, near, far, all_parts, ff_parts)
+    one_chips = over_chips(added(all_parts))
+    ff_parts = blocks_at_once(add_chips(ff_parts), me)
+    conv_zero = reduce_core(near, far)
+    g_top, near, far = back_in(0, gv, g_mid, ())
+    g_top, near, far, one_chips, ff_parts, conv_zero = settle(g_top, near, far, one_chips, ff_parts, conv_zero)
+
+    token_grads = to_blocks(g_top)
+    in_zero = reduce_core(near, far)
+    one_group = (one_chips, wide_shift(one_chips, 1))
+    in_zero, one_group, ff_zero = settle(in_zero, one_group, added(ff_parts))
+    mix_parts = move_chips(join_rows(conv_zero, in_zero))
+    flat = finish(1, one_group, [])
+    flat, mix_parts = settle(flat, mix_parts)
+    zero_chips = over_chips(jnp.concatenate([ff_zero, reduce_blocks(add_chips(mix_parts))], axis=0))
+    zero_chips, token_grads = settle(zero_chips, token_grads)
+    zero_group = (zero_chips, wide_shift(zero_chips, 1))
+    grad_tokens = collect(token_grads, F32)
+    flat = finish(0, zero_group, flat)
     grads = [table.reshape(LAYERS, 1, table.shape[1] * 128) for table in flat[:8]]
-    small = flat[8][:, :, :BLOCK_W]
-    filt = [jnp.stack([filter_grads[layer][at] for layer in range(LAYERS)]) for at in range(5)]
+    three, g_gain_one, g_gain_two, g_skip, g_taps, g_decay, g_mask, g_one, g_bias, g_two = flat[8:]
     return (
         mixed_out,
         grad_tokens,
-        small[0, 17],
-        small[:, 16],
+        g_mask[0],
+        g_gain_one,
         grads[0],
         grads[1],
-        jnp.concatenate([small[:, 3:6], small[:, 6:9]], axis=2)[:, :, None],
-        small[:, 2],
-        filt[4],
-        filt[0],
-        filt[1],
-        filt[2],
-        filt[3],
+        g_taps[:, :, None],
+        g_skip,
+        g_decay,
+        g_one,
+        g_bias,
+        g_two,
+        three,
         grads[2],
         grads[3],
-        small[:, 1],
+        g_gain_two,
         grads[4],
         grads[5],
         grads[6],

time: 578 us -> 445 us (0.77)
  waiting for transfers between devices: 138 us -> 65.7 us
  starting transfers between devices: 121 us -> 94.7 us
  local copies, waits for them, and re-layouts: 46.9 us -> 26 us
  matrix products: 14.4 us -> 2.79 us
  Pallas kernels: 222 us -> 228 us
    ppermute x42 -> x15, starting transfers between devices: 82.1 us -> 26.4 us  [narrow_shift(): lax.ppermute(x, 'narrow', [(i, (i + by) % narrow) for i in range(narrow)])]
    ppermute x42 -> x15, waiting for transfers between devices: 80.4 us -> 31.9 us  [narrow_shift(): lax.ppermute(x, 'narrow', [(i, (i + by) % narrow) for i in range(narrow)])]
    all_to_all x0 -> x6, starting transfers between devices: none -> 31.1 us  [the longest x2 13.5 us: others_at_once(): lax.all_to_all(jnp.stack([piece] * BLOCKS), 'narrow', split_axis=0, conca...]
    ppermute x42, waiting for transfers between devices: 57.1 us -> 32.1 us  [wide_shift(): lax.ppermute(x, 'wide', [(i, i ^ mask) for i in range(lax.axis_size('wide...]
    squeeze x18 -> x4, local copies, waits for them, and re-layouts: 20.1 us -> 2.28 us  [the longest x2 0.9 us: blocks_at_once(): return [moved[b] for b in range(BLOCKS)]]
    dot_general x18 -> x4, matrix products: 14.4 us -> 2.79 us  [the longest x2 1.41 us: filter_hidden(): two = jnp.dot(hidden_one, weight_two, precision=HIGHEST)]
    pallas_call x0 -> x2, Pallas kernels: none -> 9.49 us  [finish(): pl.pallas_call(functools.partial(finish_kernel, layer), grid=(1,), out_sh...]
    pallas_call x17 -> x14, Pallas kernels: 222 us -> 219 us  [call(): return lambda *arrays: made(*arrays, *deps)]
  transfers between devices with their start and end apart: 84 -> 63, of which waited for: 33 -> 16; matrix products, arithmetic and copies ran while one was open for 10% -> 6% of each run, Pallas kernels for 32% -> 50%
where the time goes in v2:
time: 445 us; the launch traced here: 439 us
  Pallas kernels  228 us (51%)
  starting transfers between devices  94.7 us (21%)
  waiting for transfers between devices  65.7 us (15%)
  local copies, waits for them, and re-layouts  26 us (6%)
  other arithmetic  19.7 us (4%)
    pallas_call x14, Pallas kernels, call(): return lambda *arrays: made(*arrays, *deps)  219 us
    ppermute x42, starting transfers between devices, wide_shift(): lax.ppermute(x, 'wide', [(i, i ^ mask) for i in range(lax.axis_size('wide...  37.3 us
    ppermute x42, waiting for transfers between devices, wide_shift(): lax.ppermute(x, 'wide', [(i, i ^ mask) for i in range(lax.axis_size('wide...  32.1 us
    ppermute x15, waiting for transfers between devices, narrow_shift(): lax.ppermute(x, 'narrow', [(i, (i + by) % narrow) for i in range(narrow)])  31.9 us
    ppermute x15, starting transfers between devices, narrow_shift(): lax.ppermute(x, 'narrow', [(i, (i + by) % narrow) for i in range(narrow)])  26.4 us
    unnamed x113, local copies, waits for them, and re-layouts  15.7 us
    all_to_all x2, starting transfers between devices, others_at_once(): lax.all_to_all(jnp.stack([piece] * BLOCKS), 'narrow', split_axis=0, conca...  13.5 us
    pallas_call x2, Pallas kernels, finish(): pl.pallas_call(functools.partial(finish_kernel, layer), grid=(1,), out_sh...  9.49 us
  transfers between devices with their start and end apart: 63, of which 16 were waited for; matrix products, arithmetic and copies ran while one was open for 6% of the time, Pallas kernels for 50%

profile of v2, /device:TPU:0, one launch (start us, length us, event | category | flops | bytes accessed | tf_op | source)
XLA Modules:
  0.0 438.8 jit_solution(11433236188091604109)
XLA Ops:
  27.7 4.0 collective-permute-start.7
  38.3 6.5 %collective-permute-done.8 = bf16[176,384]{1,0:T(8,128)(2,1)S(1)} collective-permute-done((bf16[176,384]{1,0:T(8,128)(2,1)}, bf16[176,384]{1,0:T(8,128)(2,1)S(1)}, u32[]{:S(2)}, u32[]{:S(2)}) %collective-permute-start.8) | collective-permute-done | bytes 135200 | tf_op jit(solution)/shard_map/ppermute | solution.py:706
  48.7 11.3 %collective-permute-done.10.refs_6_ = bf16[192,768]{1,0:T(8,128)(2,1)} collective-permute-done((bf16[192,768]{1,0:T(8,128)(2,1)}, bf16[192,768]{1,0:T(8,128)(2,1)}, u32[]{:S(2)}, u32[]{:S(2)}) %collective-permute-start.10) | collective-permute-done | bytes 294944 | tf_op jit(solution)/shard_map/ppermute | solution.py:706
  69.0 8.4 %all-to-all-start = ((bf16[4,128,384]{2,1,0:T(8,128)(2,1)}), bf16[4,128,384]{2,1,0:T(8,128)(2,1)S(1)}, u32[]{:S(2)}, u32[]{:S(2)}) async-start(bf16[4,128,384]{2,1,0:T(8,128)(2,1)} %stack.241), calls=%async_computation | async-start | bytes 786432 | tf_op jit(solution)/shard_map/all_to_all | solution.py:730
  78.6 18.7 %shard_map.412 = (f32[768,768]{1,0:T(8,128)}, bf16[4,384,768]{2,1,0:T(8,128)(2,1)}, bf16[4,384,768]{2,1,0:T(8,128)(2,1)}, bf16[768,768]{1,0:T(8,128)(2,1)}, bf16...) custom-call(s32[2]{0:T(128)} %pad_add_fusion.refs_0_.idx, ...), custom_call_target="tpu_custom_call" | custom-call | flops 17999998976 | bytes 1048576 | tf_op jit(solution)/shard_map/pallas_call | solution.py:691
  108.5 5.1 %all-to-all-start.1 = ((bf16[4,176,384]{2,1,0:T(8,128)(2,1)}), bf16[4,176,384]{2,1,0:T(8,128)(2,1)S(1)}, u32[]{:S(2)}, u32[]{:S(2)}) async-start(bf16[4,176,384]{2,1,0:T(8,128)(2,1)} %stack.248), calls=%async_computation.1 | async-start | bytes 1081344 | tf_op jit(solution)/shard_map/all_to_all | solution.py:730
  113.6 15.0 %shard_map.413 = (bf16[4,192,768]{2,1,0:T(8,128)(2,1)}, bf16[4,1536,768]{2,1,0:T(8,128)(2,1)}, bf16[4,192,768]{2,1,0:T(8,128)(2,1)}, f32[768,768]{1,0:T(8,128)}, f32[8,768]{1,0:T(8,128)}) custom-call(s32[2]{0:T(128)} %pad_add_fusion.refs_0_.idx, bf16[1408,384]{1,0:T(8,128)(2,1)} %get-tuple-element.278.refs_1_, bf16[4,3,176,384]{3,2,1,0:T(8,128)(2,1)} %copy-done.3, ...), custom_call_target="tpu_custom_call" | custom-call | flops 15000000512 | bytes 1048576 | tf_op jit(solution)/shard_map/pallas_call | solution.py:691
  141.1 17.2 %shard_map.414 = (bf16[4,384,768]{2,1,0:T(8,128)(2,1)}, bf16[4,384,768]{2,1,0:T(8,128)(2,1)}, bf16[768,768]{1,0:T(8,128)(2,1)}, bf16[768,768]{1,0:T(8,128)(2,1)}...) custom-call(s32[2]{0:T(128)} %pad_add_fusion.refs_0_.idx, ...), custom_call_target="tpu_custom_call" | custom-call | flops 17999998976 | bytes 1048576 | tf_op jit(solution)/shard_map/pallas_call | solution.py:691
  163.3 15.5 %shard_map.415 = (bf16[4,192,768]{2,1,0:T(8,128)(2,1)}, bf16[4,1536,768]{2,1,0:T(8,128)(2,1)}, bf16[4,192,768]{2,1,0:T(8,128)(2,1)}, bf16[4,192,768]{2,1,0:T(8,128)(2,1)}, f32[8,768]{1,0:T(8,128)}) custom-call(s32[2]{0:T(128)} %pad_add_fusion.refs_0_.idx, bf16[1408,384]{1,0:T(8,128)(2,1)} %get-tuple-element.302.refs_1_, bf16[4,3,176,384]{3,2,1,0:T(8,128)(2,1)} %copy-done.4, ...), custom_call_target="tpu_custom_call" | custom-call | flops 15000000512 | bytes 1048576 | tf_op jit(solution)/shard_map/pallas_call | solution.py:691
  183.1 27.3 %shard_map.416 = (f32[768,768]{1,0:T(8,128)}, bf16[4,4,176,384]{3,2,1,0:T(8,128)(2,1)}, bf16[4,4,176,384]{3,2,1,0:T(8,128)(2,1)}, f32[4,16,192]{2,1,0:T(8,128)}) custom-call(s32[2]{0:T(128)} %pad_add_fusion.refs_0_.idx, bf16[1408,384]{1,0:T(8,128)(2,1)} %get-tuple-element.302.refs_1_, bf16[4,3,176,384]{3,2,1,0:T(8,128)(2,1)} %copy-done.4, ...), custom_call_target="tpu_custom_call" | custom-call | flops 27000000512 | bytes 1048576 | tf_op jit(solution)/shard_map/pallas_call | solution.py:691
  215.5 28.8 %shard_map.418 = (bf16[4,384,768]{2,1,0:T(8,128)(2,1)}, bf16[4,4,48,384]{3,2,1,0:T(8,128)(2,1)}, bf16[4,4,48,384]{3,2,1,0:T(8,128)(2,1)}) custom-call(s32[2]{0:T(128)} %pad_add_fusion.refs_0_.idx, bf16[1024,384]{1,0:T(8,128)(2,1)} %get-tuple-element.290.refs_1_, bf16[4,3,128,384]{3,2,1,0:T(8,128)(2,1)} %copy-done.7, bf16[4,3,128,384]{3,2,1,0:T(8,128)(2,1)} %copy-done.45, ...), custom_call_target="tpu_custom_call" | custom-call | flops 23000000512 | bytes 1048576 | tf_op jit(solution)/shard_map/pallas_call | solution.py:691
  248.2 13.6 %shard_map.419 = (f32[768,768]{1,0:T(8,128)}, bf16[4,4,80,384]{3,2,1,0:T(8,128)(2,1)}, bf16[4,4,80,384]{3,2,1,0:T(8,128)(2,1)}) custom-call(s32[2]{0:T(128)} %pad_add_fusion.refs_0_.idx, bf16[1024,384]{1,0:T(8,128)(2,1)} %get-tuple-element.290.refs_1_, bf16[4,3,128,384]{3,2,1,0:T(8,128)(2,1)} %copy-done.7, bf16[4,3,128,384]{3,2,1,0:T(8,128)(2,1)} %copy-done.45, ...), custom_call_target="tpu_custom_call" | custom-call | flops 12000000000 | bytes 1048576 | tf_op jit(solution)/shard_map/pallas_call | solution.py:691
  269.0 27.6 %shard_map.420 = (f32[768,768]{1,0:T(8,128)}, bf16[4,4,176,384]{3,2,1,0:T(8,128)(2,1)}, bf16[4,4,176,384]{3,2,1,0:T(8,128)(2,1)}, f32[4,16,192]{2,1,0:T(8,128)}) custom-call(s32[2]{0:T(128)} %pad_add_fusion.refs_0_.idx, bf16[1408,384]{1,0:T(8,128)(2,1)} %get-tuple-element.278.refs_1_, bf16[4,3,176,384]{3,2,1,0:T(8,128)(2,1)} %copy-done.3, ...), custom_call_target="tpu_custom_call" | custom-call | flops 27000000512 | bytes 1048576 | tf_op jit(solution)/shard_map/pallas_call | solution.py:691
  312.5 28.7 %shard_map.421 = (bf16[4,384,768]{2,1,0:T(8,128)(2,1)}, bf16[4,4,48,384]{3,2,1,0:T(8,128)(2,1)}, bf16[4,4,48,384]{3,2,1,0:T(8,128)(2,1)}) custom-call(s32[2]{0:T(128)} %pad_add_fusion.refs_0_.idx, bf16[1024,384]{1,0:T(8,128)(2,1)} %get-tuple-element.262.refs_1_, bf16[4,3,128,384]{3,2,1,0:T(8,128)(2,1)} %copy-done.6, ...), custom_call_target="tpu_custom_call" | custom-call | flops 23000000512 | bytes 1048576 | tf_op jit(solution)/shard_map/pallas_call | solution.py:691
  347.6 5.2 %all-to-all-start.4 = ((bf16[4,176,384]{2,1,0:T(8,128)(2,1)}), bf16[4,176,384]{2,1,0:T(8,128)(2,1)S(1)}, u32[]{:S(2)}, u32[]{:S(2)}) async-start(bf16[4,176,384]{2,1,0:T(8,128)(2,1)} %pad_maximum_fusion.9), calls=%async_computation.4 | async-start | bytes 1081344 | tf_op jit(solution)/shard_map/all_to_all | solution.py:762
  352.8 13.9 %shard_map.422 = (bf16[4,192,768]{2,1,0:T(8,128)(2,1)}, bf16[4,4,80,384]{3,2,1,0:T(8,128)(2,1)}, bf16[4,4,80,384]{3,2,1,0:T(8,128)(2,1)}) custom-call(s32[2]{0:T(128)} %pad_add_fusion.refs_0_.idx, bf16[1024,384]{1,0:T(8,128)(2,1)} %get-tuple-element.262.refs_1_, bf16[4,3,128,384]{3,2,1,0:T(8,128)(2,1)} %copy-done.6, ...), custom_call_target="tpu_custom_call" | custom-call | flops 12000000000 | bytes 1048576 | tf_op jit(solution)/shard_map/pallas_call | solution.py:691
  371.1 5.1 %all-to-all-start.5 = ((bf16[4,192,768]{2,1,0:T(8,128)(2,1)}), bf16[4,192,768]{2,1,0:T(8,128)(2,1)S(1)}, u32[]{:S(2)}, u32[]{:S(2)}) async-start(bf16[4,192,768]{2,1,0:T(8,128)(2,1)} %get-tuple-element.453), calls=%async_computation.5 | async-start | bytes 2359296 | tf_op jit(solution)/shard_map/all_to_all | solution.py:997
  382.1 4.6 %shard_map.423 = (f32[2,576,128]{2,1,0:T(8,128)}, f32[2,1152,128]{2,1,0:T(8,128)}, f32[2,288,128]{2,1,0:T(8,128)}, f32[2,288,128]{2,1,0:T(8,128)}, f32[2,288,128...) custom-call(s32[2]{0:T(128)} %pad_add_fusion.refs_0_.idx, ...), custom_call_target="tpu_custom_call" | custom-call | flops 4000000000 | bytes 1048576 | tf_op jit(solution)/shard_map/pallas_call | solution.py:975
  386.7 4.5 %collective-permute-done.49 = bf16[4,128,384]{2,1,0:T(8,128)(2,1)S(1)} collective-permute-done((bf16[4,128,384]{2,1,0:T(8,128)(2,1)S(1)}, bf16[4,128,384]{2,1,0:T(8,128)(2,1)S(1)}, u32[]{:S(2)}, u32[]{:S(2)}) %collective-permute-start.49) | collective-permute-done | bytes 393248 | tf_op jit(solution)/shard_map/ppermute | solution.py:701
  391.3 7.2 %collective-permute-done.48 = bf16[4,128,384]{2,1,0:T(8,128)(2,1)S(1)} collective-permute-done((bf16[4,128,384]{2,1,0:T(8,128)(2,1)S(1)}, bf16[4,128,384]{2,1,0:T(8,128)(2,1)S(1)}, u32[]{:S(2)}, u32[]{:S(2)}) %collective-permute-start.48) | collective-permute-done | bytes 393248 | tf_op jit(solution)/shard_map/ppermute | solution.py:701
  406.9 6.5 %collective-permute-done.51 = bf16[128,384]{1,0:T(8,128)(2,1)S(1)} collective-permute-done((bf16[128,384]{1,0:T(8,128)(2,1)S(1)}, bf16[128,384]{1,0:T(8,128)(2,1)S(1)}, u32[]{:S(2)}, u32[]{:S(2)}) %collective-permute-start.51) | collective-permute-done | bytes 98336 | tf_op jit(solution)/shard_map/ppermute | solution.py:706
  417.0 5.1 %collective-permute-done.53 = bf16[304,384]{1,0:T(8,128)(2,1)S(1)} collective-permute-done((bf16[304,384]{1,0:T(8,128)(2,1)S(1)}, bf16[304,384]{1,0:T(8,128)(2,1)S(1)}, u32[]{:S(2)}, u32[]{:S(2)}) %collective-permute-start.53) | collective-permute-done | bytes 233504 | tf_op jit(solution)/shard_map/ppermute | solution.py:701
  422.2 3.9 collective-permute-done.54
  431.1 4.9 %shard_map.425 = (f32[2,576,128]{2,1,0:T(8,128)}, f32[2,1152,128]{2,1,0:T(8,128)}, f32[2,288,128]{2,1,0:T(8,128)}, f32[2,288,128]{2,1,0:T(8,128)}, f32[2,288,128...) custom-call(s32[2]{0:T(128)} %pad_add_fusion.refs_0_.idx, ...), custom_call_target="tpu_custom_call", output_to_operand_aliasing={{0}: (3, {}), {1}: (4, {}), {2}: (5, {}), {3}: (6, {}), {4}... | custom-call | flops 4000000000 | bytes 1048576 | tf_op jit(solution)/shard_map/pallas_call | solution.py:975
  (299 shorter events, 148.3 us)
Async XLA Ops:
  64.7 32.6 %collective-permute-start.13 = (bf16[3,176,384]{2,1,0:T(8,128)(2,1)S(1)}, bf16[3,176,384]{2,1,0:T(8,128)(2,1)S(1)}, u32[]{:S(2)}, u32[]{:S(2)}) collective-permute-start(bf16[3,176,384]{2,1,0:T(8,128)(2,1)S(1)} %pad_maximum_fusion.12), channel_id=1, source_target_pairs={{0,8},{4,12},{8,0},{12,4},{16,24},{20,28},{24,16},{28,20},{1,9},{5... | collective-permute-start | bytes 1216520 | tf_op jit(solution)/shard_map/ppermute | solution.py:701
  66.2 31.1 %collective-permute-start.14 = (bf16[3,176,384]{2,1,0:T(8,128)(2,1)S(1)}, bf16[3,176,384]{2,1,0:T(8,128)(2,1)S(1)}, u32[]{:S(2)}, u32[]{:S(2)}) collective-permute-start(bf16[3,176,384]{2,1,0:T(8,128)(2,1)S(1)} %pad_maximum_fusion.12), channel_id=1, source_target_pairs={{0,16},{4,20},{8,24},{12,28},{16,0},{20,4},{24,8},{28,12},{1,17},{... | collective-permute-start | bytes 1216520 | tf_op jit(solution)/shard_map/ppermute | solution.py:701
  67.7 29.6 %collective-permute-start.15 = (bf16[3,176,384]{2,1,0:T(8,128)(2,1)S(1)}, bf16[3,176,384]{2,1,0:T(8,128)(2,1)}, u32[]{:S(2)}, u32[]{:S(2)}) collective-permute-start(bf16[3,176,384]{2,1,0:T(8,128)(2,1)S(1)} %pad_maximum_fusion.12), channel_id=1, source_target_pairs={{0,24},{4,28},{8,16},{12,20},{16,8},{20,12},{24,0},{28,4},{1,25},{... | collective-permute-start | bytes 1216520 | tf_op jit(solution)/shard_map/ppermute | solution.py:701
  69.0 30.5 %all-to-all-start = ((bf16[4,128,384]{2,1,0:T(8,128)(2,1)}), bf16[4,128,384]{2,1,0:T(8,128)(2,1)S(1)}, u32[]{:S(2)}, u32[]{:S(2)}) async-start(bf16[4,128,384]{2,1,0:T(8,128)(2,1)} %stack.241), calls=%async_computation | async-start | bytes 786432 | tf_op jit(solution)/shard_map/all_to_all | solution.py:730
  103.5 25.0 %collective-permute-start.17 = (bf16[3,128,384]{2,1,0:T(8,128)(2,1)S(1)}, bf16[3,128,384]{2,1,0:T(8,128)(2,1)S(1)}, u32[]{:S(2)}, u32[]{:S(2)}) collective-permute-start(bf16[3,128,384]{2,1,0:T(8,128)(2,1)S(1)} %pad_maximum_fusion.23), channel_id=1, source_target_pairs={{0,8},{4,12},{8,0},{12,4},{16,24},{20,28},{24,16},{28,20},{1,9},{5... | collective-permute-start | bytes 884744 | tf_op jit(solution)/shard_map/ppermute | solution.py:701
  105.0 23.6 %collective-permute-start.18 = (bf16[3,128,384]{2,1,0:T(8,128)(2,1)S(1)}, bf16[3,128,384]{2,1,0:T(8,128)(2,1)S(1)}, u32[]{:S(2)}, u32[]{:S(2)}) collective-permute-start(bf16[3,128,384]{2,1,0:T(8,128)(2,1)S(1)} %pad_maximum_fusion.23), channel_id=1, source_target_pairs={{0,16},{4,20},{8,24},{12,28},{16,0},{20,4},{24,8},{28,12},{1,17},{... | collective-permute-start | bytes 884744 | tf_op jit(solution)/shard_map/ppermute | solution.py:701
  133.6 24.7 %collective-permute-start.21 = (bf16[3,176,384]{2,1,0:T(8,128)(2,1)S(1)}, bf16[3,176,384]{2,1,0:T(8,128)(2,1)S(1)}, u32[]{:S(2)}, u32[]{:S(2)}) collective-permute-start(bf16[3,176,384]{2,1,0:T(8,128)(2,1)S(1)} %pad_maximum_fusion.13), channel_id=1, source_target_pairs={{0,8},{4,12},{8,0},{12,4},{16,24},{20,28},{24,16},{28,20},{1,9},{5... | collective-permute-start | bytes 1216520 | tf_op jit(solution)/shard_map/ppermute | solution.py:701
  134.5 23.8 %collective-permute-start.22 = (bf16[3,176,384]{2,1,0:T(8,128)(2,1)S(1)}, bf16[3,176,384]{2,1,0:T(8,128)(2,1)S(1)}, u32[]{:S(2)}, u32[]{:S(2)}) collective-permute-start(bf16[3,176,384]{2,1,0:T(8,128)(2,1)S(1)} %pad_maximum_fusion.13), channel_id=1, source_target_pairs={{0,16},{4,20},{8,24},{12,28},{16,0},{20,4},{24,8},{28,12},{1,17},{... | collective-permute-start | bytes 1216520 | tf_op jit(solution)/shard_map/ppermute | solution.py:701
  136.0 22.3 %collective-permute-start.23 = (bf16[3,176,384]{2,1,0:T(8,128)(2,1)S(1)}, bf16[3,176,384]{2,1,0:T(8,128)(2,1)S(1)}, u32[]{:S(2)}, u32[]{:S(2)}) collective-permute-start(bf16[3,176,384]{2,1,0:T(8,128)(2,1)S(1)} %pad_maximum_fusion.13), channel_id=1, source_target_pairs={{0,24},{4,28},{8,16},{12,20},{16,8},{20,12},{24,0},{28,4},{1,25},{... | collective-permute-start | bytes 1216520 | tf_op jit(solution)/shard_map/ppermute | solution.py:701
  179.5 32.6 %all-to-all-start.2 = ((bf16[4,192,768]{2,1,0:T(8,128)(2,1)}), bf16[4,192,768]{2,1,0:T(8,128)(2,1)S(1)}, u32[]{:S(2)}, u32[]{:S(2)}) async-start(bf16[4,192,768]{2,1,0:T(8,128)(2,1)} %get-tuple-element.323), calls=%async_computation.2 | async-start | bytes 2359296 | tf_op jit(solution)/shard_map/all_to_all | solution.py:997
  212.2 32.2 %collective-permute-start.28 = (bf16[4,4,176,384]{3,2,1,0:T(8,128)(2,1)}, bf16[4,4,176,384]{3,2,1,0:T(8,128)(2,1)S(1)}, u32[]{:S(2)}, u32[]{:S(2)}) collective-permute-start(bf16[4,4,176,384]{3,2,1,0:T(8,128)(2,1)} %get-tuple-element.336), channel_id=1, source_target_pairs={{0,4},{4,0},{8,12},{12,8},{16,20},{20,16},{24,28},{28,24},{1,5},{5... | collective-permute-start | bytes 6488072 | tf_op jit(solution)/shard_map/ppermute | solution.py:701
  262.2 34.4 %collective-permute-start.36 = (bf16[4,176,384]{2,1,0:T(8,128)(2,1)S(1)}, bf16[4,176,384]{2,1,0:T(8,128)(2,1)S(1)}, u32[]{:S(2)}, u32[]{:S(2)}) collective-permute-start(bf16[4,176,384]{2,1,0:T(8,128)(2,1)S(1)} %get-tuple-element.375), channel_id=1, source_target_pairs={{0,24},{4,28},{8,16},{12,20},{16,8},{20,12},{24,0},{28,4},{1,25},{... | collective-permute-start | bytes 1622024 | tf_op jit(solution)/shard_map/ppermute | solution.py:701
  265.4 31.2 %collective-permute-start.33 = (bf16[4,128,384]{2,1,0:T(8,128)(2,1)S(1)}, bf16[4,128,384]{2,1,0:T(8,128)(2,1)S(1)}, u32[]{:S(2)}, u32[]{:S(2)}) collective-permute-start(bf16[4,128,384]{2,1,0:T(8,128)(2,1)S(1)} %pad_maximum_fusion.15), channel_id=1, source_target_pairs={{0,8},{4,12},{8,0},{12,4},{16,24},{20,28},{24,16},{28,20},{1,9},{5... | collective-permute-start | bytes 1179656 | tf_op jit(solution)/shard_map/ppermute | solution.py:701
  266.6 30.1 %collective-permute-start.34 = (bf16[4,128,384]{2,1,0:T(8,128)(2,1)S(1)}, bf16[4,128,384]{2,1,0:T(8,128)(2,1)S(1)}, u32[]{:S(2)}, u32[]{:S(2)}) collective-permute-start(bf16[4,128,384]{2,1,0:T(8,128)(2,1)S(1)} %pad_maximum_fusion.16), channel_id=1, source_target_pairs={{0,16},{4,20},{8,24},{12,28},{16,0},{20,4},{24,8},{28,12},{1,17},{... | collective-permute-start | bytes 1179656 | tf_op jit(solution)/shard_map/ppermute | solution.py:701
  267.1 29.6 %collective-permute-start.35 = (bf16[4,128,384]{2,1,0:T(8,128)(2,1)S(1)}, bf16[4,128,384]{2,1,0:T(8,128)(2,1)S(1)}, u32[]{:S(2)}, u32[]{:S(2)}) collective-permute-start(bf16[4,128,384]{2,1,0:T(8,128)(2,1)S(1)} %pad_maximum_fusion.17), channel_id=1, source_target_pairs={{0,24},{4,28},{8,16},{12,20},{16,8},{20,12},{24,0},{28,4},{1,25},{... | collective-permute-start | bytes 1179656 | tf_op jit(solution)/shard_map/ppermute | solution.py:701
  305.2 36.0 %all-to-all-start.3 = ((bf16[4,304,384]{2,1,0:T(8,128)(2,1)}), bf16[4,304,384]{2,1,0:T(8,128)(2,1)S(1)}, u32[]{:S(2)}, u32[]{:S(2)}) async-start(bf16[4,304,384]{2,1,0:T(8,128)(2,1)} %pad_maximum_fusion.5), calls=%async_computation.3 | async-start | bytes 1867776 | tf_op jit(solution)/shard_map/all_to_all | solution.py:762
  309.0 32.4 %collective-permute-start.38 = (bf16[4,176,384]{2,1,0:T(8,128)(2,1)}, bf16[4,176,384]{2,1,0:T(8,128)(2,1)S(1)}, u32[]{:S(2)}, u32[]{:S(2)}) collective-permute-start(bf16[4,176,384]{2,1,0:T(8,128)(2,1)} %get-tuple-element.394.refs_20_), channel_id=1, source_target_pairs={{0,8},{4,12},{8,0},{12,4},{16,24},{20,28},{24,16},{28,20},{1,9},{5... | collective-permute-start | bytes 1622024 | tf_op jit(solution)/shard_map/ppermute | solution.py:701
  310.2 31.2 %collective-permute-start.39 = (bf16[4,176,384]{2,1,0:T(8,128)(2,1)}, bf16[4,176,384]{2,1,0:T(8,128)(2,1)S(1)}, u32[]{:S(2)}, u32[]{:S(2)}) collective-permute-start(bf16[4,176,384]{2,1,0:T(8,128)(2,1)} %get-tuple-element.395.refs_21_), channel_id=1, source_target_pairs={{0,16},{4,20},{8,24},{12,28},{16,0},{20,4},{24,8},{28,12},{1,17},{... | collective-permute-start | bytes 1622024 | tf_op jit(solution)/shard_map/ppermute | solution.py:701
  310.7 30.8 %collective-permute-start.40 = (bf16[4,176,384]{2,1,0:T(8,128)(2,1)}, bf16[4,176,384]{2,1,0:T(8,128)(2,1)}, u32[]{:S(2)}, u32[]{:S(2)}) collective-permute-start(bf16[4,176,384]{2,1,0:T(8,128)(2,1)} %get-tuple-element.396.refs_22_), channel_id=1, source_target_pairs={{0,24},{4,28},{8,16},{12,20},{16,8},{20,12},{24,0},{28,4},{1,25},{... | collective-permute-start | bytes 1622024 | tf_op jit(solution)/shard_map/ppermute | solution.py:701
  341.5 25.1 %collective-permute-start.41 = (bf16[304,384]{1,0:T(8,128)(2,1)S(1)}, bf16[304,384]{1,0:T(8,128)(2,1)S(1)}, u32[]{:S(2)}, u32[]{:S(2)}) collective-permute-start(bf16[304,384]{1,0:T(8,128)(2,1)S(1)} %add_convert_fusion.16), channel_id=1, source_target_pairs={{0,8},{4,12},{8,0},{12,4},{16,24},{20,28},{24,16},{28,20},{1,9},{5... | collective-permute-start | bytes 700424 | tf_op jit(solution)/shard_map/ppermute | solution.py:701
  342.7 23.9 %collective-permute-start.42 = (bf16[304,384]{1,0:T(8,128)(2,1)S(1)}, bf16[304,384]{1,0:T(8,128)(2,1)}, u32[]{:S(2)}, u32[]{:S(2)}) collective-permute-start(bf16[304,384]{1,0:T(8,128)(2,1)S(1)} %add_convert_fusion.16), channel_id=1, source_target_pairs={{0,16},{4,20},{8,24},{12,28},{16,0},{20,4},{24,8},{28,12},{1,17},{... | collective-permute-start | bytes 700424 | tf_op jit(solution)/shard_map/ppermute | solution.py:701
  343.2 23.5 %collective-permute-start.43 = (bf16[304,384]{1,0:T(8,128)(2,1)S(1)}, bf16[304,384]{1,0:T(8,128)(2,1)}, u32[]{:S(2)}, u32[]{:S(2)}) collective-permute-start(bf16[304,384]{1,0:T(8,128)(2,1)S(1)} %add_convert_fusion.16), channel_id=1, source_target_pairs={{0,24},{4,28},{8,16},{12,20},{16,8},{20,12},{24,0},{28,4},{1,25},{... | collective-permute-start | bytes 700424 | tf_op jit(solution)/shard_map/ppermute | solution.py:701
  345.1 23.8 %collective-permute-start.44 = (bf16[4,4,48,384]{3,2,1,0:T(8,128)(2,1)}, bf16[4,4,48,384]{3,2,1,0:T(8,128)(2,1)S(1)}, u32[]{:S(2)}, u32[]{:S(2)}) collective-permute-start(bf16[4,4,48,384]{3,2,1,0:T(8,128)(2,1)} %get-tuple-element.420), channel_id=1, source_target_pairs={{0,4},{4,0},{8,12},{12,8},{16,20},{20,16},{24,28},{28,24},{1,5},{5... | collective-permute-start | bytes 1769480 | tf_op jit(solution)/shard_map/ppermute | solution.py:701
  371.1 55.2 %all-to-all-start.5 = ((bf16[4,192,768]{2,1,0:T(8,128)(2,1)}), bf16[4,192,768]{2,1,0:T(8,128)(2,1)S(1)}, u32[]{:S(2)}, u32[]{:S(2)}) async-start(bf16[4,192,768]{2,1,0:T(8,128)(2,1)} %get-tuple-element.453), calls=%async_computation.5 | async-start | bytes 2359296 | tf_op jit(solution)/shard_map/all_to_all | solution.py:997
  (92 other events, 782.7 us)

commit v3 on v2

--- a/solution.py
+++ b/solution.py
@@ -53,6 +53,11 @@
     return lax.broadcasted_iota(jnp.int32, shape, 1)
 
 
+def column(cols, rows, at, lanes=LENGTH):
+    one = jnp.broadcast_to(cols[rows, at : at + 1], (BLOCK_W, LENGTH))
+    return one if lanes == LENGTH else jnp.concatenate([one] * (lanes // LENGTH), axis=1)
+
+
 def later(v, lane):
     return jnp.where(lane == 0, 0.0, pltpu.roll(v, 1, 1))
 
@@ -83,38 +88,50 @@
     pad, hidden, ahead_full, ahead, back, *refs = refs
     if first:
         h_ref, *refs = refs
-    q1, proj, conv, gated, q2, middle, stats, cols, kspec, w, normed, xs, gs, sem = refs
-    fetch_table(idx, own, rel_a, rel_b, w, sem)
-    make_params(w, hidden, ahead_full, cols, kspec)
+    q1, proj, conv, gated, q2, middle, stats, cols, kspec, table, normed, xs, gs, sem = refs
+    at = distances(idx)
+    fetched = fetch_table(idx, own, rel_a, rel_b, table.buffer, sem)
+    w = table.buffer
     if first:
+        fetched()
+        make_params(w, at, hidden, ahead_full, cols, kspec)
         keep = chosen_ref[0:1, :]
         for k, part in enumerate(parts):
             rows = pl.ds(pl.multiple_of(block_of(idx, k) * BLOCK_W, BLOCK_W), BLOCK_W)
-            h_ref[rows, :] = part[...].astype(F32) * (1.0 - keep) + keep * cols[rows, MASK : MASK + 1]
+            h_ref.buffer[rows, :] = part[...].astype(F32) * (1.0 - keep) + keep * column(cols, rows, MASK, seqs * LENGTH)
+        h_ref.start()
+        h_ref = h_ref.buffer
     mean, inv = norm_rows([block(h_ref, b) for b in range(BLOCKS)])
+    if not first:
+        fetched()
+        make_params(w, at, hidden, ahead_full, cols, kspec)
+    table.start()
     stats[0:1, :] = mean
     stats[1:2, :] = inv
     for b in range(BLOCKS):
         rows = pl.ds(b * BLOCK_W, BLOCK_W)
-        normed[rows, :] = ((h_ref[rows, :] - mean) * inv * cols[rows, GAIN_ONE : GAIN_ONE + 1]).astype(BF16)
+        normed[rows, :] = ((h_ref[rows, :] - mean) * inv * column(cols, rows, GAIN_ONE, seqs * LENGTH)).astype(BF16)
     for b in range(BLOCKS):
-        inner = tn(w[b, IN_ONE : IN_ONE + 192, :], block(normed, b)).astype(BF16)
+        inner = tn(w[at[b], IN_ONE : IN_ONE + 192, :], block(normed, b)).astype(BF16)
         for c in range(BLOCKS):
-            q1[c, 96 * b : 96 * b + 96, :] = inner[96 * c : 96 * c + 96]
+            q1.buffer[c, 96 * b : 96 * b + 96, :] = inner[96 * c : 96 * c + 96]
+    q1.start()
     lane = lanes_of((BLOCK_W, LENGTH))
     row_lane = lanes_of((BLOCK_W, LENGTH))
     for c in range(BLOCKS):
         rows = pl.ds(c * BLOCK_W, BLOCK_W)
-        value = tn(w[c, IN_TWO : IN_TWO + 384, :], q1[c]) * pad[0:1, :]
-        proj[c] = value.astype(BF16)
+        value = tn(w[at[c], IN_TWO : IN_TWO + 384, :], q1.buffer[c]) * pad[0:1, :]
+        proj.buffer[c] = value.astype(BF16)
+        taps = [[column(cols, rows, tap + n) for n in range(3)] for tap in (TAP_X, TAP_G)]
+        skip = column(cols, rows, SKIP)
         for s in range(seqs):
             here = slice(s * LENGTH, (s + 1) * LENGTH)
-            for part, tap, out in ((0, TAP_X, xs), (192, TAP_G, gs)):
+            for part, tap, out in ((0, taps[0], xs), (192, taps[1], gs)):
                 v = value[part : part + 192, here]
                 out[:, here] = (
-                    cols[rows, tap : tap + 1] * later(v, lane)
-                    + cols[rows, tap + 1 : tap + 2] * v
-                    + cols[rows, tap + 2 : tap + 3] * earlier(v, lane)
+                    tap[0] * later(v, lane)
+                    + tap[1] * v
+                    + tap[2] * earlier(v, lane)
                 )
         signal = jnp.concatenate([xs[:, s * LENGTH : (s + 1) * LENGTH] for s in range(seqs)], axis=0)
         spec = nn(signal.astype(BF16), ahead[...])
@@ -132,16 +149,18 @@
         y = nn(jnp.concatenate(made, axis=0), back[...])
         for s in range(seqs):
             here = slice(s * LENGTH, (s + 1) * LENGTH)
-            value = y[s * 192 : s * 192 + 192] + cols[rows, SKIP : SKIP + 1] * xs[:, here]
-            conv[rows, here] = value.astype(BF16)
-            gated[rows, here] = (value * gs[:, here]).astype(BF16)
+            value = y[s * 192 : s * 192 + 192] + skip * xs[:, here]
+            conv.buffer[rows, here] = value.astype(BF16)
+            gated.buffer[rows, here] = (value * gs[:, here]).astype(BF16)
+    for part in (proj, conv, gated):
+        part.start()
     for b in range(BLOCKS):
-        inner = tn(w[b, OUT_ROWS : OUT_ROWS + 192, 0:192], block(gated, b)).astype(BF16)
+        inner = tn(w[at[b], OUT_ROWS : OUT_ROWS + 192, 0:192], block(gated.buffer, b)).astype(BF16)
         for c in range(BLOCKS):
             q2[c, 48 * b : 48 * b + 48, :] = inner[48 * c : 48 * c + 48]
     for c in range(BLOCKS):
         rows = pl.ds(c * BLOCK_W, BLOCK_W)
-        middle[rows, :] = h_ref[rows, :] + tn(w[c, OUT_ROWS : OUT_ROWS + 192, 192:384], q2[c])
+        middle[rows, :] = h_ref[rows, :] + tn(w[at[c], OUT_ROWS : OUT_ROWS + 192, 192:384], q2[c])
 
 
 def gelu_parts(v):
@@ -149,96 +168,123 @@
     return jnp.tanh(inner)
 
 
-def fwd_ff_kernel(last, idx, own, rel_a, rel_b, middle, cols, q3, gate_up, q4, h_next, stats, w, normed, act, sem):
-    fetch_table(idx, own, rel_a, rel_b, w, sem)
+def fwd_ff_kernel(last, idx, own, rel_a, rel_b, middle, cols, q3, gate_up, q4, h_next, stats, table, normed, act, sem):
+    at = distances(idx)
+    fetched = fetch_table(idx, own, rel_a, rel_b, table.buffer, sem)
+    w = table.buffer
     mean, inv = norm_rows([block(middle, b) for b in range(BLOCKS)])
     stats[0:1, :] = mean
     stats[1:2, :] = inv
     for b in range(BLOCKS):
         rows = pl.ds(b * BLOCK_W, BLOCK_W)
-        normed[rows, :] = ((middle[rows, :] - mean) * inv * cols[rows, GAIN_TWO : GAIN_TWO + 1]).astype(BF16)
+        normed[rows, :] = ((middle[rows, :] - mean) * inv * column(cols, rows, GAIN_TWO, middle.shape[1])).astype(BF16)
+    fetched()
+    table.start()
     for b in range(BLOCKS):
-        inner = tn(w[b, UP_ONE : UP_ONE + 192, 0:192], block(normed, b)).astype(BF16)
+        inner = tn(w[at[b], UP_ONE : UP_ONE + 192, 0:192], block(normed, b)).astype(BF16)
         for c in range(BLOCKS):
-            q3[c, 48 * b : 48 * b + 48, :] = inner[48 * c : 48 * c + 48]
+            q3.buffer[c, 48 * b : 48 * b + 48, :] = inner[48 * c : 48 * c + 48]
+    q3.start()
     for c in range(BLOCKS):
         for half in range(2):
             ups = []
             for piece in (half, half + 2):
-                ups.append(tn(w[c, UP_TWO + 192 * piece : UP_TWO + 192 * piece + 192, :], q3[c]))
+                ups.append(tn(w[at[c], UP_TWO + 192 * piece : UP_TWO + 192 * piece + 192, :], q3.buffer[c]))
             gate, up = ups
-            gate_up[c, 384 * half : 384 * half + 384, :] = gate.astype(BF16)
-            gate_up[c, 768 + 384 * half : 768 + 384 * half + 384, :] = up.astype(BF16)
+            gate_up.buffer[c, 384 * half : 384 * half + 384, :] = gate.astype(BF16)
+            gate_up.buffer[c, 768 + 384 * half : 768 + 384 * half + 384, :] = up.astype(BF16)
             act[384 * half : 384 * half + 384, :] = (
                 0.5 * gate * (1.0 + gelu_parts(gate)) * up
             ).astype(BF16)
+        gate_up.start(c)
         inner = (
-            tn(w[c, DOWN_ONE : DOWN_ONE + 384, 0:192], act[0:384, :])
-            + tn(w[c, DOWN_ONE : DOWN_ONE + 384, 192:384], act[384:768, :])
+            tn(w[at[c], DOWN_ONE : DOWN_ONE + 384, 0:192], act[0:384, :])
+            + tn(w[at[c], DOWN_ONE : DOWN_ONE + 384, 192:384], act[384:768, :])
         ).astype(BF16)
         for to in range(BLOCKS):
             q4[to, 48 * c : 48 * c + 48, :] = inner[48 * to : 48 * to + 48]
     for c in range(BLOCKS):
         rows = pl.ds(c * BLOCK_W, BLOCK_W)
-        value = middle[rows, :] + tn(w[c, UP_ONE : UP_ONE + 192, 192:384], q4[c])
+        value = middle[rows, :] + tn(w[at[c], UP_ONE : UP_ONE + 192, 192:384], q4[c])
         if last:
             h_next[c] = value.astype(BF16)
         else:
             h_next[rows, :] = value
 
 
-def bwd_ff_kernel(last, idx, own, rel_a, rel_b, *refs):
+def bwd_ff_kernel(last, idx, table, *refs):
     parts = refs[: BLOCKS if last else 1]
-    q4, gate_up, q3, middle, stats, cols, g_mid, g_near, g_far, small, w, g_w, g_low, gi4, gi3, g_gu, g_n, sem = refs[len(parts) :]
-    fetch_table(idx, own, rel_a, rel_b, w, sem)
+    q4, gate_up, q3, middle, stats, cols, g_mid, g_near, g_far, small, g_w, g_low, gi4, gi3, g_gu, g_n, sem = refs[len(parts) :]
+    at = distances(idx)
+    for part in parts:
+        part.start()
+    q4.start()
+    table.start((slice(None), slice(UP_ONE, UP_ONE + 192)))
+    gate_up.start(0)
+    table.start((slice(None), slice(DOWN_ONE, FF_USED)))
+    table.start((slice(None), slice(UP_TWO, DOWN_ONE)))
+    q3.start()
+    for b in range(1, BLOCKS):
+        gate_up.start(b)
+    for part in (middle, cols):
+        part.start()
+    w = table.buffer
     mean = stats[0:1, :]
     inv = stats[1:2, :]
     if last:
         for k, part in enumerate(parts):
-            g_low[pl.ds(pl.multiple_of(block_of(idx, k) * BLOCK_W, BLOCK_W), BLOCK_W), :] = part[...]
+            g_low[pl.ds(pl.multiple_of(block_of(idx, k) * BLOCK_W, BLOCK_W), BLOCK_W), :] = part.wait()[...]
         g_top = g_low
     else:
-        (g_top,) = parts
+        g_top = parts[0].wait()
         for c in range(BLOCKS):
             g_low[c * 192 : c * 192 + 192, :] = block(g_top, c).astype(BF16)
     for b in range(BLOCKS):
-        g_w[b, FF_USED:FF_ROWS, :] = jnp.zeros((FF_ROWS - FF_USED, 384), BF16)
+        g_w[at[b], FF_USED:FF_ROWS, :] = jnp.zeros((FF_ROWS - FF_USED, 384), BF16)
+    table.wait(0)
+    q4 = q4.wait()
     for c in range(BLOCKS):
         gt = block(g_low, c)
-        g_w[c, UP_ONE : UP_ONE + 192, 192:384] = nt(q4[c], gt).astype(BF16)
-        gq = nn(w[c, UP_ONE : UP_ONE + 192, 192:384], gt).astype(BF16)
+        g_w[at[c], UP_ONE : UP_ONE + 192, 192:384] = nt(q4[c], gt).astype(BF16)
+        gq = nn(w[at[c], UP_ONE : UP_ONE + 192, 192:384], gt).astype(BF16)
         for b in range(BLOCKS):
             gi4[b, 48 * c : 48 * c + 48, :] = gq[48 * b : 48 * b + 48]
     rate = math.sqrt(2.0 / math.pi)
+    table.wait(1)
     for b in range(BLOCKS):
+        gate_up.wait(b)
+        if b == 0:
+            table.wait()
+            q3.wait()
         for half in range(2):
             span = slice(192 * half, 192 * half + 192)
-            gate = gate_up[b, 384 * half : 384 * half + 384, :].astype(F32)
-            up = gate_up[b, 768 + 384 * half : 768 + 384 * half + 384, :].astype(F32)
-            ga = nn(w[b, DOWN_ONE : DOWN_ONE + 384, span], gi4[b])
+            gate = gate_up.buffer[b, 384 * half : 384 * half + 384, :].astype(F32)
+            up = gate_up.buffer[b, 768 + 384 * half : 768 + 384 * half + 384, :].astype(F32)
+            ga = nn(w[at[b], DOWN_ONE : DOWN_ONE + 384, span], gi4[b])
             square = gate * gate
             t = jnp.tanh(rate * gate * (1.0 + 0.044715 * square))
             rise = 0.5 * (1.0 + t)
             gelu = gate * rise
             slope = rise + 0.5 * gelu_slope(gate, square, t, rate)
             act = (gelu * up).astype(BF16)
-            g_w[b, DOWN_ONE : DOWN_ONE + 384, span] = nt(act, gi4[b]).astype(BF16)
+            g_w[at[b], DOWN_ONE : DOWN_ONE + 384, span] = nt(act, gi4[b]).astype(BF16)
             g_gu[384 * half : 384 * half + 384, :] = (ga * up * slope).astype(BF16)
             g_gu[768 + 384 * half : 768 + 384 * half + 384, :] = (ga * gelu).astype(BF16)
         gq = None
         for piece in range(4):
             rows = slice(UP_TWO + 192 * piece, UP_TWO + 192 * piece + 192)
             gg = g_gu[384 * piece : 384 * piece + 384, :]
-            g_w[b, rows, :] = nt(q3[b], gg).astype(BF16)
-            term = nn(w[b, rows, :], gg)
+            g_w[at[b], rows, :] = nt(q3.buffer[b], gg).astype(BF16)
+            term = nn(w[at[b], rows, :], gg)
             gq = term if gq is None else gq + term
         gq = gq.astype(BF16)
         for to in range(BLOCKS):
             gi3[to, 48 * b : 48 * b + 48, :] = gq[48 * to : 48 * to + 48]
+    finish = send_early(g_w, (g_near, g_far), idx, sem, UP_ONE + 192)
     norm_back(
-        middle, mean, inv, cols, GAIN_TWO, w, slice(UP_ONE, UP_ONE + 192), slice(0, 192), gi3, g_n, g_w, small, 1, g_top, g_mid
+        at, middle.wait(), mean, inv, cols.wait(), GAIN_TWO, w, slice(UP_ONE, UP_ONE + 192), slice(0, 192), gi3, g_n, g_w, small, 1, g_top, g_mid
     )
-    send_pieces(g_w, (g_near, g_far), idx, sem)
+    finish()
 
 
 def gelu_slope(gate, square, t, rate):
@@ -256,14 +302,14 @@
     return nt(pick, high) + nt(pick, low)
 
 
-def norm_back(h, mean, inv, cols, gain_at, w, w_rows, w_lanes, gi, g_n, g_w, small, place, g_in, g_out):
+def norm_back(at, h, mean, inv, cols, gain_at, w, w_rows, w_lanes, gi, g_n, g_w, small, place, g_in, g_out):
     plain = cross = 0.0
     for b in range(BLOCKS):
         rows = pl.ds(b * 192, 192)
-        gain = cols[rows, gain_at : gain_at + 1]
+        gain = column(cols, rows, gain_at, h.shape[1])
         xh = (h[rows, :] - mean) * inv
-        gn = nn(w[b, w_rows, w_lanes], gi[b])
-        g_w[b, w_rows, w_lanes] = nt((xh * gain).astype(BF16), gi[b]).astype(BF16)
+        gn = nn(w[at[b], w_rows, w_lanes], gi[b])
+        g_w[at[b], w_rows, w_lanes] = nt((xh * gain).astype(BF16), gi[b]).astype(BF16)
         gx = gn * xh
         small[b] = row_sums(place, gx)
         g_n[rows, :] = gn * gain
@@ -274,53 +320,68 @@
     for b in range(BLOCKS):
         rows = pl.ds(b * 192, 192)
         xh = (h[rows, :] - mean) * inv
-        g_out[rows, :] = g_in[rows, :].astype(F32) + inv * (g_n[rows, :] - plain - xh * cross)
+        value = g_in[rows, :].astype(F32) + inv * (g_n[rows, :] - plain - xh * cross)
+        if isinstance(g_out, Move):
+            g_out.buffer[rows, :] = value
+            g_out.start((rows, slice(None)))
+        else:
+            g_out[rows, :] = value
 
 
 def bwd_conv_kernel(
-    seqs, penalty, idx, own, rel_a, rel_b, g_mid, q2, gated, conv, proj, pad, cols, kspec, ahead, back, small_ff,
-    filt, weight_two, features, back_full, gv, g_near, g_far, w, g_w, gi2, gcs, xs, sem
+    seqs, penalty, idx, table, g_mid, q2, gated, conv, proj, pad, cols, kspec, ahead, back, small_ff,
+    filt, weight_two, features, back_full, gv, g_near, g_far, g_w, gi2, gcs, xs, sem
 ):
-    fetch_table(idx, own, rel_a, rel_b, w, sem)
+    at = distances(idx)
+    table.start((slice(None), slice(OUT_ROWS, PARAM_ROWS + BLOCK_W)))
+    for part in (q2, g_mid, gated, proj, conv, kspec):
+        part.start()
+    w, q2, g_mid = table.wait(), q2.wait(), g_mid.wait()
     for c in range(BLOCKS):
         gt = block(g_mid, c).astype(BF16)
-        g_w[c, 0:192, 192:384] = nt(q2[c], gt).astype(BF16)
-        gq = nn(w[c, OUT_ROWS : OUT_ROWS + 192, 192:384], gt).astype(BF16)
+        g_w[at[c], 0:192, 192:384] = nt(q2[c], gt).astype(BF16)
+        gq = nn(w[at[c], OUT_ROWS : OUT_ROWS + 192, 192:384], gt).astype(BF16)
         for b in range(BLOCKS):
             gi2[b, 48 * c : 48 * c + 48, :] = gq[48 * b : 48 * b + 48]
     lane = lanes_of((BLOCK_W, LENGTH))
     first_lane = lane == 0
+    for part in (gated, proj, conv):
+        part.wait()
+    kspec = kspec.wait()
     for b in range(BLOCKS):
         rows = pl.ds(b * 192, 192)
-        g_gated = nn(w[b, OUT_ROWS : OUT_ROWS + 192, 0:192], gi2[b])
-        g_w[b, 0:192, 0:192] = nt(block(gated, b), gi2[b]).astype(BF16)
+        g_gated = nn(w[at[b], OUT_ROWS : OUT_ROWS + 192, 0:192], gi2[b])
+        g_w[at[b], 0:192, 0:192] = nt(block(gated.buffer, b), gi2[b]).astype(BF16)
+        tap_x = [column(cols, rows, TAP_X + n) for n in range(3)]
+        tap_g = [column(cols, rows, TAP_G + n) for n in range(3)]
+        skip = column(cols, rows, SKIP)
         sums = [0.0] * 7
         for s in range(seqs):
             here = slice(s * LENGTH, (s + 1) * LENGTH)
-            v = proj[b, 0:192, here].astype(F32)
+            v = proj.buffer[b, 0:192, here].astype(F32)
             xs[:, here] = (
-                cols[rows, TAP_X : TAP_X + 1] * later(v, lane)
-                + cols[rows, TAP_X + 1 : TAP_X + 2] * v
-                + cols[rows, TAP_X + 2 : TAP_X + 3] * earlier(v, lane)
+                tap_x[0] * later(v, lane)
+                + tap_x[1] * v
+                + tap_x[2] * earlier(v, lane)
             )
-            v = proj[b, 192:384, here].astype(F32)
+            v = proj.buffer[b, 192:384, here].astype(F32)
             after, before = later(v, lane), earlier(v, lane)
             gate = (
-                cols[rows, TAP_G : TAP_G + 1] * after
-                + cols[rows, TAP_G + 1 : TAP_G + 2] * v
-                + cols[rows, TAP_G + 2 : TAP_G + 3] * before
+                tap_g[0] * after
+                + tap_g[1] * v
+                + tap_g[2] * before
             )
             gg = g_gated[:, here]
             gcs[:, here] = gg * gate
-            z = gg * conv[rows, here].astype(F32)
+            z = gg * conv.buffer[rows, here].astype(F32)
             sums[4] = sums[4] + z * after
             sums[5] = sums[5] + z * v
             sums[6] = sums[6] + z * before
-            gv[b, 192:384, here] = (
+            gv.buffer[b, 192:384, here] = (
                 (
-                    cols[rows, TAP_G : TAP_G + 1] * earlier(z, lane)
-                    + cols[rows, TAP_G + 1 : TAP_G + 2] * z
-                    + cols[rows, TAP_G + 2 : TAP_G + 3] * later(z, lane)
+                    tap_g[0] * earlier(z, lane)
+                    + tap_g[1] * z
+                    + tap_g[2] * later(z, lane)
                 )
                 * pad[0:1, here]
             ).astype(BF16)
@@ -338,9 +399,9 @@
         for s in range(seqs):
             x_re = spec[s * 192 : s * 192 + 192, 0:LENGTH]
             x_im = spec[s * 192 : s * 192 + 192, LENGTH : 2 * LENGTH]
-            at = (seqs + s) * 192
-            g_re = spec[at : at + 192, 0:LENGTH]
-            g_im = spec[at : at + 192, LENGTH : 2 * LENGTH]
+            start = (seqs + s) * 192
+            g_re = spec[start : start + 192, 0:LENGTH]
+            g_im = spec[start : start + 192, LENGTH : 2 * LENGTH]
             p_re = p_re + g_re * x_re
             p_im = p_im + g_im * x_im
             p_off = p_off + (g_im * x_re - g_re * x_im)
@@ -355,77 +416,89 @@
             1,
             0,
         )
-        last, envelope, table = filter_values(w, b, cols, filt[HIDDEN_TWO])
-        g_table = g_table + penalty * table
-        g_decay = -(g_table * table * filter_lag())
+        last, envelope, kernel = filter_values(w, at, b, cols, filt[HIDDEN_TWO])
+        g_table = g_table + penalty * kernel
+        g_decay = -(g_table * kernel * filter_lag())
         g_shape = g_table * envelope
-        g_w[b, 192:384, 0:128] = exact(g_shape, filt[HIDDEN_TWO], 1, 0).astype(BF16)
+        g_w[at[b], 192:384, 0:128] = exact(g_shape, filt[HIDDEN_TWO], 1, 0).astype(BF16)
         term = exact(g_shape, last, 0, 0)
         g_hidden = term if b == 0 else g_hidden + term
         y = nn(jnp.concatenate(made, axis=0), back[...])
         for s in range(seqs):
             here = slice(s * LENGTH, (s + 1) * LENGTH)
-            z = y[s * 192 : s * 192 + 192] + cols[rows, SKIP : SKIP + 1] * gcs[:, here]
-            v = proj[b, 0:192, here].astype(F32)
+            z = y[s * 192 : s * 192 + 192] + skip * gcs[:, here]
+            v = proj.buffer[b, 0:192, here].astype(F32)
             sums[1] = sums[1] + z * later(v, lane)
             sums[2] = sums[2] + z * v
             sums[3] = sums[3] + z * earlier(v, lane)
-            gv[b, 0:192, here] = (
+            gv.buffer[b, 0:192, here] = (
                 (
-                    cols[rows, TAP_X : TAP_X + 1] * earlier(z, lane)
-                    + cols[rows, TAP_X + 1 : TAP_X + 2] * z
-                    + cols[rows, TAP_X + 2 : TAP_X + 3] * later(z, lane)
+                    tap_x[0] * earlier(z, lane)
+                    + tap_x[1] * z
+                    + tap_x[2] * later(z, lane)
                 )
                 * pad[0:1, here]
             ).astype(BF16)
-        table = small_ff[b]
-        for at, value in enumerate(sums + [g_decay]):
-            table = table + row_sums(2 + at, value)
-        table = table.astype(BF16)
-        g_w[b, 192:208, 256:384] = table[:, 0:128]
-        g_w[b, 208:224, 256:320] = table[:, 128:192]
-        g_w[b, 208:224, 320:384] = jnp.zeros((16, 64), BF16)
-        g_w[b, 224:384, 256:384] = jnp.zeros((160, 128), BF16)
+        gv.start(b)
+        totals = small_ff[b]
+        for place, value in enumerate(sums + [g_decay]):
+            totals = totals + row_sums(2 + place, value)
+        totals = totals.astype(BF16)
+        g_w[at[b], 192:208, 256:384] = totals[:, 0:128]
+        g_w[at[b], 208:224, 256:320] = totals[:, 128:192]
+        g_w[at[b], 208:224, 320:384] = jnp.zeros((16, 64), BF16)
+        g_w[at[b], 224:384, 256:384] = jnp.zeros((160, 128), BF16)
     g_two = g_hidden * filt[SLOPE_TWO]
     g_one = exact(g_two, weight_two[...], 1, 1) * filt[SLOPE_ONE]
     g_weight_two = exact(filt[HIDDEN_ONE], g_two, 0, 0).astype(BF16)
     g_weight_one = exact(features[...], g_one, 0, 0)[0:16, :].astype(BF16)
     for b in range(BLOCKS):
-        g_w[b, 192:320, 128:256] = g_weight_two
-        g_w[b, 320:336, 128:256] = g_weight_one
-        g_w[b, 336:384, 128:256] = jnp.zeros((48, 128), BF16)
+        g_w[at[b], 192:320, 128:256] = g_weight_two
+        g_w[at[b], 320:336, 128:256] = g_weight_one
+        g_w[at[b], 336:384, 128:256] = jnp.zeros((48, 128), BF16)
     send_pieces(g_w, (g_near, g_far), idx, sem)
 
 
 def bwd_in_kernel(first, *refs):
     refs = list(refs)
-    idx, own, rel_a, rel_b, gv, g_mid, q1, h, stats, cols = refs[:10]
-    refs = refs[10:]
+    idx, table, gv, g_mid, q1, h, stats, cols = refs[:8]
+    refs = refs[8:]
     chosen = refs.pop(0) if first else None
-    g_out, g_near, g_far, w, g_w, gi1, g_n, small, sem = refs[:9]
-    g_h = refs[9] if first else g_out
-    fetch_table(idx, own, rel_a, rel_b, w, sem)
+    g_out, g_near, g_far, g_w, gi1, g_n, small, sem = refs[:8]
+    g_h = refs[8] if first else g_out
+    at = distances(idx)
+    for c in range(BLOCKS):
+        gv.start(c)
+        q1.start(c)
+        if c == 0:
+            table.start((slice(None), slice(IN_ONE, OUT_ROWS)))
+    for part in (h, g_mid):
+        part.start()
+    w = table.wait()
     mean = stats[0:1, :]
     inv = stats[1:2, :]
     for c in range(BLOCKS):
-        g_w[c, IN_TWO : IN_TWO + 384, :] = nt(q1[c], gv[c]).astype(BF16)
-        gq = nn(w[c, IN_TWO : IN_TWO + 384, :], gv[c]).astype(BF16)
+        gv.wait(c)
+        q1.wait(c)
+        g_w[at[c], IN_TWO : IN_TWO + 384, :] = nt(q1.buffer[c], gv.buffer[c]).astype(BF16)
+        gq = nn(w[at[c], IN_TWO : IN_TWO + 384, :], gv.buffer[c]).astype(BF16)
         for b in range(BLOCKS):
             gi1[b, 96 * c : 96 * c + 96, :] = gq[96 * b : 96 * b + 96]
     norm_back(
-        h, mean, inv, cols, GAIN_ONE, w, slice(IN_ONE, IN_ONE + 192), slice(0, 384), gi1, g_n, g_w, small, 0, g_mid, g_h
+        at, h.wait(), mean, inv, cols, GAIN_ONE, w, slice(IN_ONE, IN_ONE + 192), slice(0, 384), gi1, g_n, g_w, small, 0, g_mid.wait(), g_h
     )
     for b in range(BLOCKS):
         rows = pl.ds(b * 192, 192)
-        table = small[b]
+        totals = small[b]
         if first:
             value = g_h[rows, :]
             masked = value * chosen[0:1, :]
-            table = table + row_sums(1, masked)
-            g_out[b] = (value - masked).astype(BF16)
-        g_w[b, 576:592, 0:192] = table.astype(BF16)
-        g_w[b, 576:592, 192:384] = jnp.zeros((16, 192), BF16)
-        g_w[b, 592:640, :] = jnp.zeros((48, 384), BF16)
+            totals = totals + row_sums(1, masked)
+            g_out.buffer[b] = (value - masked).astype(BF16)
+            g_out.start(b)
+        g_w[at[b], 576:592, 0:192] = totals.astype(BF16)
+        g_w[at[b], 576:592, 192:384] = jnp.zeros((16, 192), BF16)
+        g_w[at[b], 592:640, :] = jnp.zeros((48, 384), BF16)
     send_pieces(g_w, (g_near, g_far), idx, sem)
 
 
@@ -437,36 +510,64 @@
     return (idx[0] - k) & (BLOCKS - 1)
 
 
-def run_copies(pairs, sem):
+def distances(idx):
+    return [(idx[0] - b) & (BLOCKS - 1) for b in range(BLOCKS)]
+
+
+def start_copies(pairs, sem):
     copies = [pltpu.make_async_copy(source, target, sem.at[at]) for at, (source, target) in enumerate(pairs)]
     for copy in copies:
         copy.start()
-    for copy in copies:
-        copy.wait()
+
+    def wait():
+        for copy in copies:
+            copy.wait()
+
+    return wait
+
+
+def run_copies(pairs, sem):
+    start_copies(pairs, sem)()
+
+
+def send_early(table, outs, idx, sem, done):
+    rows = outs[0].shape[2]
+    late = -(-done // rows)
+    copies = []
+    for core in range(2):
+        for chip in range(4):
+            at = idx[1] ^ (2 * chip + core)
+            copy = pltpu.make_async_copy(
+                table.at[:, piece_rows(idx, core, chip, rows), :], outs[core].at[chip], sem.at[len(copies)]
+            )
+            pl.when(at >= late)(copy.start)
+            copies.append((at, copy))
+
+    def finish():
+        for at, copy in copies:
+            pl.when(at < late)(copy.start)
+        for _, copy in copies:
+            copy.wait()
+
+    return finish
 
 
 def send_pieces(table, outs, idx, sem):
     rows = outs[0].shape[2]
     run_copies(
-        [
-            (table.at[block_of(idx, k), piece_rows(idx, core, chip, rows), :], outs[core].at[chip, k])
-            for core in range(2)
-            for chip in range(4)
-            for k in range(BLOCKS)
-        ],
+        [(table.at[:, piece_rows(idx, core, chip, rows), :], outs[core].at[chip]) for core in range(2) for chip in range(4)],
         sem,
     )
 
 
 def fetch_table(idx, own, rel_a, rel_b, table, sem):
     rows = rel_a.shape[2]
-    run_copies(
-        [(own, table.at[idx[0]])]
+    return start_copies(
+        [(own, table.at[0])]
         + [
-            (rel.at[chip, k - 1], table.at[block_of(idx, k), piece_rows(idx, core, chip, rows), :])
+            (rel.at[chip], table.at[1:BLOCKS, piece_rows(idx, core, chip, rows), :])
             for core, rel in enumerate((rel_a, rel_b))
             for chip in range(4)
-            for k in range(1, BLOCKS)
         ],
         sem,
     )
@@ -483,8 +584,8 @@
     return jnp.where(place < LENGTH, place, 2 * LENGTH - place).astype(F32)
 
 
-def filter_values(w, b, cols, hidden):
-    packed = w[b, PARAM_ROWS : PARAM_ROWS + BLOCK_W, 0:256].astype(F32)
+def filter_values(w, at, b, cols, hidden):
+    packed = w[at[b], PARAM_ROWS : PARAM_ROWS + BLOCK_W, 0:256].astype(F32)
     last = packed[:, 0:128] + packed[:, 128:256]
     lag = filter_lag()
     envelope = jnp.exp(-lag * cols[b * BLOCK_W : (b + 1) * BLOCK_W, DECAY : DECAY + 1]) * (1.0 / math.sqrt(LENGTH))
@@ -492,12 +593,12 @@
     return last, envelope, exact(last, hidden, 1, 1) * envelope
 
 
-def make_params(w, hidden, ahead_full, cols, kspec):
+def make_params(w, at, hidden, ahead_full, cols, kspec):
     for b in range(BLOCKS):
         rows = pl.ds(b * BLOCK_W, BLOCK_W)
-        three = w[b, PARAM_ROWS : PARAM_ROWS + BLOCK_W, 256:384].astype(F32)
+        three = w[at[b], PARAM_ROWS : PARAM_ROWS + BLOCK_W, 256:384].astype(F32)
         cols[rows, :] = three + pltpu.roll(three, 128 - 16, 1) + pltpu.roll(three, 128 - 32, 1)
-        kspec[rows, :] = exact(filter_values(w, b, cols, hidden[HIDDEN_TWO])[2], ahead_full[...], 1, 0)
+        kspec[rows, :] = exact(filter_values(w, at, b, cols, hidden[HIDDEN_TWO])[2], ahead_full[...], 1, 0)
 
 
 def fold_back(lines, wide, count):
@@ -595,20 +696,36 @@
         own_piece(idx, table, pieces[layer])
 
 
-def finish_kernel(layer, idx, *refs):
-    pieces, refs = refs[:2], refs[2:]
+def finish_kernel(layer, groups, idx, *refs):
+    count = 2 * len(groups)
+    pieces, refs = refs[:count], refs[count:]
+    names = sum(groups, ())
+    with_ff, with_mix = "ff" in names, "conv" in names
+    outs = 4 * with_ff + 5 * with_mix
     if layer == 0:
-        other, refs = refs[9], refs[10:]
-    in_one, in_two, out_one, out_two, up_one, up_two, down_one, down_two, three = refs[:9]
-    rest, (ff, conv, inp, wide, sem) = refs[9:-5], refs[-5:]
+        refs = refs[outs:]
+        if with_mix:
+            other, refs = refs[0], refs[1:]
+    if with_ff:
+        up_one, up_two, down_one, down_two = refs[:4]
+        refs = refs[4:]
+    if with_mix:
+        in_one, in_two, out_one, out_two, three = refs[:5]
+        refs = refs[5:]
+    rest, (ff, conv, inp, wide, sem) = refs[:-5], refs[-5:]
+    tables = {"ff": ff, "conv": conv, "in": inp}
     pairs = []
-    for core, rel in enumerate(pieces):
-        first = 0
-        for name, table in (("ff", ff), ("conv", conv), ("in", inp)):
-            rows = PIECE_ROWS[name]
-            for chip in range(4):
-                pairs.append((rel.at[chip, pl.ds(first, rows), :], table.at[piece_rows(idx, core, chip, rows), :]))
-            first += rows
+    for at, group in enumerate(groups):
+        for core in range(2):
+            rel = pieces[2 * at + core]
+            first = 0
+            for name in group:
+                rows = PIECE_ROWS[name]
+                for chip in range(4):
+                    pairs.append(
+                        (rel.at[chip, pl.ds(first, rows), :], tables[name].at[piece_rows(idx, core, chip, rows), :])
+                    )
+                first += rows
     run_copies(pairs, sem)
 
     def spread(out, values, lanes, first):
@@ -622,19 +739,22 @@
         wide[1, 0:count, 0:64] = values[:, 128:192].astype(F32)
         fold_out(wide, out, count)
 
+    if with_ff:
+        for q in range(4):
+            at = UP_TWO + 192 * q
+            spread(up_two, ff[at : at + 192, :], 12, 3 * q)
+        narrow_of(up_one, ff[UP_ONE : UP_ONE + 192, 0:192])
+        narrow_of(down_two, ff[UP_ONE : UP_ONE + 192, 192:384])
+        narrow_of(
+            down_one,
+            jnp.concatenate([ff[DOWN_ONE : DOWN_ONE + 384, 0:192], ff[DOWN_ONE : DOWN_ONE + 384, 192:384]], axis=0),
+        )
+    if not with_mix:
+        return
     spread(in_one, inp[IN_ONE : IN_ONE + 192, :], 3, 0)
     spread(in_two, inp[IN_TWO : IN_TWO + 384, :], 3, 0)
-    for q in range(4):
-        at = UP_TWO + 192 * q
-        spread(up_two, ff[at : at + 192, :], 12, 3 * q)
     narrow_of(out_one, conv[0:192, 0:192])
     narrow_of(out_two, conv[0:192, 192:384])
-    narrow_of(up_one, ff[UP_ONE : UP_ONE + 192, 0:192])
-    narrow_of(down_two, ff[UP_ONE : UP_ONE + 192, 192:384])
-    narrow_of(
-        down_one,
-        jnp.concatenate([ff[DOWN_ONE : DOWN_ONE + 384, 0:192], ff[DOWN_ONE : DOWN_ONE + 384, 192:384]], axis=0),
-    )
     three[...] = conv[192:384, 0:128].astype(F32)
     if layer > 0:
         rest[0][0:192, :] = conv[192:384, 128:384].astype(F32)
@@ -653,11 +773,13 @@
         g_gain_one[here, :] = last[0:1]
         g_gain_two[here, :] = small[1:2]
         g_skip[here, :] = small[2:3]
-        g_taps[at, :, 0:192] = small[3:6]
-        g_taps[at, :, 192:384] = small[6:9]
+        both = jnp.concatenate([small[3:6], small[6:9]], axis=1)
+        for tap in range(3):
+            g_taps[at, tap, :, :] = both[tap : tap + 1]
         g_decay[here, :] = small[9:10]
         g_two[at] = shared[0:128]
-        g_one[at] = shared[128:133]
+        for row in range(5):
+            g_one[row, here, :] = shared[128 + row : 129 + row]
         g_bias[here, :] = shared[133:134]
         if at == 0:
             g_mask[...] = last[1:2]
@@ -672,23 +794,68 @@
     return jax.ShapeDtypeStruct(shape, dtype)
 
 
-def call(kernel, outs, scratch, in_specs, out_specs, micros, deps=(), aliases=None):
-    count = len(in_specs)
+EARLY = "early"
+LATE = "late"
+
+
+class Move:
+    def __init__(self, buffer, operand, sem, inward):
+        self.buffer, self.operand, self.sem, self.inward = buffer, operand, sem, inward
+        self.open = []
+
+    def start(self, part=None):
+        here = self.buffer if part is None else self.buffer.at[part]
+        there = self.operand if part is None else self.operand.at[part]
+        pair = (there, here) if self.inward else (here, there)
+        copy = pltpu.make_async_copy(*pair, self.sem.at[len(self.open)])
+        copy.start()
+        self.open.append(copy)
+
+    def wait(self, at=None):
+        for n, copy in enumerate(self.open):
+            if copy is not None and (at is None or n == at):
+                copy.wait()
+                self.open[n] = None
+        return self.buffer
+
+
+def call(kernel, outs, scratch, in_specs, out_specs, micros, deps=()):
+    outs = list(outs) if isinstance(outs, (list, tuple)) else [outs]
+    out_specs = list(out_specs) if isinstance(out_specs, (list, tuple)) else [out_specs]
+    ins, own = len(in_specs), len(scratch)
+    early = [at for at, spec in enumerate(in_specs) if spec is EARLY]
+    late = [at for at, spec in enumerate(out_specs) if spec is LATE]
 
     def body(*refs):
-        kernel(*refs[:count], *refs[count + len(deps) :])
-
-    made = pl.pallas_call(
-        body,
-        out_shape=outs,
-        in_specs=list(in_specs) + [ANY] * len(deps),
-        out_specs=out_specs,
-        scratch_shapes=scratch,
-        input_output_aliases=aliases or {},
-        compiler_params=pltpu.CompilerParams(vmem_limit_bytes=56 << 20),
-        cost_estimate=pl.CostEstimate(flops=int(micros * 1e9), bytes_accessed=1 << 20, transcendentals=0),
-    )
-    return lambda *arrays: made(*arrays, *deps)
+        inputs = list(refs[:ins])
+        refs = refs[ins + len(deps) :]
+        results = list(refs[: len(outs)])
+        mine, refs = refs[len(outs) : len(outs) + own], refs[len(outs) + own :]
+        for j, at in enumerate(early):
+            inputs[at] = Move(refs[j], inputs[at], refs[-1].at[j], True)
+        for j, at in enumerate(late):
+            results[at] = Move(refs[len(early) + j], results[at], refs[-1].at[len(early) + j], False)
+        kernel(*inputs, *results, *mine)
+        for at in late:
+            results[at].wait()
+
+    def run(*arrays):
+        buffers = [pltpu.VMEM(arrays[at].shape, arrays[at].dtype) for at in early]
+        buffers += [pltpu.VMEM(outs[at].shape, outs[at].dtype) for at in late]
+        if buffers:
+            buffers.append(pltpu.SemaphoreType.DMA((len(buffers), BLOCKS)))
+        made = pl.pallas_call(
+            body,
+            out_shape=outs,
+            in_specs=[ANY if spec is EARLY else spec for spec in in_specs] + [ANY] * len(deps),
+            out_specs=[ANY if spec is LATE else spec for spec in out_specs],
+            scratch_shapes=list(scratch) + buffers,
+            compiler_params=pltpu.CompilerParams(vmem_limit_bytes=58 << 20),
+            cost_estimate=pl.CostEstimate(flops=int(micros * 1e9), bytes_accessed=1 << 20, transcendentals=0),
+        )(*arrays, *deps)
+        return made if len(outs) > 1 else made[0]
+
+    return run
 
 
 def place_parts_kernel(table, out):
@@ -726,8 +893,8 @@
     return jnp.stack([narrow_shift(piece, k) for k in range(1, BLOCKS)])
 
 
-def others_at_once(piece, me):
-    moved = lax.all_to_all(jnp.stack([piece] * BLOCKS), "narrow", split_axis=0, concat_axis=0, tiled=True)
+def others_at_once(pieces, me):
+    moved = lax.all_to_all(pieces, "narrow", split_axis=0, concat_axis=0, tiled=True)
     return jnp.stack([lax.dynamic_index_in_dim(moved, (me - k) % BLOCKS, 0, keepdims=False) for k in range(1, BLOCKS)])
 
 
@@ -849,27 +1016,6 @@
     *mix, mix_zero, mix_one = pack(
         pack_mix_kernel, MIX_ROWS, lines[:4] + per_feature, scratch=[pltpu.VMEM((16, BLOCK_W), F32)]
     )
-    *ff, ff_zero, ff_one = pack(pack_ff_kernel, FF_ROWS, lines[4:], (mix_zero,))
-
-    parts = token_parts(tokens)
-    near, across, far = (narrow_shift(parts[k], k) for k in range(1, BLOCKS))
-    mix_zero = over_blocks(mix_zero)
-    ff_zero = over_blocks(after(ff_zero, mix_zero))
-    mix_chips = over_chips(after(mix_zero, near))
-    mix_chips, ff_zero, across, far = settle(mix_chips, ff_zero, across, far)
-    mix_zero = (mix[0], mix_chips, wide_shift(mix_chips, 1))
-    tokens_here = [parts[0], near, across, far]
-    mix_zero, tokens_here, ff_zero, mix_one = settle(mix_zero, tokens_here, ff_zero, mix_one)
-    ff_chips = over_chips(ff_zero)
-    mix_one = others_at_once(mix_one, me)
-
-    own_lengths = lax.dynamic_slice_in_dim(lengths, me * seqs, seqs, 0)
-    own_masked = lax.dynamic_slice_in_dim(masked, me * seqs, seqs, 0)
-    positions = jnp.arange(LENGTH, dtype=jnp.int32)
-    pad = (positions[None, :] < own_lengths[:, None]).astype(F32).reshape(1, span)
-    pad = jnp.broadcast_to(pad, (8, span))
-    chosen = jnp.broadcast_to(own_masked.astype(F32).reshape(1, span), (8, span))
-
     ahead, back = spectrum_tables()
     ahead_low = jnp.asarray(ahead[:LENGTH]).astype(BF16)
     back_low = jnp.asarray(back[:, :LENGTH]).astype(BF16)
@@ -879,11 +1025,34 @@
     hidden = [
         filter_hidden(features, filter_one[layer], filter_bias[layer], filter_two[layer]) for layer in range(LAYERS)
     ]
+    own_lengths = lax.dynamic_slice_in_dim(lengths, me * seqs, seqs, 0)
+    own_masked = lax.dynamic_slice_in_dim(masked, me * seqs, seqs, 0)
+    positions = jnp.arange(LENGTH, dtype=jnp.int32)
+    pad = (positions[None, :] < own_lengths[:, None]).astype(F32).reshape(1, span)
+    pad = jnp.broadcast_to(pad, (8, span))
+    chosen = jnp.broadcast_to(own_masked.astype(F32).reshape(1, span), (8, span))
+
+    parts = token_parts(tokens)
+    near, across = narrow_shift(parts[1], 1), narrow_shift(parts[2], 2)
+
+    mix_zero = others_at_once(jnp.stack([mix_zero] * BLOCKS), me)
+    *ff, ff_zero, ff_one = pack(pack_ff_kernel, FF_ROWS, lines[4:], (near, across))
+    mix_zero, ff_zero, hidden, near, across, far, pad, chosen = settle(
+        mix_zero, ff_zero, hidden, near, across, parts[3], pad, chosen
+    )
+    far = narrow_shift(far, 3)
+    mix_chips = over_chips(mix_zero)
+    ff_zero = others_at_once(jnp.stack([ff_zero] * BLOCKS), me)
+    one = jnp.stack([jnp.concatenate([mix_one, ff_one], axis=0)] * BLOCKS)
+    mix_chips, ff_zero, one, far = settle(mix_chips, ff_zero, one, far)
+    mix_zero = (mix[0], mix_chips, wide_shift(mix_chips, 1))
+    tokens_here = [parts[0], near, across, far]
+
     penalty = 4.0 * math.sqrt(all_tokens) / (wide_count * BLOCKS)
-    mix_scratch = pltpu.VMEM((BLOCKS, MIX_ROWS, 384), BF16)
-    ff_scratch = pltpu.VMEM((BLOCKS, FF_ROWS, 384), BF16)
-    fetched = pltpu.SemaphoreType.DMA((25,))
-    sent = pltpu.SemaphoreType.DMA((32,))
+    mix_table = shaped(BF16, BLOCKS, MIX_ROWS, 384)
+    ff_table = shaped(BF16, BLOCKS, FF_ROWS, 384)
+    fetched = pltpu.SemaphoreType.DMA((9,))
+    sent = pltpu.SemaphoreType.DMA((8,))
     table_specs = [SCALARS, ANY, ANY, ANY]
 
     def ahead_mix(layer, table, h, deps=()):
@@ -901,16 +1070,16 @@
                 shaped(F32, 8, span),
                 shaped(F32, D, 128),
                 shaped(F32, D, 256),
+                mix_table,
             ],
             [
-                mix_scratch,
                 pltpu.VMEM((D, span), BF16),
                 pltpu.VMEM((BLOCK_W, span), F32),
                 pltpu.VMEM((BLOCK_W, span), F32),
                 fetched,
             ],
             table_specs + [WHOLE] * (BLOCKS + 1 if first else 1) + [WHOLE] * 5,
-            [WHOLE] * (10 if first else 9),
+            ([LATE] if first else []) + [LATE] * 4 + [WHOLE] * 5 + [LATE],
             18,
             deps,
         )(idx, *table, *([*h, chosen] if first else [h]), pad, hidden[layer], ahead_full, ahead_low, back_low)
@@ -925,55 +1094,62 @@
                 shaped(BF16, BLOCKS, 192, span),
                 shaped(BF16, BLOCKS, BLOCK_W, span) if last else shaped(F32, D, span),
                 shaped(F32, 8, span),
+                ff_table,
             ],
-            [ff_scratch, pltpu.VMEM((D, span), BF16), pltpu.VMEM((FF_BLOCK, span), BF16), fetched],
+            [pltpu.VMEM((D, span), BF16), pltpu.VMEM((FF_BLOCK, span), BF16), fetched],
             table_specs + [WHOLE] * 2,
-            [WHOLE] * 5,
+            [LATE] * 2 + [WHOLE] * 3 + [LATE],
             15,
             deps,
         )(idx, *table, middle, cols)
 
     saved = []
-    h, q1, proj, conv, gated, q2, middle, stats_one, cols, kspec = ahead_mix(0, mix_zero, tokens_here)
+    mix_zero, tokens_here, ff_zero, one = settle(mix_zero, tokens_here, ff_zero, one)
+    ff_chips = over_chips(ff_zero)
+    one = others_at_once(one, me)
+    h, q1, proj, conv, gated, q2, middle, stats_one, cols, kspec, mix_w = ahead_mix(0, mix_zero, tokens_here)
     parts = token_parts(cotangent)
-    middle, ff_chips, mix_one, ff_one = settle(middle, ff_chips, mix_one, ff_one)
+    middle, ff_chips, one, parts = settle(middle, ff_chips, one, parts)
     ff_zero = (ff[0], ff_chips, wide_shift(ff_chips, 1))
-    middle, ff_zero, mix_one, ff_one = settle(middle, ff_zero, mix_one, ff_one)
-    mix_chips = over_chips(mix_one)
-    ff_one = others_at_once(ff_one, me)
-    q3, gate_up, q4, h_next, stats_two = ahead_ff(0, ff_zero, middle, cols)
-    saved.append((h, q1, proj, conv, gated, q2, middle, stats_one, cols, kspec, q3, gate_up, q4, stats_two))
-    h, mix_chips, ff_one = settle(h_next, mix_chips, ff_one)
+    middle, ff_zero, one, parts = settle(middle, ff_zero, one, parts)
+    rows = MIX_ROWS // 8
+    mix_chips = over_chips(one[:, :rows])
+    near, far = narrow_shift(parts[1], 1), narrow_shift(parts[3], 3)
+    q3, gate_up, q4, h_next, stats_two, ff_w = ahead_ff(0, ff_zero, middle, cols)
+    saved.append((h, q1, proj, conv, gated, q2, middle, stats_one, cols, kspec, q3, gate_up, q4, stats_two, mix_w, ff_w))
+    h, mix_chips, ff_one, near, far, across = settle(h_next, mix_chips, one[:, rows:], near, far, parts[2])
     mix_one = (mix[1], mix_chips, wide_shift(mix_chips, 1))
-    h, mix_one, ff_one, parts = settle(h, mix_one, ff_one, parts)
+    h, mix_one, ff_one, across = settle(h, mix_one, ff_one, across)
     ff_chips = over_chips(ff_one)
-    near, far = narrow_shift(parts[1], 1), narrow_shift(parts[3], 3)
-    q1, proj, conv, gated, q2, middle, stats_one, cols, kspec = ahead_mix(1, mix_one, h)
-    middle, ff_chips, near, far = settle(middle, ff_chips, near, far)
-    ff_one = (ff[1], ff_chips, wide_shift(ff_chips, 1))
-    middle, ff_one, across = settle(middle, ff_one, parts[2])
     across = narrow_shift(across, 2)
     cotangent_here = [parts[0], near, across, far]
-    q3, gate_up, q4, h_last, stats_two = ahead_ff(1, ff_one, middle, cols)
-    saved.append((h, q1, proj, conv, gated, q2, middle, stats_one, cols, kspec, q3, gate_up, q4, stats_two))
-    weights_mix, weights_ff = (mix_zero, mix_one), (ff_zero, ff_one)
+    q1, proj, conv, gated, q2, middle, stats_one, cols, kspec, mix_w = ahead_mix(1, mix_one, h)
+    middle, ff_chips, cotangent_here = settle(middle, ff_chips, cotangent_here)
+    ff_one = (ff[1], ff_chips, wide_shift(ff_chips, 1))
+    middle, ff_one = settle(middle, ff_one)
+    q3, gate_up, q4, h_last, stats_two, ff_w = ahead_ff(1, ff_one, middle, cols)
+    saved.append((h, q1, proj, conv, gated, q2, middle, stats_one, cols, kspec, q3, gate_up, q4, stats_two, mix_w, ff_w))
 
     sizes = [weight.shape[2] // 128 for weight in factors]
 
-    def finish(layer, group, earlier):
-        shapes = [(LAYERS, size, 128) for size in sizes] + [(LAYERS, BLOCK_W, 128)]
+    def finish(layer, names, groups, earlier):
+        with_ff, with_mix = "ff" in sum(names, ()), "conv" in sum(names, ())
+        shapes = [(LAYERS, size, 128) for size in (sizes[4:] if with_ff else []) + (sizes[:4] if with_mix else [])]
+        shapes += [(LAYERS, BLOCK_W, 128)] if with_mix else []
         specs = [pl.BlockSpec((None, *shape[1:]), lambda _: (layer, 0, 0)) for shape in shapes]
-        if layer:
+        rest = []
+        if with_mix and layer:
             rest = [(208, 256)]
-        else:
-            rest = [(LAYERS, BLOCK_W)] * 3 + [(LAYERS, 3, 384), (LAYERS, BLOCK_W), (1, BLOCK_W)]
-            rest += [(LAYERS, 5, 128), (LAYERS, 128), (LAYERS, 128, 128)]
+        elif with_mix:
+            rest = [(LAYERS, BLOCK_W)] * 3 + [(LAYERS, 3, 1, 384), (LAYERS, BLOCK_W), (1, BLOCK_W)]
+            rest += [(5, LAYERS, 128), (LAYERS, 128), (LAYERS, 128, 128)]
         specs += [pl.BlockSpec(shape, lambda _, n=len(shape): (0,) * n) for shape in rest]
-        inputs = [SCALARS] + [ANY] * (2 + len(earlier))
-        if earlier:
+        arrays = [part for group in groups for part in group]
+        inputs = [SCALARS] + [ANY] * (len(arrays) + len(earlier))
+        if earlier and with_mix:
             inputs[-1] = pl.BlockSpec(earlier[-1].shape, lambda _: (0, 0))
         return pl.pallas_call(
-            functools.partial(finish_kernel, layer),
+            functools.partial(finish_kernel, layer, names),
             grid=(1,),
             out_shape=[shaped(F32, *shape) for shape in shapes + rest],
             in_specs=inputs,
@@ -985,10 +1161,10 @@
                 pltpu.VMEM((2, 768, 128), F32),
                 pltpu.SemaphoreType.DMA((24,)),
             ],
-            input_output_aliases={3 + at: at for at in range(9)} if earlier else {},
+            input_output_aliases={1 + len(arrays) + at: at for at in range(len(shapes))} if earlier else {},
             compiler_params=pltpu.CompilerParams(vmem_limit_bytes=56 << 20),
             cost_estimate=pl.CostEstimate(flops=4 * 10**9, bytes_accessed=1 << 20, transcendentals=0),
-        )(idx, *group, *earlier)
+        )(idx, *arrays, *earlier)
 
     def collect(table, dtype):
         return call(place_parts_kernel, shaped(dtype, BLOCK_W, BLOCKS * span), [], [WHOLE], WHOLE, 2)(table)
@@ -998,12 +1174,11 @@
 
     def back_ff(layer, g_top, deps):
         last = layer == LAYERS - 1
-        h, q1, proj, conv, gated, q2, middle, stats_one, cols, kspec, q3, gate_up, q4, stats_two = saved[layer]
+        h, q1, proj, conv, gated, q2, middle, stats_one, cols, kspec, q3, gate_up, q4, stats_two, mix_w, ff_w = saved[layer]
         return call(
             functools.partial(bwd_ff_kernel, last),
             [shaped(F32, D, span), *[shaped(BF16, 4, BLOCKS, FF_ROWS // 8, 384)] * 2, shaped(F32, BLOCKS, 16, BLOCK_W)],
             [
-                ff_scratch,
                 pltpu.VMEM((BLOCKS, FF_ROWS, 384), BF16),
                 pltpu.VMEM((D, span), BF16),
                 pltpu.VMEM((BLOCKS, 192, span), BF16),
@@ -1012,32 +1187,31 @@
                 pltpu.VMEM((D, span), F32),
                 sent,
             ],
-            table_specs + [WHOLE] * (BLOCKS if last else 1) + [WHOLE] * 6,
-            [WHOLE, ANY, ANY, WHOLE],
+            [SCALARS, EARLY] + [EARLY] * (BLOCKS if last else 1) + [EARLY] * 4 + [WHOLE, EARLY],
+            [LATE, ANY, ANY, WHOLE],
             27,
             deps,
-        )(idx, *weights_ff[layer], *(g_top if last else [g_top]), q4, gate_up, q3, middle, stats_two, cols)
+        )(idx, ff_w, *(g_top if last else [g_top]), q4, gate_up, q3, middle, stats_two, cols)
 
     def back_conv(layer, g_mid, small_ff, deps):
-        h, q1, proj, conv, gated, q2, middle, stats_one, cols, kspec, q3, gate_up, q4, stats_two = saved[layer]
+        h, q1, proj, conv, gated, q2, middle, stats_one, cols, kspec, q3, gate_up, q4, stats_two, mix_w, ff_w = saved[layer]
         return call(
             functools.partial(bwd_conv_kernel, seqs, penalty),
             [shaped(BF16, BLOCKS, 384, span), *[shaped(BF16, 4, BLOCKS, 48, 384)] * 2],
             [
-                mix_scratch,
                 pltpu.VMEM((BLOCKS, 384, 384), BF16),
                 pltpu.VMEM((BLOCKS, 192, span), BF16),
                 pltpu.VMEM((BLOCK_W, span), F32),
                 pltpu.VMEM((BLOCK_W, span), F32),
                 sent,
             ],
-            table_specs + [WHOLE] * 15,
-            [WHOLE, ANY, ANY],
+            [SCALARS, EARLY] + [EARLY] * 5 + [WHOLE] * 2 + [EARLY] + [WHOLE] * 7,
+            [LATE, ANY, ANY],
             23,
             deps,
         )(
             idx,
-            *weights_mix[layer],
+            mix_w,
             g_mid,
             q2,
             gated,
@@ -1057,7 +1231,7 @@
 
     def back_in(layer, gv, g_mid, deps):
         first = layer == 0
-        h, q1, proj, conv, gated, q2, middle, stats_one, cols, kspec, q3, gate_up, q4, stats_two = saved[layer]
+        h, q1, proj, conv, gated, q2, middle, stats_one, cols, kspec, q3, gate_up, q4, stats_two, mix_w, ff_w = saved[layer]
         return call(
             functools.partial(bwd_in_kernel, first),
             [
@@ -1065,7 +1239,6 @@
                 *[shaped(BF16, 4, BLOCKS, IN_GRAD_ROWS // 8, 384)] * 2,
             ],
             [
-                mix_scratch,
                 pltpu.VMEM((BLOCKS, IN_GRAD_ROWS, 384), BF16),
                 pltpu.VMEM((BLOCKS, 384, span), BF16),
                 pltpu.VMEM((D, span), F32),
@@ -1073,11 +1246,11 @@
                 sent,
             ]
             + ([pltpu.VMEM((D, span), F32)] if first else []),
-            table_specs + [WHOLE] * (7 if first else 6),
-            [WHOLE, ANY, ANY],
+            [SCALARS] + [EARLY] * 5 + [WHOLE] * (3 if first else 2),
+            [LATE, ANY, ANY],
             12,
             deps,
-        )(idx, *weights_mix[layer], gv, g_mid, q1, h, stats_one, cols, *([chosen] if first else []))
+        )(idx, mix_w, gv, g_mid, q1, h, stats_one, cols, *([chosen] if first else []))
 
     def spread(piece):
         chips = over_chips(piece)
@@ -1109,24 +1282,33 @@
     ff_parts = move_chips(ff_zero)
     gv, near, far = back_conv(0, g_mid, small_ff, ff_zero)
     gv, near, far, all_parts, ff_parts = settle(gv, near, far, all_parts, ff_parts)
-    one_chips = over_chips(added(all_parts))
+    all_one = added(all_parts)
+    one_chips = [all_one] + [wide_shift(all_one, 2 * m) for m in range(1, 4)]
     ff_parts = blocks_at_once(add_chips(ff_parts), me)
     conv_zero = reduce_core(near, far)
     g_top, near, far = back_in(0, gv, g_mid, ())
-    g_top, near, far, one_chips, ff_parts, conv_zero = settle(g_top, near, far, one_chips, ff_parts, conv_zero)
+    ff_zero = added(ff_parts)
+    g_top, near, far, one_chips, ff_zero, conv_zero = settle(g_top, near, far, one_chips, ff_zero, conv_zero)
 
     token_grads = to_blocks(g_top)
     in_zero = reduce_core(near, far)
+    in_zero, conv_zero, one_chips = settle(in_zero, conv_zero, one_chips)
+    mix_parts = move_chips(join_rows(conv_zero, in_zero))
+    one_chips = jnp.stack(one_chips)
     one_group = (one_chips, wide_shift(one_chips, 1))
-    in_zero, one_group, ff_zero = settle(in_zero, one_group, added(ff_parts))
-    mix_parts = move_chips(join_rows(conv_zero, in_zero))
-    flat = finish(1, one_group, [])
-    flat, mix_parts = settle(flat, mix_parts)
-    zero_chips = over_chips(jnp.concatenate([ff_zero, reduce_blocks(add_chips(mix_parts))], axis=0))
-    zero_chips, token_grads = settle(zero_chips, token_grads)
-    zero_group = (zero_chips, wide_shift(zero_chips, 1))
+    *flat, table_one = finish(1, (("ff", "conv", "in"),), (one_group,), [])
+    ff_chips = over_chips(after(ff_zero, table_one))
+    mix_parts, flat, ff_chips = settle(mix_parts, flat, ff_chips)
+    mix_zero = reduce_blocks(add_chips(mix_parts))
+    ff_group = (ff_chips, wide_shift(ff_chips, 1))
     grad_tokens = collect(token_grads, F32)
-    flat = finish(0, zero_group, flat)
+    mix_zero, ff_group, grad_tokens = settle(mix_zero, ff_group, grad_tokens)
+    flat_ff = finish(0, (("ff",),), (ff_group,), flat[:4])
+    mix_chips = over_chips(mix_zero)
+    mix_chips, flat_ff = settle(mix_chips, flat_ff)
+    mix_group = (mix_chips, wide_shift(mix_chips, 1))
+    flat_mix = finish(0, (("conv", "in"),), (mix_group,), [*flat[4:], table_one])
+    flat = [*flat_mix[:4], *flat_ff, *flat_mix[4:]]
     grads = [table.reshape(LAYERS, 1, table.shape[1] * 128) for table in flat[:8]]
     three, g_gain_one, g_gain_two, g_skip, g_taps, g_decay, g_mask, g_one, g_bias, g_two = flat[8:]
     return (
@@ -1136,10 +1318,10 @@
         g_gain_one,
         grads[0],
         grads[1],
-        g_taps[:, :, None],
+        g_taps,
         g_skip,
         g_decay,
-        g_one,
+        g_one.transpose(1, 0, 2),
         g_bias,
         g_two,
         three,

time: 445 us -> 408 us (0.917)
  Pallas kernels: 228 us -> 188 us
  waiting for transfers between devices: 65.7 us -> 76.4 us
  starting transfers between devices: 94.7 us -> 88.6 us
    pallas_call x16 -> x17, Pallas kernels: 228 us -> 188 us  [the longest x14 176 us: run(): pl.pallas_call(body, out_shape=outs, in_specs=[ANY if spec is EARLY else...]
    ppermute x15 -> x9, waiting for transfers between devices: 31.9 us -> 9.35 us  [narrow_shift(): lax.ppermute(x, 'narrow', [(i, (i + by) % narrow) for i in range(narrow)])]
    ppermute x42 -> x46, waiting for transfers between devices: 32.1 us -> 52.4 us  [wide_shift(): lax.ppermute(x, 'wide', [(i, i ^ mask) for i in range(lax.axis_size('wide...]
    ppermute x15 -> x9, starting transfers between devices: 26.4 us -> 18.4 us  [narrow_shift(): lax.ppermute(x, 'narrow', [(i, (i + by) % narrow) for i in range(narrow)])]
    all_to_all x2, waiting for transfers between devices: 0.01 us -> 4.9 us  [blocks_at_once(): lax.all_to_all(table, 'narrow', split_axis=0, concat_axis=0, tiled=True)]
    unnamed x113 -> x139, local copies, waits for them, and re-layouts: 15.7 us -> 11.5 us
    ppermute x42 -> x46, starting transfers between devices: 37.3 us -> 40.7 us  [wide_shift(): lax.ppermute(x, 'wide', [(i, i ^ mask) for i in range(lax.axis_size('wide...]
    all_to_all x2 -> x3, starting transfers between devices: 13.5 us -> 13.8 us  [others_at_once(): lax.all_to_all(pieces, 'narrow', split_axis=0, concat_axis=0, tiled=True)]
  transfers between devices with their start and end apart: 63 -> 62, of which waited for: 16 -> 29; matrix products, arithmetic and copies ran while one was open for 6% -> 6% of each run, Pallas kernels for 50% -> 43%
where the time goes in v3:
time: 408 us; the launch traced here: 401 us
  Pallas kernels  188 us (46%)
  starting transfers between devices  88.6 us (22%)
  waiting for transfers between devices  76.4 us (19%)
  local copies, waits for them, and re-layouts  23 us (6%)
  other arithmetic  19 us (5%)
    pallas_call x14, Pallas kernels, run(): pl.pallas_call(body, out_shape=outs, in_specs=[ANY if spec is EARLY else...  176 us
    ppermute x46, waiting for transfers between devices, wide_shift(): lax.ppermute(x, 'wide', [(i, i ^ mask) for i in range(lax.axis_size('wide...  52.4 us
    ppermute x46, starting transfers between devices, wide_shift(): lax.ppermute(x, 'wide', [(i, i ^ mask) for i in range(lax.axis_size('wide...  40.7 us
    ppermute x9, starting transfers between devices, narrow_shift(): lax.ppermute(x, 'narrow', [(i, (i + by) % narrow) for i in range(narrow)])  18.4 us
    all_to_all x3, starting transfers between devices, others_at_once(): lax.all_to_all(pieces, 'narrow', split_axis=0, concat_axis=0, tiled=True)  13.8 us
    pallas_call x3, Pallas kernels, finish(): pl.pallas_call(functools.partial(finish_kernel, layer, names), grid=(1,),...  12.3 us
    unnamed x139, local copies, waits for them, and re-layouts  11.5 us
    ppermute x9, waiting for transfers between devices, narrow_shift(): lax.ppermute(x, 'narrow', [(i, (i + by) % narrow) for i in range(narrow)])  9.35 us
  transfers between devices with their start and end apart: 62, of which 29 were waited for; matrix products, arithmetic and copies ran while one was open for 6% of the time, Pallas kernels for 43%

profile of v3, /device:TPU:0, one launch (start us, length us, event | category | flops | bytes accessed | tf_op | source)
XLA Modules:
  0.0 400.5 jit_solution(14428744789973043025)
XLA Ops:
  45.3 3.9 collective-permute-start.5
  51.7 6.5 %collective-permute-done.3 = bf16[3,128,384]{2,1,0:T(8,128)(2,1)S(1)} collective-permute-done((bf16[3,128,384]{2,1,0:T(8,128)(2,1)S(1)}, bf16[3,128,384]{2,1,0:T(8,128)(2,1)S(1)}, u32[]{:S(2)}, u32[]{:S(2)}) %collective-permute-start.3) | collective-permute-done | bytes 294944 | tf_op jit(solution)/shard_map/ppermute | solution.py:868
  67.4 6.8 %all-to-all-start.2 = ((bf16[4,304,384]{2,1,0:T(8,128)(2,1)}), bf16[4,304,384]{2,1,0:T(8,128)(2,1)S(1)}, u32[]{:S(2)}, u32[]{:S(2)}) async-start(bf16[4,304,384]{2,1,0:T(8,128)(2,1)} %stack.241), calls=%async_computation.2 | async-start | bytes 1867776 | tf_op jit(solution)/shard_map/all_to_all | solution.py:897
  74.2 17.9 %shard_map.412 = (f32[768,768]{1,0:T(8,128)}, bf16[4,384,768]{2,1,0:T(8,128)(2,1)}, bf16[4,384,768]{2,1,0:T(8,128)(2,1)}, bf16[768,768]{1,0:T(8,128)(2,1)}, bf16...) custom-call(s32[2]{0:T(128)} %pad_add_fusion.refs_0_.idx, ...), custom_call_target="tpu_custom_call" | custom-call | flops 17999998976 | bytes 1048576 | tf_op jit(solution)/shard_map/pallas_call | solution.py:847
  105.8 4.2 %collective-permute-start.15 = (bf16[192,768]{1,0:T(8,128)(2,1)S(1)}, bf16[192,768]{1,0:T(8,128)(2,1)S(1)}, u32[]{:S(2)}, u32[]{:S(2)}) collective-permute-start(bf16[192,768]{1,0:T(8,128)(2,1)S(1)} %copy-done.45), channel_id=1, source_target_pairs={{0,3},{1,0},{2,1},{3,2},{4,7},{5,4},{6,5},{7,6},{8,11},{9,8},{10,9... | collective-permute-start | bytes 884744 | tf_op jit(solution)/shard_map/ppermute | solution.py:873
  110.0 13.1 %shard_map.413 = (bf16[4,192,768]{2,1,0:T(8,128)(2,1)}, bf16[4,1536,768]{2,1,0:T(8,128)(2,1)}, bf16[4,192,768]{2,1,0:T(8,128)(2,1)}, f32[768,768]{1,0:T(8,128)},...) custom-call(s32[2]{0:T(128)} %pad_add_fusion.refs_0_.idx, bf16[1408,384]{1,0:T(8,128)(2,1)} %get-tuple-element.318.refs_1_, ...), custom_call_target="tpu_custom_call" | custom-call | flops 15000000512 | bytes 1048576 | tf_op jit(solution)/shard_map/pallas_call | solution.py:847
  129.8 14.5 %shard_map.414 = (bf16[4,384,768]{2,1,0:T(8,128)(2,1)}, bf16[4,384,768]{2,1,0:T(8,128)(2,1)}, bf16[768,768]{1,0:T(8,128)(2,1)}, bf16[768,768]{1,0:T(8,128)(2,1)}...) custom-call(s32[2]{0:T(128)} %pad_add_fusion.refs_0_.idx, ...), custom_call_target="tpu_custom_call" | custom-call | flops 17999998976 | bytes 1048576 | tf_op jit(solution)/shard_map/pallas_call | solution.py:847
  152.4 12.7 %shard_map.415 = (bf16[4,192,768]{2,1,0:T(8,128)(2,1)}, bf16[4,1536,768]{2,1,0:T(8,128)(2,1)}, bf16[4,192,768]{2,1,0:T(8,128)(2,1)}, bf16[4,192,768]{2,1,0:T(8,1...) custom-call(s32[2]{0:T(128)} %pad_add_fusion.refs_0_.idx, bf16[1408,384]{1,0:T(8,128)(2,1)} %get-tuple-element.347.refs_1_, ...), custom_call_target="tpu_custom_call" | custom-call | flops 15000000512 | bytes 1048576 | tf_op jit(solution)/shard_map/pallas_call | solution.py:847
  165.1 3.8 all-to-all-start.3
  168.9 23.1 %shard_map.416 = (f32[768,768]{1,0:T(8,128)}, bf16[4,4,176,384]{3,2,1,0:T(8,128)(2,1)}, bf16[4,4,176,384]{3,2,1,0:T(8,128)(2,1)}, f32[4,16,192]{2,1,0:T(8,128)}) custom-call(s32[2]{0:T(128)} %pad_add_fusion.refs_0_.idx, bf16[4,1408,384]{2,1,0:T(8,128)(2,1)} %get-tuple-element.352.refs_1_, bf16[192,768]{1,0:T(8,128)(2,1)} %get-tuple-element.358.refs_2_, ...), custom_call_target="tpu_custom_call" | custom-call | flops 27000000512 | bytes 1048576 | tf_op jit(solution)/shard_map/pallas_call | solution.py:847
  192.0 5.8 %all-to-all-done.3.refs_0_ = bf16[4,192,768]{2,1,0:T(8,128)(2,1)S(1)} async-done(((bf16[4,192,768]{2,1,0:T(8,128)(2,1)}), bf16[4,192,768]{2,1,0:T(8,128)(2,1)S(1)}, u32[]{:S(2)}, u32[]{:S(2)}) %all-to-all-start.3) | async-done | bytes 1179680 | tf_op jit(solution)/shard_map/all_to_all | solution.py:1173
  201.1 18.6 %shard_map.418 = (bf16[4,384,768]{2,1,0:T(8,128)(2,1)}, bf16[4,4,48,384]{3,2,1,0:T(8,128)(2,1)}, bf16[4,4,48,384]{3,2,1,0:T(8,128)(2,1)}) custom-call(s32[2]{0:T(128)} %pad_add_fusion.refs_0_.idx, bf16[4,1024,384]{2,1,0:T(8,128)(2,1)} %get-tuple-element.373.refs_1_, f32[768,768]{1,0:T(8,128)} %get-tuple-element.374.refs_2_.refs_3_, ...), custom_call_target="tpu_custom_call" | custom-call | flops 23000000512 | bytes 1048576 | tf_op jit(solution)/shard_map/pallas_call | solution.py:847
  223.6 11.3 %shard_map.419 = (f32[768,768]{1,0:T(8,128)}, bf16[4,4,80,384]{3,2,1,0:T(8,128)(2,1)}, bf16[4,4,80,384]{3,2,1,0:T(8,128)(2,1)}) custom-call(s32[2]{0:T(128)} %pad_add_fusion.refs_0_.idx, bf16[4,1024,384]{2,1,0:T(8,128)(2,1)} %get-tuple-element.373.refs_1_, bf16[4,384,768]{2,1,0:T(8,128)(2,1)} %get-tuple-element.386.refs_2_, ...), custom_call_target="tpu_custom_call" | custom-call | flops 12000000000 | bytes 1048576 | tf_op jit(solution)/shard_map/pallas_call | solution.py:847
  243.5 22.9 %shard_map.420 = (f32[768,768]{1,0:T(8,128)}, bf16[4,4,176,384]{3,2,1,0:T(8,128)(2,1)}, bf16[4,4,176,384]{3,2,1,0:T(8,128)(2,1)}, f32[4,16,192]{2,1,0:T(8,128)}) custom-call(s32[2]{0:T(128)} %pad_add_fusion.refs_0_.idx, bf16[4,1408,384]{2,1,0:T(8,128)(2,1)} %get-tuple-element.372.refs_1_, f32[768,768]{1,0:T(8,128)} %get-tuple-element.409.refs_2_, ...), custom_call_target="tpu_custom_call" | custom-call | flops 27000000512 | bytes 1048576 | tf_op jit(solution)/shard_map/pallas_call | solution.py:847
  284.6 18.5 %shard_map.421 = (bf16[4,384,768]{2,1,0:T(8,128)(2,1)}, bf16[4,4,48,384]{3,2,1,0:T(8,128)(2,1)}, bf16[4,4,48,384]{3,2,1,0:T(8,128)(2,1)}) custom-call(s32[2]{0:T(128)} %pad_add_fusion.refs_0_.idx, bf16[4,1024,384]{2,1,0:T(8,128)(2,1)} %get-tuple-element.371.refs_1_, f32[768,768]{1,0:T(8,128)} %get-tuple-element.425.refs_2_.refs_3_, ...), custom_call_target="tpu_custom_call" | custom-call | flops 23000000512 | bytes 1048576 | tf_op jit(solution)/shard_map/pallas_call | solution.py:847
  314.7 4.7 %all-to-all-start.5 = ((bf16[4,176,384]{2,1,0:T(8,128)(2,1)}), bf16[4,176,384]{2,1,0:T(8,128)(2,1)S(1)}, u32[]{:S(2)}, u32[]{:S(2)}) async-start(bf16[4,176,384]{2,1,0:T(8,128)(2,1)} %pad_maximum_fusion.9), calls=%async_computation.5 | async-start | bytes 1081344 | tf_op jit(solution)/shard_map/all_to_all | solution.py:929
  319.4 11.4 %shard_map.422 = (bf16[4,192,768]{2,1,0:T(8,128)(2,1)}, bf16[4,4,80,384]{3,2,1,0:T(8,128)(2,1)}, bf16[4,4,80,384]{3,2,1,0:T(8,128)(2,1)}) custom-call(s32[2]{0:T(128)} %pad_add_fusion.refs_0_.idx, bf16[4,1024,384]{2,1,0:T(8,128)(2,1)} %get-tuple-element.371.refs_1_, bf16[4,384,768]{2,1,0:T(8,128)(2,1)} %get-tuple-element.453.refs_2_, ...), custom_call_target="tpu_custom_call" | custom-call | flops 12000000000 | bytes 1048576 | tf_op jit(solution)/shard_map/pallas_call | solution.py:847
  340.8 3.7 all-to-all-start.6
  347.1 4.7 %shard_map.423 = (f32[2,288,128]{2,1,0:T(8,128)}, f32[2,2304,128]{2,1,0:T(8,128)}, f32[2,1152,128]{2,1,0:T(8,128)}, f32[2,288,128]{2,1,0:T(8,128)}, f32[2,576,12...) custom-call(s32[2]{0:T(128)} %pad_add_fusion.refs_0_.idx, ...), custom_call_target="tpu_custom_call" | custom-call | flops 4000000000 | bytes 1048576 | tf_op jit(solution)/shard_map/pallas_call | solution.py:1151
  355.5 4.4 %collective-permute-done.44 = bf16[176,384]{1,0:T(8,128)(2,1)S(1)} collective-permute-done((bf16[176,384]{1,0:T(8,128)(2,1)S(1)}, bf16[176,384]{1,0:T(8,128)(2,1)S(1)}, u32[]{:S(2)}, u32[]{:S(2)}) %collective-permute-start.44) | collective-permute-done | bytes 135200 | tf_op jit(solution)/shard_map/ppermute | solution.py:868
  361.3 7.5 %collective-permute-done.45 = bf16[176,384]{1,0:T(8,128)(2,1)S(1)} collective-permute-done((bf16[176,384]{1,0:T(8,128)(2,1)S(1)}, bf16[176,384]{1,0:T(8,128)(2,1)S(1)}, u32[]{:S(2)}, u32[]{:S(2)}) %collective-permute-start.45) | collective-permute-done | bytes 135200 | tf_op jit(solution)/shard_map/ppermute | solution.py:868
  380.1 4.9 %collective-permute-done.48 = bf16[128,384]{1,0:T(8,128)(2,1)S(1)} collective-permute-done((bf16[128,384]{1,0:T(8,128)(2,1)S(1)}, bf16[128,384]{1,0:T(8,128)(2,1)S(1)}, u32[]{:S(2)}, u32[]{:S(2)}) %collective-permute-start.48) | collective-permute-done | bytes 98336 | tf_op jit(solution)/shard_map/ppermute | solution.py:873
  389.6 3.9 shard_map.425
  396.4 3.7 shard_map.426
  (326 shorter events, 165.9 us)
Async XLA Ops:
  2.8 25.7 %collective-permute-start = (bf16[192,768]{1,0:T(8,128)(2,1)S(1)}, bf16[192,768]{1,0:T(8,128)(2,1)}, u32[]{:S(2)}, u32[]{:S(2)}) collective-permute-start(bf16[192,768]{1,0:T(8,128)(2,1)S(1)} %get-tuple-element.631), channel_id=1, source_target_pairs={{0,1},{1,2},{2,3},{3,0},{4,5},{5,6},{6,7},{7,4},{8,9},{9,10},{10,1... | collective-permute-start | bytes 884744 | tf_op jit(solution)/shard_map/ppermute | solution.py:873
  5.9 26.1 %collective-permute-start.1 = (bf16[192,768]{1,0:T(8,128)(2,1)S(1)}, bf16[192,768]{1,0:T(8,128)(2,1)}, u32[]{:S(2)}, u32[]{:S(2)}) collective-permute-start(bf16[192,768]{1,0:T(8,128)(2,1)S(1)} %get-tuple-element.630), channel_id=1, source_target_pairs={{0,2},{1,3},{2,0},{3,1},{4,6},{5,7},{6,4},{7,5},{8,10},{9,11},{10,... | collective-permute-start | bytes 884744 | tf_op jit(solution)/shard_map/ppermute | solution.py:873
  63.5 28.7 %collective-permute-start.7 = (bf16[3,176,384]{2,1,0:T(8,128)(2,1)S(1)}, bf16[3,176,384]{2,1,0:T(8,128)(2,1)S(1)}, u32[]{:S(2)}, u32[]{:S(2)}) collective-permute-start(bf16[3,176,384]{2,1,0:T(8,128)(2,1)S(1)} %pad_maximum_fusion.13), channel_id=1, source_target_pairs={{0,8},{4,12},{8,0},{12,4},{16,24},{20,28},{24,16},{28,20},{1,9},{5... | collective-permute-start | bytes 1216520 | tf_op jit(solution)/shard_map/ppermute | solution.py:868
  65.0 27.2 %collective-permute-start.8 = (bf16[3,176,384]{2,1,0:T(8,128)(2,1)S(1)}, bf16[3,176,384]{2,1,0:T(8,128)(2,1)}, u32[]{:S(2)}, u32[]{:S(2)}) collective-permute-start(bf16[3,176,384]{2,1,0:T(8,128)(2,1)S(1)} %pad_maximum_fusion.13), channel_id=1, source_target_pairs={{0,16},{4,20},{8,24},{12,28},{16,0},{20,4},{24,8},{28,12},{1,17},{... | collective-permute-start | bytes 1216520 | tf_op jit(solution)/shard_map/ppermute | solution.py:868
  66.5 25.7 %collective-permute-start.9 = (bf16[3,176,384]{2,1,0:T(8,128)(2,1)S(1)}, bf16[3,176,384]{2,1,0:T(8,128)(2,1)}, u32[]{:S(2)}, u32[]{:S(2)}) collective-permute-start(bf16[3,176,384]{2,1,0:T(8,128)(2,1)S(1)} %pad_maximum_fusion.13), channel_id=1, source_target_pairs={{0,24},{4,28},{8,16},{12,20},{16,8},{20,12},{24,0},{28,4},{1,25},{... | collective-permute-start | bytes 1216520 | tf_op jit(solution)/shard_map/ppermute | solution.py:868
  67.4 29.8 %all-to-all-start.2 = ((bf16[4,304,384]{2,1,0:T(8,128)(2,1)}), bf16[4,304,384]{2,1,0:T(8,128)(2,1)S(1)}, u32[]{:S(2)}, u32[]{:S(2)}) async-start(bf16[4,304,384]{2,1,0:T(8,128)(2,1)} %stack.241), calls=%async_computation.2 | async-start | bytes 1867776 | tf_op jit(solution)/shard_map/all_to_all | solution.py:897
  102.2 20.9 %collective-permute-start.11 = (bf16[3,128,384]{2,1,0:T(8,128)(2,1)S(1)}, bf16[3,128,384]{2,1,0:T(8,128)(2,1)S(1)}, u32[]{:S(2)}, u32[]{:S(2)}) collective-permute-start(bf16[3,128,384]{2,1,0:T(8,128)(2,1)S(1)} %get-tuple-element.645), channel_id=1, source_target_pairs={{0,8},{4,12},{8,0},{12,4},{16,24},{20,28},{24,16},{28,20},{1,9},{5... | collective-permute-start | bytes 884744 | tf_op jit(solution)/shard_map/ppermute | solution.py:868
  165.1 32.6 %all-to-all-start.3 = ((bf16[4,192,768]{2,1,0:T(8,128)(2,1)}), bf16[4,192,768]{2,1,0:T(8,128)(2,1)S(1)}, u32[]{:S(2)}, u32[]{:S(2)}) async-start(bf16[4,192,768]{2,1,0:T(8,128)(2,1)} %get-tuple-element.369), calls=%async_computation.3 | async-start | bytes 2359296 | tf_op jit(solution)/shard_map/all_to_all | solution.py:1173
  197.7 22.0 %collective-permute-start.22 = (bf16[4,4,176,384]{3,2,1,0:T(8,128)(2,1)}, bf16[4,4,176,384]{3,2,1,0:T(8,128)(2,1)S(1)}, u32[]{:S(2)}, u32[]{:S(2)}) collective-permute-start(bf16[4,4,176,384]{3,2,1,0:T(8,128)(2,1)} %get-tuple-element.385), channel_id=1, source_target_pairs={{0,4},{4,0},{8,12},{12,8},{16,20},{20,16},{24,28},{28,24},{1,5},{5... | collective-permute-start | bytes 6488072 | tf_op jit(solution)/shard_map/ppermute | solution.py:868
  236.7 29.7 %collective-permute-start.30 = (bf16[4,176,384]{2,1,0:T(8,128)(2,1)S(1)}, bf16[4,176,384]{2,1,0:T(8,128)(2,1)S(1)}, u32[]{:S(2)}, u32[]{:S(2)}) collective-permute-start(bf16[4,176,384]{2,1,0:T(8,128)(2,1)S(1)} %get-tuple-element.424), channel_id=1, source_target_pairs={{0,24},{4,28},{8,16},{12,20},{16,8},{20,12},{24,0},{28,4},{1,25},{... | collective-permute-start | bytes 1622024 | tf_op jit(solution)/shard_map/ppermute | solution.py:868
  240.0 26.5 %collective-permute-start.27 = (bf16[4,128,384]{2,1,0:T(8,128)(2,1)S(1)}, bf16[4,128,384]{2,1,0:T(8,128)(2,1)S(1)}, u32[]{:S(2)}, u32[]{:S(2)}) collective-permute-start(bf16[4,128,384]{2,1,0:T(8,128)(2,1)S(1)} %pad_maximum_fusion.15), channel_id=1, source_target_pairs={{0,8},{4,12},{8,0},{12,4},{16,24},{20,28},{24,16},{28,20},{1,9},{5... | collective-permute-start | bytes 1179656 | tf_op jit(solution)/shard_map/ppermute | solution.py:868
  241.3 25.2 %collective-permute-start.28 = (bf16[4,128,384]{2,1,0:T(8,128)(2,1)S(1)}, bf16[4,128,384]{2,1,0:T(8,128)(2,1)S(1)}, u32[]{:S(2)}, u32[]{:S(2)}) collective-permute-start(bf16[4,128,384]{2,1,0:T(8,128)(2,1)S(1)} %pad_maximum_fusion.16), channel_id=1, source_target_pairs={{0,16},{4,20},{8,24},{12,28},{16,0},{20,4},{24,8},{28,12},{1,17},{... | collective-permute-start | bytes 1179656 | tf_op jit(solution)/shard_map/ppermute | solution.py:868
  242.3 26.9 %collective-permute-start.29 = (bf16[4,128,384]{2,1,0:T(8,128)(2,1)S(1)}, bf16[4,128,384]{2,1,0:T(8,128)(2,1)S(1)}, u32[]{:S(2)}, u32[]{:S(2)}) collective-permute-start(bf16[4,128,384]{2,1,0:T(8,128)(2,1)S(1)} %pad_maximum_fusion.17), channel_id=1, source_target_pairs={{0,24},{4,28},{8,16},{12,20},{16,8},{20,12},{24,0},{28,4},{1,25},{... | collective-permute-start | bytes 1179656 | tf_op jit(solution)/shard_map/ppermute | solution.py:868
  277.5 27.3 %all-to-all-start.4 = ((bf16[4,304,384]{2,1,0:T(8,128)(2,1)}), bf16[4,304,384]{2,1,0:T(8,128)(2,1)S(1)}, u32[]{:S(2)}, u32[]{:S(2)}) async-start(bf16[4,304,384]{2,1,0:T(8,128)(2,1)} %pad_maximum_fusion.5), calls=%async_computation.4 | async-start | bytes 1867776 | tf_op jit(solution)/shard_map/all_to_all | solution.py:929
  281.0 23.9 %collective-permute-start.32 = (bf16[4,176,384]{2,1,0:T(8,128)(2,1)}, bf16[4,176,384]{2,1,0:T(8,128)(2,1)S(1)}, u32[]{:S(2)}, u32[]{:S(2)}) collective-permute-start(bf16[4,176,384]{2,1,0:T(8,128)(2,1)} %get-tuple-element.443.refs_18_), channel_id=1, source_target_pairs={{0,8},{4,12},{8,0},{12,4},{16,24},{20,28},{24,16},{28,20},{1,9},{5... | collective-permute-start | bytes 1622024 | tf_op jit(solution)/shard_map/ppermute | solution.py:868
  282.3 24.5 %collective-permute-start.33 = (bf16[4,176,384]{2,1,0:T(8,128)(2,1)}, bf16[4,176,384]{2,1,0:T(8,128)(2,1)S(1)}, u32[]{:S(2)}, u32[]{:S(2)}) collective-permute-start(bf16[4,176,384]{2,1,0:T(8,128)(2,1)} %get-tuple-element.444.refs_19_), channel_id=1, source_target_pairs={{0,16},{4,20},{8,24},{12,28},{16,0},{20,4},{24,8},{28,12},{1,17},{... | collective-permute-start | bytes 1622024 | tf_op jit(solution)/shard_map/ppermute | solution.py:868
  283.4 24.9 %collective-permute-start.34 = (bf16[4,176,384]{2,1,0:T(8,128)(2,1)}, bf16[4,176,384]{2,1,0:T(8,128)(2,1)}, u32[]{:S(2)}, u32[]{:S(2)}) collective-permute-start(bf16[4,176,384]{2,1,0:T(8,128)(2,1)} %get-tuple-element.445.refs_20_), channel_id=1, source_target_pairs={{0,24},{4,28},{8,16},{12,20},{16,8},{20,12},{24,0},{28,4},{1,25},{... | collective-permute-start | bytes 1622024 | tf_op jit(solution)/shard_map/ppermute | solution.py:868
  308.4 27.2 %collective-permute-start.35 = (bf16[304,384]{1,0:T(8,128)(2,1)S(1)}, bf16[304,384]{1,0:T(8,128)(2,1)S(1)}, u32[]{:S(2)}, u32[]{:S(2)}) collective-permute-start(bf16[304,384]{1,0:T(8,128)(2,1)S(1)} %add_convert_fusion.16), channel_id=1, source_target_pairs={{0,8},{4,12},{8,0},{12,4},{16,24},{20,28},{24,16},{28,20},{1,9},{5... | collective-permute-start | bytes 700424 | tf_op jit(solution)/shard_map/ppermute | solution.py:868
  309.3 26.3 %collective-permute-start.36 = (bf16[304,384]{1,0:T(8,128)(2,1)S(1)}, bf16[304,384]{1,0:T(8,128)(2,1)}, u32[]{:S(2)}, u32[]{:S(2)}) collective-permute-start(bf16[304,384]{1,0:T(8,128)(2,1)S(1)} %add_convert_fusion.16), channel_id=1, source_target_pairs={{0,16},{4,20},{8,24},{12,28},{16,0},{20,4},{24,8},{28,12},{1,17},{... | collective-permute-start | bytes 700424 | tf_op jit(solution)/shard_map/ppermute | solution.py:868
  310.7 24.9 %collective-permute-start.37 = (bf16[304,384]{1,0:T(8,128)(2,1)S(1)}, bf16[304,384]{1,0:T(8,128)(2,1)}, u32[]{:S(2)}, u32[]{:S(2)}) collective-permute-start(bf16[304,384]{1,0:T(8,128)(2,1)S(1)} %add_convert_fusion.16), channel_id=1, source_target_pairs={{0,24},{4,28},{8,16},{12,20},{16,8},{20,12},{24,0},{28,4},{1,25},{... | collective-permute-start | bytes 700424 | tf_op jit(solution)/shard_map/ppermute | solution.py:868
  314.7 20.2 %all-to-all-start.5 = ((bf16[4,176,384]{2,1,0:T(8,128)(2,1)}), bf16[4,176,384]{2,1,0:T(8,128)(2,1)S(1)}, u32[]{:S(2)}, u32[]{:S(2)}) async-start(bf16[4,176,384]{2,1,0:T(8,128)(2,1)} %pad_maximum_fusion.9), calls=%async_computation.5 | async-start | bytes 1081344 | tf_op jit(solution)/shard_map/all_to_all | solution.py:929
  340.8 35.4 %all-to-all-start.6 = ((bf16[4,192,768]{2,1,0:T(8,128)(2,1)}), bf16[4,192,768]{2,1,0:T(8,128)(2,1)S(1)}, u32[]{:S(2)}, u32[]{:S(2)}) async-start(bf16[4,192,768]{2,1,0:T(8,128)(2,1)} %get-tuple-element.509), calls=%async_computation.6 | async-start | bytes 2359296 | tf_op jit(solution)/shard_map/all_to_all | solution.py:1173
  344.6 26.7 %collective-permute-start.42 = (bf16[4,128,384]{2,1,0:T(8,128)(2,1)S(1)}, bf16[4,128,384]{2,1,0:T(8,128)(2,1)S(1)}, u32[]{:S(2)}, u32[]{:S(2)}) collective-permute-start(bf16[4,128,384]{2,1,0:T(8,128)(2,1)S(1)} %pad_maximum_fusion.21), channel_id=1, source_target_pairs={{0,24},{4,28},{8,16},{12,20},{16,8},{20,12},{24,0},{28,4},{1,25},{... | collective-permute-start | bytes 1179656 | tf_op jit(solution)/shard_map/ppermute | solution.py:868
  346.4 24.9 %collective-permute-start.41 = (bf16[4,128,384]{2,1,0:T(8,128)(2,1)S(1)}, bf16[4,128,384]{2,1,0:T(8,128)(2,1)S(1)}, u32[]{:S(2)}, u32[]{:S(2)}) collective-permute-start(bf16[4,128,384]{2,1,0:T(8,128)(2,1)S(1)} %pad_maximum_fusion.20), channel_id=1, source_target_pairs={{0,16},{4,20},{8,24},{12,28},{16,0},{20,4},{24,8},{28,12},{1,17},{... | collective-permute-start | bytes 1179656 | tf_op jit(solution)/shard_map/ppermute | solution.py:868
  (105 other events, 798.5 us)

commit v4 on v3

--- a/solution.py
+++ b/solution.py
@@ -90,6 +90,8 @@
         h_ref, *refs = refs
     q1, proj, conv, gated, q2, middle, stats, cols, kspec, table, normed, xs, gs, sem = refs
     at = distances(idx)
+    if not first:
+        h_ref.start()
     fetched = fetch_table(idx, own, rel_a, rel_b, table.buffer, sem)
     w = table.buffer
     if first:
@@ -101,6 +103,8 @@
             h_ref.buffer[rows, :] = part[...].astype(F32) * (1.0 - keep) + keep * column(cols, rows, MASK, seqs * LENGTH)
         h_ref.start()
         h_ref = h_ref.buffer
+    else:
+        h_ref = h_ref.wait()
     mean, inv = norm_rows([block(h_ref, b) for b in range(BLOCKS)])
     if not first:
         fetched()
@@ -157,10 +161,12 @@
     for b in range(BLOCKS):
         inner = tn(w[at[b], OUT_ROWS : OUT_ROWS + 192, 0:192], block(gated.buffer, b)).astype(BF16)
         for c in range(BLOCKS):
-            q2[c, 48 * b : 48 * b + 48, :] = inner[48 * c : 48 * c + 48]
+            q2.buffer[c, 48 * b : 48 * b + 48, :] = inner[48 * c : 48 * c + 48]
+    q2.start()
     for c in range(BLOCKS):
         rows = pl.ds(c * BLOCK_W, BLOCK_W)
-        middle[rows, :] = h_ref[rows, :] + tn(w[at[c], OUT_ROWS : OUT_ROWS + 192, 192:384], q2[c])
+        middle.buffer[rows, :] = h_ref[rows, :] + tn(w[at[c], OUT_ROWS : OUT_ROWS + 192, 192:384], q2.buffer[c])
+        middle.start((rows, slice(None)))
 
 
 def gelu_parts(v):
@@ -170,8 +176,11 @@
 
 def fwd_ff_kernel(last, idx, own, rel_a, rel_b, middle, cols, q3, gate_up, q4, h_next, stats, table, normed, act, sem):
     at = distances(idx)
+    middle.start()
+    cols.start()
     fetched = fetch_table(idx, own, rel_a, rel_b, table.buffer, sem)
     w = table.buffer
+    middle, cols = middle.wait(), cols.wait()
     mean, inv = norm_rows([block(middle, b) for b in range(BLOCKS)])
     stats[0:1, :] = mean
     stats[1:2, :] = inv
@@ -202,14 +211,17 @@
             + tn(w[at[c], DOWN_ONE : DOWN_ONE + 384, 192:384], act[384:768, :])
         ).astype(BF16)
         for to in range(BLOCKS):
-            q4[to, 48 * c : 48 * c + 48, :] = inner[48 * to : 48 * to + 48]
+            q4.buffer[to, 48 * c : 48 * c + 48, :] = inner[48 * to : 48 * to + 48]
+    q4.start()
     for c in range(BLOCKS):
         rows = pl.ds(c * BLOCK_W, BLOCK_W)
-        value = middle[rows, :] + tn(w[at[c], UP_ONE : UP_ONE + 192, 192:384], q4[c])
+        value = middle[rows, :] + tn(w[at[c], UP_ONE : UP_ONE + 192, 192:384], q4.buffer[c])
         if last:
-            h_next[c] = value.astype(BF16)
+            h_next.buffer[c] = value.astype(BF16)
+            h_next.start(c)
         else:
-            h_next[rows, :] = value
+            h_next.buffer[rows, :] = value
+            h_next.start((rows, slice(None)))
 
 
 def bwd_ff_kernel(last, idx, table, *refs):
@@ -494,8 +506,9 @@
             value = g_h[rows, :]
             masked = value * chosen[0:1, :]
             totals = totals + row_sums(1, masked)
-            g_out.buffer[b] = (value - masked).astype(BF16)
-            g_out.start(b)
+            ahead_by = (b - idx[0]) & (BLOCKS - 1)
+            g_out.buffer[ahead_by] = (value - masked).astype(BF16)
+            g_out.start(ahead_by)
         g_w[at[b], 576:592, 0:192] = totals.astype(BF16)
         g_w[at[b], 576:592, 192:384] = jnp.zeros((16, 192), BF16)
         g_w[at[b], 592:640, :] = jnp.zeros((48, 384), BF16)
@@ -858,6 +871,13 @@
     return run
 
 
+def place_distances_kernel(idx, *refs):
+    parts, out = refs[:BLOCKS], refs[BLOCKS]
+    span = parts[0].shape[1]
+    for k, part in enumerate(parts):
+        out[:, pl.ds(pl.multiple_of(block_of(idx, k) * span, 128), span)] = part[...].astype(out.dtype)
+
+
 def place_parts_kernel(table, out):
     span = table.shape[2]
     for b in range(BLOCKS):
@@ -923,9 +943,12 @@
     return added([total[0]] + [narrow_shift(total[k], -k) for k in range(1, BLOCKS)])
 
 
-def blocks_at_once(total, me):
+def in_order(total, me):
     table = jnp.stack(total)
-    table = jnp.stack([lax.dynamic_index_in_dim(table, (me - b) % BLOCKS, 0, keepdims=False) for b in range(BLOCKS)])
+    return jnp.stack([lax.dynamic_index_in_dim(table, (me - b) % BLOCKS, 0, keepdims=False) for b in range(BLOCKS)])
+
+
+def blocks_at_once(table):
     moved = lax.all_to_all(table, "narrow", split_axis=0, concat_axis=0, tiled=True)
     return [moved[b] for b in range(BLOCKS)]
 
@@ -1078,8 +1101,8 @@
                 pltpu.VMEM((BLOCK_W, span), F32),
                 fetched,
             ],
-            table_specs + [WHOLE] * (BLOCKS + 1 if first else 1) + [WHOLE] * 5,
-            ([LATE] if first else []) + [LATE] * 4 + [WHOLE] * 5 + [LATE],
+            table_specs + ([WHOLE] * (BLOCKS + 1) if first else [EARLY]) + [WHOLE] * 5,
+            ([LATE] if first else []) + [LATE] * 6 + [WHOLE] * 3 + [LATE],
             18,
             deps,
         )(idx, *table, *([*h, chosen] if first else [h]), pad, hidden[layer], ahead_full, ahead_low, back_low)
@@ -1097,8 +1120,8 @@
                 ff_table,
             ],
             [pltpu.VMEM((D, span), BF16), pltpu.VMEM((FF_BLOCK, span), BF16), fetched],
-            table_specs + [WHOLE] * 2,
-            [LATE] * 2 + [WHOLE] * 3 + [LATE],
+            table_specs + [EARLY] * 2,
+            [LATE] * 4 + [WHOLE] + [LATE],
             15,
             deps,
         )(idx, *table, middle, cols)
@@ -1109,7 +1132,7 @@
     one = others_at_once(one, me)
     h, q1, proj, conv, gated, q2, middle, stats_one, cols, kspec, mix_w = ahead_mix(0, mix_zero, tokens_here)
     parts = token_parts(cotangent)
-    middle, ff_chips, one, parts = settle(middle, ff_chips, one, parts)
+    middle, ff_chips, parts = settle(middle, ff_chips, parts)
     ff_zero = (ff[0], ff_chips, wide_shift(ff_chips, 1))
     middle, ff_zero, one, parts = settle(middle, ff_zero, one, parts)
     rows = MIX_ROWS // 8
@@ -1262,53 +1285,63 @@
     h_last, cotangent_here = settle(h_last, cotangent_here)
     mixed_parts = to_blocks(h_last)
     g_mid, near, far, small_ff = back_ff(1, cotangent_here, ())
-    g_mid, near, far, mixed_parts = settle(g_mid, near, far, mixed_parts)
-    mixed_out = collect(mixed_parts, BF16)
+    g_mid, near, far = settle(g_mid, near, far)
     ff_one = reduce_core(near, far)
-    gv, near, far = back_conv(1, g_mid, small_ff, (mixed_out,))
+    gv, near, far = back_conv(1, g_mid, small_ff, ())
     gv, near, far, ff_one = settle(gv, near, far, ff_one)
     conv_one = reduce_core(near, far)
     ff_parts = [ff_one[0], wide_shift(ff_one[1], 2), wide_shift(ff_one[2], 4)]
     g_top, near, far = back_in(1, gv, g_mid, ())
-    g_top, near, far, conv_one, ff_parts, last = settle(g_top, near, far, conv_one, ff_parts, ff_one[3])
-    near, far = settle(near, reduce_core(near, far))
+    g_top, near, far, conv_one, ff_parts, last, mixed_parts = settle(
+        g_top, near, far, conv_one, ff_parts, ff_one[3], mixed_parts
+    )
+    mixed_out = collect(mixed_parts, BF16)
+    near, far, mixed_out = settle(near, reduce_core(near, far), mixed_out)
     mix_parts, g_top = settle(join_rows(conv_one, far), g_top)
     ff_parts = ff_parts + [wide_shift(last, 6)]
     mix_parts = move_chips(mix_parts)
     g_mid, near, far, small_ff = back_ff(0, g_top, ())
     g_mid, near, far, mix_parts, ff_parts = settle(g_mid, near, far, mix_parts, ff_parts)
-    all_one, ff_zero = settle(join_rows(add_chips(ff_parts), add_chips(mix_parts)), reduce_core(near, far))
-    all_parts = blocks_at_once(all_one, me)
+    all_one = in_order(join_rows(add_chips(ff_parts), add_chips(mix_parts)), me)
+    all_one, ff_zero = settle(all_one, reduce_core(near, far))
+    all_parts = blocks_at_once(all_one)
     ff_parts = move_chips(ff_zero)
     gv, near, far = back_conv(0, g_mid, small_ff, ff_zero)
     gv, near, far, all_parts, ff_parts = settle(gv, near, far, all_parts, ff_parts)
     all_one = added(all_parts)
     one_chips = [all_one] + [wide_shift(all_one, 2 * m) for m in range(1, 4)]
-    ff_parts = blocks_at_once(add_chips(ff_parts), me)
+    ff_parts = blocks_at_once(in_order(add_chips(ff_parts), me))
     conv_zero = reduce_core(near, far)
     g_top, near, far = back_in(0, gv, g_mid, ())
     ff_zero = added(ff_parts)
-    g_top, near, far, one_chips, ff_zero, conv_zero = settle(g_top, near, far, one_chips, ff_zero, conv_zero)
-
-    token_grads = to_blocks(g_top)
-    in_zero = reduce_core(near, far)
-    in_zero, conv_zero, one_chips = settle(in_zero, conv_zero, one_chips)
+    g_top, near, far, one_chips = settle(g_top, near, far, one_chips)
+    token_near, across = narrow_shift(g_top[1], 1), narrow_shift(g_top[2], 2)
+    in_zero, ff_zero, conv_zero, one_chips = settle(reduce_core(near, far), ff_zero, conv_zero, one_chips)
+
     mix_parts = move_chips(join_rows(conv_zero, in_zero))
     one_chips = jnp.stack(one_chips)
     one_group = (one_chips, wide_shift(one_chips, 1))
     *flat, table_one = finish(1, (("ff", "conv", "in"),), (one_group,), [])
-    ff_chips = over_chips(after(ff_zero, table_one))
-    mix_parts, flat, ff_chips = settle(mix_parts, flat, ff_chips)
+    mix_parts, flat, ff_zero, token_near, across = settle(mix_parts, flat, ff_zero, token_near, across)
     mix_zero = reduce_blocks(add_chips(mix_parts))
+    ff_chips = over_chips(ff_zero)
+    mix_zero, ff_chips, token_far = settle(mix_zero, ff_chips, g_top[3])
+    mix_chips = over_chips(mix_zero)
     ff_group = (ff_chips, wide_shift(ff_chips, 1))
-    grad_tokens = collect(token_grads, F32)
-    mix_zero, ff_group, grad_tokens = settle(mix_zero, ff_group, grad_tokens)
+    token_far = narrow_shift(token_far, 3)
     flat_ff = finish(0, (("ff",),), (ff_group,), flat[:4])
-    mix_chips = over_chips(mix_zero)
-    mix_chips, flat_ff = settle(mix_chips, flat_ff)
+    mix_chips, flat_ff, token_far = settle(mix_chips, flat_ff, token_far)
     mix_group = (mix_chips, wide_shift(mix_chips, 1))
     flat_mix = finish(0, (("conv", "in"),), (mix_group,), [*flat[4:], table_one])
     flat = [*flat_mix[:4], *flat_ff, *flat_mix[4:]]
+    grad_tokens = call(
+        place_distances_kernel,
+        shaped(F32, BLOCK_W, BLOCKS * span),
+        [],
+        [SCALARS] + [WHOLE] * BLOCKS,
+        WHOLE,
+        2,
+    )(idx, g_top[0], token_near, across, token_far)
     grads = [table.reshape(LAYERS, 1, table.shape[1] * 128) for table in flat[:8]]
     three, g_gain_one, g_gain_two, g_skip, g_taps, g_decay, g_mask, g_one, g_bias, g_two = flat[8:]
     return (

time: 408 us -> 390 us (0.956)
  waiting for transfers between devices: 76.4 us -> 54.4 us
  starting transfers between devices: 88.6 us -> 94.4 us
    ppermute x46, waiting for transfers between devices: 52.4 us -> 26.8 us  [wide_shift(): lax.ppermute(x, 'wide', [(i, i ^ mask) for i in range(lax.axis_size('wide...]
    ppermute x9 -> x12, waiting for transfers between devices: 9.35 us -> 19.6 us  [narrow_shift(): lax.ppermute(x, 'narrow', [(i, (i + by) % narrow) for i in range(narrow)])]
    ppermute x9 -> x12, starting transfers between devices: 18.4 us -> 24.9 us  [narrow_shift(): lax.ppermute(x, 'narrow', [(i, (i + by) % narrow) for i in range(narrow)])]
    all_to_all x2 -> x1, waiting for transfers between devices: 5.76 us -> 0.01 us  [to_blocks(): lax.all_to_all(table, 'narrow', split_axis=0, concat_axis=0, tiled=True)]
    unnamed x139 -> x129, local copies, waits for them, and re-layouts: 11.5 us -> 10.3 us
  transfers between devices with their start and end apart: 62 -> 64, of which waited for: 29 -> 24; matrix products, arithmetic and copies ran while one was open for 6% -> 7% of each run, Pallas kernels for 43% -> 39%
where the time goes in v4:
time: 390 us; the launch traced here: 383 us
  Pallas kernels  189 us (48%)
  starting transfers between devices  94.4 us (24%)
  waiting for transfers between devices  54.4 us (14%)
  local copies, waits for them, and re-layouts  22.5 us (6%)
  other arithmetic  17.6 us (5%)
    pallas_call x14, Pallas kernels, run(): pl.pallas_call(body, out_shape=outs, in_specs=[ANY if spec is EARLY else...  177 us
    ppermute x46, starting transfers between devices, wide_shift(): lax.ppermute(x, 'wide', [(i, i ^ mask) for i in range(lax.axis_size('wide...  41.3 us
    ppermute x46, waiting for transfers between devices, wide_shift(): lax.ppermute(x, 'wide', [(i, i ^ mask) for i in range(lax.axis_size('wide...  26.8 us
    ppermute x12, starting transfers between devices, narrow_shift(): lax.ppermute(x, 'narrow', [(i, (i + by) % narrow) for i in range(narrow)])  24.9 us
    ppermute x12, waiting for transfers between devices, narrow_shift(): lax.ppermute(x, 'narrow', [(i, (i + by) % narrow) for i in range(narrow)])  19.6 us
    all_to_all x3, starting transfers between devices, others_at_once(): lax.all_to_all(pieces, 'narrow', split_axis=0, concat_axis=0, tiled=True)  14.1 us
    pallas_call x3, Pallas kernels, finish(): pl.pallas_call(functools.partial(finish_kernel, layer, names), grid=(1,),...  12.3 us
    unnamed x129, local copies, waits for them, and re-layouts  10.3 us
  transfers between devices with their start and end apart: 64, of which 24 were waited for; matrix products, arithmetic and copies ran while one was open for 7% of the time, Pallas kernels for 39%

profile of v4, /device:TPU:0, one launch (start us, length us, event | category | flops | bytes accessed | tf_op | source)
XLA Modules:
  0.0 382.7 jit_solution(4212281692326446446)
XLA Ops:
  32.0 3.6 shard_map.411
  38.2 3.6 all-to-all-start.1
  45.3 3.9 %collective-permute-start.5 = (bf16[192,768]{1,0:T(8,128)(2,1)S(1)}, bf16[192,768]{1,0:T(8,128)(2,1)}, u32[]{:S(2)}, u32[]{:S(2)}) collective-permute-start(bf16[192,768]{1,0:T(8,128)(2,1)S(1)} %get-tuple-element.284), channel_id=1, source_target_pairs={{0,3},{1,0},{2,1},{3,2},{4,7},{5,4},{6,5},{7,6},{8,11},{9,8},{10,9... | collective-permute-start | bytes 884744 | tf_op jit(solution)/shard_map/ppermute | solution.py:893
  51.7 6.5 %collective-permute-done.3 = bf16[3,128,384]{2,1,0:T(8,128)(2,1)S(1)} collective-permute-done((bf16[3,128,384]{2,1,0:T(8,128)(2,1)S(1)}, bf16[3,128,384]{2,1,0:T(8,128)(2,1)S(1)}, u32[]{:S(2)}, u32[]{:S(2)}) %collective-permute-start.3) | collective-permute-done | bytes 294944 | tf_op jit(solution)/shard_map/ppermute | solution.py:888
  67.4 7.0 %all-to-all-start.2 = ((bf16[4,304,384]{2,1,0:T(8,128)(2,1)}), bf16[4,304,384]{2,1,0:T(8,128)(2,1)S(1)}, u32[]{:S(2)}, u32[]{:S(2)}) async-start(bf16[4,304,384]{2,1,0:T(8,128)(2,1)} %stack.241), calls=%async_computation.2 | async-start | bytes 1867776 | tf_op jit(solution)/shard_map/all_to_all | solution.py:917
  74.5 17.9 %shard_map.412 = (f32[768,768]{1,0:T(8,128)}, bf16[4,384,768]{2,1,0:T(8,128)(2,1)}, bf16[4,384,768]{2,1,0:T(8,128)(2,1)}, bf16[768,768]{1,0:T(8,128)(2,1)}, bf16...) custom-call(s32[2]{0:T(128)} %pad_add_fusion.refs_0_.idx, ...), custom_call_target="tpu_custom_call" | custom-call | flops 17999998976 | bytes 1048576 | tf_op jit(solution)/shard_map/pallas_call | solution.py:860
  93.9 3.6 all-to-all-done.2
  105.3 13.2 %shard_map.413 = (bf16[4,192,768]{2,1,0:T(8,128)(2,1)}, bf16[4,1536,768]{2,1,0:T(8,128)(2,1)}, bf16[4,192,768]{2,1,0:T(8,128)(2,1)}, f32[768,768]{1,0:T(8,128)},...) custom-call(s32[2]{0:T(128)} %pad_add_fusion.refs_0_.idx, bf16[1408,384]{1,0:T(8,128)(2,1)} %get-tuple-element.311.refs_1_, ...), custom_call_target="tpu_custom_call" | custom-call | flops 15000000512 | bytes 1048576 | tf_op jit(solution)/shard_map/pallas_call | solution.py:860
  126.2 14.8 %shard_map.414 = (bf16[4,384,768]{2,1,0:T(8,128)(2,1)}, bf16[4,384,768]{2,1,0:T(8,128)(2,1)}, bf16[768,768]{1,0:T(8,128)(2,1)}, bf16[768,768]{1,0:T(8,128)(2,1)}...) custom-call(s32[2]{0:T(128)} %pad_add_fusion.refs_0_.idx, ...), custom_call_target="tpu_custom_call" | custom-call | flops 17999998976 | bytes 1048576 | tf_op jit(solution)/shard_map/pallas_call | solution.py:860
  147.8 12.8 %shard_map.415 = (bf16[4,192,768]{2,1,0:T(8,128)(2,1)}, bf16[4,1536,768]{2,1,0:T(8,128)(2,1)}, bf16[4,192,768]{2,1,0:T(8,128)(2,1)}, bf16[4,192,768]{2,1,0:T(8,1...) custom-call(s32[2]{0:T(128)} %pad_add_fusion.refs_0_.idx, bf16[1408,384]{1,0:T(8,128)(2,1)} %get-tuple-element.341.refs_1_, ...), custom_call_target="tpu_custom_call" | custom-call | flops 15000000512 | bytes 1048576 | tf_op jit(solution)/shard_map/pallas_call | solution.py:860
  160.6 22.8 %shard_map.416 = (f32[768,768]{1,0:T(8,128)}, bf16[4,4,176,384]{3,2,1,0:T(8,128)(2,1)}, bf16[4,4,176,384]{3,2,1,0:T(8,128)(2,1)}, f32[4,16,192]{2,1,0:T(8,128)}) custom-call(s32[2]{0:T(128)} %pad_add_fusion.refs_0_.idx, bf16[4,1408,384]{2,1,0:T(8,128)(2,1)} %get-tuple-element.346.refs_1_, bf16[192,768]{1,0:T(8,128)(2,1)} %get-tuple-element.352.refs_2_, ...), custom_call_target="tpu_custom_call" | custom-call | flops 27000000512 | bytes 1048576 | tf_op jit(solution)/shard_map/pallas_call | solution.py:860
  184.3 4.3 %all-to-all-start.3 = ((bf16[4,192,768]{2,1,0:T(8,128)(2,1)}), bf16[4,192,768]{2,1,0:T(8,128)(2,1)}, u32[]{:S(2)}, u32[]{:S(2)}) async-start(bf16[4,192,768]{2,1,0:T(8,128)(2,1)} %get-tuple-element.387), calls=%async_computation.3 | async-start | bytes 2359296 | tf_op jit(solution)/shard_map/all_to_all | solution.py:1196
  188.6 18.9 %shard_map.417 = (bf16[4,384,768]{2,1,0:T(8,128)(2,1)}, bf16[4,4,48,384]{3,2,1,0:T(8,128)(2,1)}, bf16[4,4,48,384]{3,2,1,0:T(8,128)(2,1)}) custom-call(s32[2]{0:T(128)} %pad_add_fusion.refs_0_.idx, bf16[4,1024,384]{2,1,0:T(8,128)(2,1)} %get-tuple-element.331.refs_1_, f32[768,768]{1,0:T(8,128)} %get-tuple-element.363.refs_2_.refs_3_, ...), custom_call_target="tpu_custom_call" | custom-call | flops 23000000512 | bytes 1048576 | tf_op jit(solution)/shard_map/pallas_call | solution.py:860
  211.7 11.3 %shard_map.418 = (f32[768,768]{1,0:T(8,128)}, bf16[4,4,80,384]{3,2,1,0:T(8,128)(2,1)}, bf16[4,4,80,384]{3,2,1,0:T(8,128)(2,1)}) custom-call(s32[2]{0:T(128)} %pad_add_fusion.refs_0_.idx, bf16[4,1024,384]{2,1,0:T(8,128)(2,1)} %get-tuple-element.331.refs_1_, bf16[4,384,768]{2,1,0:T(8,128)(2,1)} %get-tuple-element.375.refs_2_, ...), custom_call_target="tpu_custom_call" | custom-call | flops 12000000000 | bytes 1048576 | tf_op jit(solution)/shard_map/pallas_call | solution.py:860
  232.5 23.0 %shard_map.420 = (f32[768,768]{1,0:T(8,128)}, bf16[4,4,176,384]{3,2,1,0:T(8,128)(2,1)}, bf16[4,4,176,384]{3,2,1,0:T(8,128)(2,1)}, f32[4,16,192]{2,1,0:T(8,128)}) custom-call(s32[2]{0:T(128)} %pad_add_fusion.refs_0_.idx, bf16[4,1408,384]{2,1,0:T(8,128)(2,1)} %get-tuple-element.393.refs_1_, f32[768,768]{1,0:T(8,128)} %get-tuple-element.403.refs_2_, ...), custom_call_target="tpu_custom_call" | custom-call | flops 27000000512 | bytes 1048576 | tf_op jit(solution)/shard_map/pallas_call | solution.py:860
  264.2 5.0 %all-to-all-start.4 = ((bf16[4,304,384]{2,1,0:T(8,128)(2,1)}), bf16[4,304,384]{2,1,0:T(8,128)(2,1)S(1)}, u32[]{:S(2)}, u32[]{:S(2)}) async-start(bf16[4,304,384]{2,1,0:T(8,128)(2,1)} %pad_maximum_fusion.5), calls=%async_computation.4 | async-start | bytes 1867776 | tf_op jit(solution)/shard_map/all_to_all | solution.py:952
  272.7 18.4 %shard_map.421 = (bf16[4,384,768]{2,1,0:T(8,128)(2,1)}, bf16[4,4,48,384]{3,2,1,0:T(8,128)(2,1)}, bf16[4,4,48,384]{3,2,1,0:T(8,128)(2,1)}) custom-call(s32[2]{0:T(128)} %pad_add_fusion.refs_0_.idx, bf16[4,1024,384]{2,1,0:T(8,128)(2,1)} %get-tuple-element.392.refs_1_, f32[768,768]{1,0:T(8,128)} %get-tuple-element.419.refs_2_.refs_3_, ...), custom_call_target="tpu_custom_call" | custom-call | flops 23000000512 | bytes 1048576 | tf_op jit(solution)/shard_map/pallas_call | solution.py:860
  302.9 4.8 %all-to-all-start.5 = ((bf16[4,176,384]{2,1,0:T(8,128)(2,1)}), bf16[4,176,384]{2,1,0:T(8,128)(2,1)S(1)}, u32[]{:S(2)}, u32[]{:S(2)}) async-start(bf16[4,176,384]{2,1,0:T(8,128)(2,1)} %pad_maximum_fusion.9), calls=%async_computation.5 | async-start | bytes 1081344 | tf_op jit(solution)/shard_map/all_to_all | solution.py:952
  307.7 11.4 %shard_map.422 = (bf16[4,192,768]{2,1,0:T(8,128)(2,1)}, bf16[4,4,80,384]{3,2,1,0:T(8,128)(2,1)}, bf16[4,4,80,384]{3,2,1,0:T(8,128)(2,1)}) custom-call(s32[2]{0:T(128)} %pad_add_fusion.refs_0_.idx, bf16[4,1024,384]{2,1,0:T(8,128)(2,1)} %get-tuple-element.392.refs_1_, bf16[4,384,768]{2,1,0:T(8,128)(2,1)} %get-tuple-element.444.refs_2_, ...), custom_call_target="tpu_custom_call" | custom-call | flops 12000000000 | bytes 1048576 | tf_op jit(solution)/shard_map/pallas_call | solution.py:860
  333.8 4.7 %shard_map.423 = (f32[2,288,128]{2,1,0:T(8,128)}, f32[2,2304,128]{2,1,0:T(8,128)}, f32[2,1152,128]{2,1,0:T(8,128)}, f32[2,288,128]{2,1,0:T(8,128)}, f32[2,576,12...) custom-call(s32[2]{0:T(128)} %pad_add_fusion.refs_0_.idx, ...), custom_call_target="tpu_custom_call" | custom-call | flops 4000000000 | bytes 1048576 | tf_op jit(solution)/shard_map/pallas_call | solution.py:1174
  338.6 10.8 %collective-permute-done.45.refs_3_ = bf16[192,768]{1,0:T(8,128)(2,1)S(1)} collective-permute-done((bf16[192,768]{1,0:T(8,128)(2,1)S(1)}, bf16[192,768]{1,0:T(8,128)(2,1)S(1)}, u32[]{:S(2)}, u32[]{:S(2)}) %collective-permute-start.45) | collective-permute-done | bytes 294944 | tf_op jit(solution)/shard_map/ppermute | solution.py:893
  365.0 3.6 collective-permute-start.56
  370.5 3.9 %shard_map.424 = (f32[2,288,128]{2,1,0:T(8,128)}, f32[2,2304,128]{2,1,0:T(8,128)}, f32[2,1152,128]{2,1,0:T(8,128)}, f32[2,288,128]{2,1,0:T(8,128)}) custom-call(s32[2]{0:T(128)} %pad_add_fusion.refs_0_.idx, bf16[4,176,384]{2,1,0:T(8,128)(2,1)} %copy-done.22, ...), custom_call_target="tpu_custom_call", output_to_operand_aliasing={{0}: (3, {}), {1}: (4, {}), {2}: (5, {}), {3}: (6, {})} | custom-call | flops 4000000000 | bytes 1048576 | tf_op jit(solution)/shard_map/pallas_call | solution.py:1174
  378.9 3.7 shard_map.426
  (321 shorter events, 147.0 us)
Async XLA Ops:
  2.8 25.7 %collective-permute-start = (bf16[192,768]{1,0:T(8,128)(2,1)S(1)}, bf16[192,768]{1,0:T(8,128)(2,1)}, u32[]{:S(2)}, u32[]{:S(2)}) collective-permute-start(bf16[192,768]{1,0:T(8,128)(2,1)S(1)} %get-tuple-element.623), channel_id=1, source_target_pairs={{0,1},{1,2},{2,3},{3,0},{4,5},{5,6},{6,7},{7,4},{8,9},{9,10},{10,1... | collective-permute-start | bytes 884744 | tf_op jit(solution)/shard_map/ppermute | solution.py:893
  5.9 26.1 %collective-permute-start.1 = (bf16[192,768]{1,0:T(8,128)(2,1)S(1)}, bf16[192,768]{1,0:T(8,128)(2,1)}, u32[]{:S(2)}, u32[]{:S(2)}) collective-permute-start(bf16[192,768]{1,0:T(8,128)(2,1)S(1)} %get-tuple-element.622), channel_id=1, source_target_pairs={{0,2},{1,3},{2,0},{3,1},{4,6},{5,7},{6,4},{7,5},{8,10},{9,11},{10,... | collective-permute-start | bytes 884744 | tf_op jit(solution)/shard_map/ppermute | solution.py:893
  38.2 20.2 %all-to-all-start.1 = ((bf16[4,176,384]{2,1,0:T(8,128)(2,1)}), bf16[4,176,384]{2,1,0:T(8,128)(2,1)S(1)}, u32[]{:S(2)}, u32[]{:S(2)}) async-start(bf16[4,176,384]{2,1,0:T(8,128)(2,1)} %stack.239), calls=%async_computation.1 | async-start | bytes 1081344 | tf_op jit(solution)/shard_map/all_to_all | solution.py:917
  63.5 28.9 %collective-permute-start.7 = (bf16[3,176,384]{2,1,0:T(8,128)(2,1)S(1)}, bf16[3,176,384]{2,1,0:T(8,128)(2,1)S(1)}, u32[]{:S(2)}, u32[]{:S(2)}) collective-permute-start(bf16[3,176,384]{2,1,0:T(8,128)(2,1)S(1)} %pad_maximum_fusion.13), channel_id=1, source_target_pairs={{0,8},{4,12},{8,0},{12,4},{16,24},{20,28},{24,16},{28,20},{1,9},{5... | collective-permute-start | bytes 1216520 | tf_op jit(solution)/shard_map/ppermute | solution.py:888
  65.0 27.4 %collective-permute-start.8 = (bf16[3,176,384]{2,1,0:T(8,128)(2,1)S(1)}, bf16[3,176,384]{2,1,0:T(8,128)(2,1)}, u32[]{:S(2)}, u32[]{:S(2)}) collective-permute-start(bf16[3,176,384]{2,1,0:T(8,128)(2,1)S(1)} %pad_maximum_fusion.13), channel_id=1, source_target_pairs={{0,16},{4,20},{8,24},{12,28},{16,0},{20,4},{24,8},{28,12},{1,17},{... | collective-permute-start | bytes 1216520 | tf_op jit(solution)/shard_map/ppermute | solution.py:888
  66.5 25.9 %collective-permute-start.9 = (bf16[3,176,384]{2,1,0:T(8,128)(2,1)S(1)}, bf16[3,176,384]{2,1,0:T(8,128)(2,1)}, u32[]{:S(2)}, u32[]{:S(2)}) collective-permute-start(bf16[3,176,384]{2,1,0:T(8,128)(2,1)S(1)} %pad_maximum_fusion.13), channel_id=1, source_target_pairs={{0,24},{4,28},{8,16},{12,20},{16,8},{20,12},{24,0},{28,4},{1,25},{... | collective-permute-start | bytes 1216520 | tf_op jit(solution)/shard_map/ppermute | solution.py:888
  67.4 30.0 %all-to-all-start.2 = ((bf16[4,304,384]{2,1,0:T(8,128)(2,1)}), bf16[4,304,384]{2,1,0:T(8,128)(2,1)S(1)}, u32[]{:S(2)}, u32[]{:S(2)}) async-start(bf16[4,304,384]{2,1,0:T(8,128)(2,1)} %stack.241), calls=%async_computation.2 | async-start | bytes 1867776 | tf_op jit(solution)/shard_map/all_to_all | solution.py:917
  97.8 20.8 %collective-permute-start.11 = (bf16[3,128,384]{2,1,0:T(8,128)(2,1)S(1)}, bf16[3,128,384]{2,1,0:T(8,128)(2,1)S(1)}, u32[]{:S(2)}, u32[]{:S(2)}) collective-permute-start(bf16[3,128,384]{2,1,0:T(8,128)(2,1)S(1)} %get-tuple-element.637), channel_id=1, source_target_pairs={{0,8},{4,12},{8,0},{12,4},{16,24},{20,28},{24,16},{28,20},{1,9},{5... | collective-permute-start | bytes 884744 | tf_op jit(solution)/shard_map/ppermute | solution.py:888
  183.4 24.1 %collective-permute-start.22 = (bf16[4,4,176,384]{3,2,1,0:T(8,128)(2,1)}, bf16[4,4,176,384]{3,2,1,0:T(8,128)(2,1)S(1)}, u32[]{:S(2)}, u32[]{:S(2)}) collective-permute-start(bf16[4,4,176,384]{3,2,1,0:T(8,128)(2,1)} %get-tuple-element.374), channel_id=1, source_target_pairs={{0,4},{4,0},{8,12},{12,8},{16,20},{20,16},{24,28},{28,24},{1,5},{5... | collective-permute-start | bytes 6488072 | tf_op jit(solution)/shard_map/ppermute | solution.py:888
  184.3 38.9 %all-to-all-start.3 = ((bf16[4,192,768]{2,1,0:T(8,128)(2,1)}), bf16[4,192,768]{2,1,0:T(8,128)(2,1)}, u32[]{:S(2)}, u32[]{:S(2)}) async-start(bf16[4,192,768]{2,1,0:T(8,128)(2,1)} %get-tuple-element.387), calls=%async_computation.3 | async-start | bytes 2359296 | tf_op jit(solution)/shard_map/all_to_all | solution.py:1196
  224.2 31.2 %collective-permute-start.30 = (bf16[4,176,384]{2,1,0:T(8,128)(2,1)}, bf16[4,176,384]{2,1,0:T(8,128)(2,1)}, u32[]{:S(2)}, u32[]{:S(2)}) collective-permute-start(bf16[4,176,384]{2,1,0:T(8,128)(2,1)} %get-tuple-element.418), channel_id=1, source_target_pairs={{0,24},{4,28},{8,16},{12,20},{16,8},{20,12},{24,0},{28,4},{1,25},{... | collective-permute-start | bytes 1622024 | tf_op jit(solution)/shard_map/ppermute | solution.py:888
  228.9 26.6 %collective-permute-start.27 = (bf16[4,128,384]{2,1,0:T(8,128)(2,1)S(1)}, bf16[4,128,384]{2,1,0:T(8,128)(2,1)S(1)}, u32[]{:S(2)}, u32[]{:S(2)}) collective-permute-start(bf16[4,128,384]{2,1,0:T(8,128)(2,1)S(1)} %pad_maximum_fusion.15), channel_id=1, source_target_pairs={{0,8},{4,12},{8,0},{12,4},{16,24},{20,28},{24,16},{28,20},{1,9},{5... | collective-permute-start | bytes 1179656 | tf_op jit(solution)/shard_map/ppermute | solution.py:888
  230.1 25.4 %collective-permute-start.28 = (bf16[4,128,384]{2,1,0:T(8,128)(2,1)S(1)}, bf16[4,128,384]{2,1,0:T(8,128)(2,1)}, u32[]{:S(2)}, u32[]{:S(2)}) collective-permute-start(bf16[4,128,384]{2,1,0:T(8,128)(2,1)S(1)} %pad_maximum_fusion.16), channel_id=1, source_target_pairs={{0,16},{4,20},{8,24},{12,28},{16,0},{20,4},{24,8},{28,12},{1,17},{... | collective-permute-start | bytes 1179656 | tf_op jit(solution)/shard_map/ppermute | solution.py:888
  230.7 26.4 %collective-permute-start.29 = (bf16[4,128,384]{2,1,0:T(8,128)(2,1)S(1)}, bf16[4,128,384]{2,1,0:T(8,128)(2,1)}, u32[]{:S(2)}, u32[]{:S(2)}) collective-permute-start(bf16[4,128,384]{2,1,0:T(8,128)(2,1)S(1)} %pad_maximum_fusion.17), channel_id=1, source_target_pairs={{0,24},{4,28},{8,16},{12,20},{16,8},{20,12},{24,0},{28,4},{1,25},{... | collective-permute-start | bytes 1179656 | tf_op jit(solution)/shard_map/ppermute | solution.py:888
  264.2 29.0 %all-to-all-start.4 = ((bf16[4,304,384]{2,1,0:T(8,128)(2,1)}), bf16[4,304,384]{2,1,0:T(8,128)(2,1)S(1)}, u32[]{:S(2)}, u32[]{:S(2)}) async-start(bf16[4,304,384]{2,1,0:T(8,128)(2,1)} %pad_maximum_fusion.5), calls=%async_computation.4 | async-start | bytes 1867776 | tf_op jit(solution)/shard_map/all_to_all | solution.py:952
  269.2 24.0 %collective-permute-start.32 = (bf16[4,176,384]{2,1,0:T(8,128)(2,1)}, bf16[4,176,384]{2,1,0:T(8,128)(2,1)}, u32[]{:S(2)}, u32[]{:S(2)}) collective-permute-start(bf16[4,176,384]{2,1,0:T(8,128)(2,1)} %get-tuple-element.437.refs_18_), channel_id=1, source_target_pairs={{0,8},{4,12},{8,0},{12,4},{16,24},{20,28},{24,16},{28,20},{1,9},{5... | collective-permute-start | bytes 1622024 | tf_op jit(solution)/shard_map/ppermute | solution.py:888
  270.4 24.4 %collective-permute-start.33 = (bf16[4,176,384]{2,1,0:T(8,128)(2,1)S(1)}, bf16[4,176,384]{2,1,0:T(8,128)(2,1)}, u32[]{:S(2)}, u32[]{:S(2)}) collective-permute-start(bf16[4,176,384]{2,1,0:T(8,128)(2,1)S(1)} %get-tuple-element.438.refs_19_), channel_id=1, source_target_pairs={{0,16},{4,20},{8,24},{12,28},{16,0},{20,4},{24,8},{28,12},{1,17},{... | collective-permute-start | bytes 1622024 | tf_op jit(solution)/shard_map/ppermute | solution.py:888
  271.6 24.9 %collective-permute-start.34 = (bf16[4,176,384]{2,1,0:T(8,128)(2,1)S(1)}, bf16[4,176,384]{2,1,0:T(8,128)(2,1)}, u32[]{:S(2)}, u32[]{:S(2)}) collective-permute-start(bf16[4,176,384]{2,1,0:T(8,128)(2,1)S(1)} %get-tuple-element.439.refs_20_), channel_id=1, source_target_pairs={{0,24},{4,28},{8,16},{12,20},{16,8},{20,12},{24,0},{28,4},{1,25},{... | collective-permute-start | bytes 1622024 | tf_op jit(solution)/shard_map/ppermute | solution.py:888
  296.5 22.6 %collective-permute-start.35 = (bf16[304,384]{1,0:T(8,128)(2,1)S(1)}, bf16[304,384]{1,0:T(8,128)(2,1)S(1)}, u32[]{:S(2)}, u32[]{:S(2)}) collective-permute-start(bf16[304,384]{1,0:T(8,128)(2,1)S(1)} %add_convert_fusion.16), channel_id=1, source_target_pairs={{0,8},{4,12},{8,0},{12,4},{16,24},{20,28},{24,16},{28,20},{1,9},{5... | collective-permute-start | bytes 700424 | tf_op jit(solution)/shard_map/ppermute | solution.py:888
  297.5 21.7 %collective-permute-start.36 = (bf16[304,384]{1,0:T(8,128)(2,1)S(1)}, bf16[304,384]{1,0:T(8,128)(2,1)S(1)}, u32[]{:S(2)}, u32[]{:S(2)}) collective-permute-start(bf16[304,384]{1,0:T(8,128)(2,1)S(1)} %add_convert_fusion.16), channel_id=1, source_target_pairs={{0,16},{4,20},{8,24},{12,28},{16,0},{20,4},{24,8},{28,12},{1,17},{... | collective-permute-start | bytes 700424 | tf_op jit(solution)/shard_map/ppermute | solution.py:888
  298.7 20.5 %collective-permute-start.37 = (bf16[304,384]{1,0:T(8,128)(2,1)S(1)}, bf16[304,384]{1,0:T(8,128)(2,1)S(1)}, u32[]{:S(2)}, u32[]{:S(2)}) collective-permute-start(bf16[304,384]{1,0:T(8,128)(2,1)S(1)} %add_convert_fusion.16), channel_id=1, source_target_pairs={{0,24},{4,28},{8,16},{12,20},{16,8},{20,12},{24,0},{28,4},{1,25},{... | collective-permute-start | bytes 700424 | tf_op jit(solution)/shard_map/ppermute | solution.py:888
  302.9 20.3 %all-to-all-start.5 = ((bf16[4,176,384]{2,1,0:T(8,128)(2,1)}), bf16[4,176,384]{2,1,0:T(8,128)(2,1)S(1)}, u32[]{:S(2)}, u32[]{:S(2)}) async-start(bf16[4,176,384]{2,1,0:T(8,128)(2,1)} %pad_maximum_fusion.9), calls=%async_computation.5 | async-start | bytes 1081344 | tf_op jit(solution)/shard_map/all_to_all | solution.py:952
  327.5 21.9 %collective-permute-start.42 = (bf16[4,128,384]{2,1,0:T(8,128)(2,1)S(1)}, bf16[4,128,384]{2,1,0:T(8,128)(2,1)S(1)}, u32[]{:S(2)}, u32[]{:S(2)}) collective-permute-start(bf16[4,128,384]{2,1,0:T(8,128)(2,1)S(1)} %pad_maximum_fusion.21), channel_id=1, source_target_pairs={{0,24},{4,28},{8,16},{12,20},{16,8},{20,12},{24,0},{28,4},{1,25},{... | collective-permute-start | bytes 1179656 | tf_op jit(solution)/shard_map/ppermute | solution.py:888
  329.2 20.2 %collective-permute-start.41 = (bf16[4,128,384]{2,1,0:T(8,128)(2,1)S(1)}, bf16[4,128,384]{2,1,0:T(8,128)(2,1)S(1)}, u32[]{:S(2)}, u32[]{:S(2)}) collective-permute-start(bf16[4,128,384]{2,1,0:T(8,128)(2,1)S(1)} %pad_maximum_fusion.20), channel_id=1, source_target_pairs={{0,16},{4,20},{8,24},{12,28},{16,0},{20,4},{24,8},{28,12},{1,17},{... | collective-permute-start | bytes 1179656 | tf_op jit(solution)/shard_map/ppermute | solution.py:888
  (102 other events, 803.2 us)

commit v5 on v4

--- a/solution.py
+++ b/solution.py
@@ -169,9 +169,9 @@
         middle.start((rows, slice(None)))
 
 
-def gelu_parts(v):
-    inner = math.sqrt(2.0 / math.pi) * (v + 0.044715 * (v * v * v))
-    return jnp.tanh(inner)
+def gelu_of(v):
+    rate = math.sqrt(2.0 / math.pi)
+    return v * (0.5 + 0.5 * jnp.tanh(v * (rate + 0.044715 * rate * (v * v))))
 
 
 def fwd_ff_kernel(last, idx, own, rel_a, rel_b, middle, cols, q3, gate_up, q4, h_next, stats, table, normed, act, sem):
@@ -199,12 +199,10 @@
             ups = []
             for piece in (half, half + 2):
                 ups.append(tn(w[at[c], UP_TWO + 192 * piece : UP_TWO + 192 * piece + 192, :], q3.buffer[c]))
-            gate, up = ups
+            gate, up = ups[0], ups[1].astype(BF16)
             gate_up.buffer[c, 384 * half : 384 * half + 384, :] = gate.astype(BF16)
-            gate_up.buffer[c, 768 + 384 * half : 768 + 384 * half + 384, :] = up.astype(BF16)
-            act[384 * half : 384 * half + 384, :] = (
-                0.5 * gate * (1.0 + gelu_parts(gate)) * up
-            ).astype(BF16)
+            gate_up.buffer[c, 768 + 384 * half : 768 + 384 * half + 384, :] = up
+            act[384 * half : 384 * half + 384, :] = gelu_of(gate).astype(BF16) * up
         gate_up.start(c)
         inner = (
             tn(w[at[c], DOWN_ONE : DOWN_ONE + 384, 0:192], act[0:384, :])
@@ -271,17 +269,15 @@
         for half in range(2):
             span = slice(192 * half, 192 * half + 192)
             gate = gate_up.buffer[b, 384 * half : 384 * half + 384, :].astype(F32)
-            up = gate_up.buffer[b, 768 + 384 * half : 768 + 384 * half + 384, :].astype(F32)
-            ga = nn(w[at[b], DOWN_ONE : DOWN_ONE + 384, span], gi4[b])
+            up = gate_up.buffer[b, 768 + 384 * half : 768 + 384 * half + 384, :]
+            ga = nn(w[at[b], DOWN_ONE : DOWN_ONE + 384, span], gi4[b]).astype(BF16)
             square = gate * gate
-            t = jnp.tanh(rate * gate * (1.0 + 0.044715 * square))
-            rise = 0.5 * (1.0 + t)
-            gelu = gate * rise
-            slope = rise + 0.5 * gelu_slope(gate, square, t, rate)
-            act = (gelu * up).astype(BF16)
-            g_w[at[b], DOWN_ONE : DOWN_ONE + 384, span] = nt(act, gi4[b]).astype(BF16)
-            g_gu[384 * half : 384 * half + 384, :] = (ga * up * slope).astype(BF16)
-            g_gu[768 + 384 * half : 768 + 384 * half + 384, :] = (ga * gelu).astype(BF16)
+            rise = 0.5 + 0.5 * jnp.tanh(gate * (rate + 0.044715 * rate * square))
+            gelu = (gate * rise).astype(BF16)
+            slope = rise * (1.0 + (1.0 - rise) * (gate * (2.0 * rate + 6.0 * 0.044715 * rate * square)))
+            g_w[at[b], DOWN_ONE : DOWN_ONE + 384, span] = nt(gelu * up, gi4[b]).astype(BF16)
+            g_gu[384 * half : 384 * half + 384, :] = ga * (up * slope.astype(BF16))
+            g_gu[768 + 384 * half : 768 + 384 * half + 384, :] = ga * gelu
         gq = None
         for piece in range(4):
             rows = slice(UP_TWO + 192 * piece, UP_TWO + 192 * piece + 192)
@@ -297,10 +293,6 @@
         at, middle.wait(), mean, inv, cols.wait(), GAIN_TWO, w, slice(UP_ONE, UP_ONE + 192), slice(0, 192), gi3, g_n, g_w, small, 1, g_top, g_mid
     )
     finish()
-
-
-def gelu_slope(gate, square, t, rate):
-    return gate * (1.0 - t * t) * (rate * (1.0 + 3.0 * 0.044715 * square))
 
 
 def row_sums(place, values):
@@ -863,7 +855,7 @@
             in_specs=[ANY if spec is EARLY else spec for spec in in_specs] + [ANY] * len(deps),
             out_specs=[ANY if spec is LATE else spec for spec in out_specs],
             scratch_shapes=list(scratch) + buffers,
-            compiler_params=pltpu.CompilerParams(vmem_limit_bytes=58 << 20),
+            compiler_params=pltpu.CompilerParams(vmem_limit_bytes=54 << 20),
             cost_estimate=pl.CostEstimate(flops=int(micros * 1e9), bytes_accessed=1 << 20, transcendentals=0),
         )(*arrays, *deps)
         return made if len(outs) > 1 else made[0]

time: 390 us -> 387 us (level)
    unnamed x129 -> x137, local copies, waits for them, and re-layouts: 10.3 us -> 9.72 us
  transfers between devices with their start and end apart: 64 -> 64, of which waited for: 24 -> 25; matrix products, arithmetic and copies ran while one was open for 7% -> 7% of each run, Pallas kernels for 39% -> 39%
where the time goes in v5:
time: 387 us; the launch traced here: 380 us
  Pallas kernels  186 us (48%)
  starting transfers between devices  94.8 us (24%)
  waiting for transfers between devices  56.4 us (15%)
  local copies, waits for them, and re-layouts  21.9 us (6%)
  other arithmetic  16.1 us (4%)
    pallas_call x14, Pallas kernels, run(): pl.pallas_call(body, out_shape=outs, in_specs=[ANY if spec is EARLY else...  173 us
    ppermute x46, starting transfers between devices, wide_shift(): lax.ppermute(x, 'wide', [(i, i ^ mask) for i in range(lax.axis_size('wide...  41.3 us
    ppermute x46, waiting for transfers between devices, wide_shift(): lax.ppermute(x, 'wide', [(i, i ^ mask) for i in range(lax.axis_size('wide...  29.6 us
    ppermute x12, starting transfers between devices, narrow_shift(): lax.ppermute(x, 'narrow', [(i, (i + by) % narrow) for i in range(narrow)])  24.9 us
    ppermute x12, waiting for transfers between devices, narrow_shift(): lax.ppermute(x, 'narrow', [(i, (i + by) % narrow) for i in range(narrow)])  19.5 us
    all_to_all x3, starting transfers between devices, others_at_once(): lax.all_to_all(pieces, 'narrow', split_axis=0, concat_axis=0, tiled=True)  14.1 us
    pallas_call x3, Pallas kernels, finish(): pl.pallas_call(functools.partial(finish_kernel, layer, names), grid=(1,),...  12.3 us
    all_to_all x2, starting transfers between devices, blocks_at_once(): lax.all_to_all(table, 'narrow', split_axis=0, concat_axis=0, tiled=True)  10.2 us
  transfers between devices with their start and end apart: 64, of which 25 were waited for; matrix products, arithmetic and copies ran while one was open for 7% of the time, Pallas kernels for 39%

profile of v5, /device:TPU:0, one launch (start us, length us, event | category | flops | bytes accessed | tf_op | source)
XLA Modules:
  0.0 379.7 jit_solution(3932853942407798686)
XLA Ops:
  32.0 3.6 shard_map.411
  38.2 3.6 all-to-all-start.1
  45.4 3.9 %collective-permute-start.5 = (bf16[192,768]{1,0:T(8,128)(2,1)S(1)}, bf16[192,768]{1,0:T(8,128)(2,1)}, u32[]{:S(2)}, u32[]{:S(2)}) collective-permute-start(bf16[192,768]{1,0:T(8,128)(2,1)S(1)} %get-tuple-element.284), channel_id=1, source_target_pairs={{0,3},{1,0},{2,1},{3,2},{4,7},{5,4},{6,5},{7,6},{8,11},{9,8},{10,9... | collective-permute-start | bytes 884744 | tf_op jit(solution)/shard_map/ppermute | solution.py:885
  51.7 6.5 %collective-permute-done.3 = bf16[3,128,384]{2,1,0:T(8,128)(2,1)S(1)} collective-permute-done((bf16[3,128,384]{2,1,0:T(8,128)(2,1)S(1)}, bf16[3,128,384]{2,1,0:T(8,128)(2,1)S(1)}, u32[]{:S(2)}, u32[]{:S(2)}) %collective-permute-start.3) | collective-permute-done | bytes 294944 | tf_op jit(solution)/shard_map/ppermute | solution.py:880
  67.4 7.0 %all-to-all-start.2 = ((bf16[4,304,384]{2,1,0:T(8,128)(2,1)}), bf16[4,304,384]{2,1,0:T(8,128)(2,1)S(1)}, u32[]{:S(2)}, u32[]{:S(2)}) async-start(bf16[4,304,384]{2,1,0:T(8,128)(2,1)} %stack.241), calls=%async_computation.2 | async-start | bytes 1867776 | tf_op jit(solution)/shard_map/all_to_all | solution.py:909
  74.5 17.9 %shard_map.412 = (f32[768,768]{1,0:T(8,128)}, bf16[4,384,768]{2,1,0:T(8,128)(2,1)}, bf16[4,384,768]{2,1,0:T(8,128)(2,1)}, bf16[768,768]{1,0:T(8,128)(2,1)}, bf16...) custom-call(s32[2]{0:T(128)} %pad_add_fusion.refs_0_.idx, ...), custom_call_target="tpu_custom_call" | custom-call | flops 17999998976 | bytes 1048576 | tf_op jit(solution)/shard_map/pallas_call | solution.py:852
  93.9 3.6 all-to-all-done.2
  105.3 12.6 %shard_map.413 = (bf16[4,192,768]{2,1,0:T(8,128)(2,1)}, bf16[4,1536,768]{2,1,0:T(8,128)(2,1)}, bf16[4,192,768]{2,1,0:T(8,128)(2,1)}, f32[768,768]{1,0:T(8,128)},...) custom-call(s32[2]{0:T(128)} %pad_add_fusion.refs_0_.idx, bf16[1408,384]{1,0:T(8,128)(2,1)} %get-tuple-element.311.refs_1_, ...), custom_call_target="tpu_custom_call" | custom-call | flops 15000000512 | bytes 1048576 | tf_op jit(solution)/shard_map/pallas_call | solution.py:852
  125.6 14.8 %shard_map.414 = (bf16[4,384,768]{2,1,0:T(8,128)(2,1)}, bf16[4,384,768]{2,1,0:T(8,128)(2,1)}, bf16[768,768]{1,0:T(8,128)(2,1)}, bf16[768,768]{1,0:T(8,128)(2,1)}...) custom-call(s32[2]{0:T(128)} %pad_add_fusion.refs_0_.idx, ...), custom_call_target="tpu_custom_call" | custom-call | flops 17999998976 | bytes 1048576 | tf_op jit(solution)/shard_map/pallas_call | solution.py:852
  147.2 12.1 %shard_map.415 = (bf16[4,192,768]{2,1,0:T(8,128)(2,1)}, bf16[4,1536,768]{2,1,0:T(8,128)(2,1)}, bf16[4,192,768]{2,1,0:T(8,128)(2,1)}, bf16[4,192,768]{2,1,0:T(8,1...) custom-call(s32[2]{0:T(128)} %pad_add_fusion.refs_0_.idx, bf16[1408,384]{1,0:T(8,128)(2,1)} %get-tuple-element.341.refs_1_, ...), custom_call_target="tpu_custom_call" | custom-call | flops 15000000512 | bytes 1048576 | tf_op jit(solution)/shard_map/pallas_call | solution.py:852
  159.4 21.9 %shard_map.416 = (f32[768,768]{1,0:T(8,128)}, bf16[4,4,176,384]{3,2,1,0:T(8,128)(2,1)}, bf16[4,4,176,384]{3,2,1,0:T(8,128)(2,1)}, f32[4,16,192]{2,1,0:T(8,128)}) custom-call(s32[2]{0:T(128)} %pad_add_fusion.refs_0_.idx, bf16[4,1408,384]{2,1,0:T(8,128)(2,1)} %get-tuple-element.346.refs_1_, bf16[192,768]{1,0:T(8,128)(2,1)} %get-tuple-element.352.refs_2_, ...), custom_call_target="tpu_custom_call" | custom-call | flops 27000000512 | bytes 1048576 | tf_op jit(solution)/shard_map/pallas_call | solution.py:852
  182.1 4.3 %all-to-all-start.3 = ((bf16[4,192,768]{2,1,0:T(8,128)(2,1)}), bf16[4,192,768]{2,1,0:T(8,128)(2,1)}, u32[]{:S(2)}, u32[]{:S(2)}) async-start(bf16[4,192,768]{2,1,0:T(8,128)(2,1)} %get-tuple-element.387), calls=%async_computation.3 | async-start | bytes 2359296 | tf_op jit(solution)/shard_map/all_to_all | solution.py:1188
  186.4 18.9 %shard_map.417 = (bf16[4,384,768]{2,1,0:T(8,128)(2,1)}, bf16[4,4,48,384]{3,2,1,0:T(8,128)(2,1)}, bf16[4,4,48,384]{3,2,1,0:T(8,128)(2,1)}) custom-call(s32[2]{0:T(128)} %pad_add_fusion.refs_0_.idx, bf16[4,1024,384]{2,1,0:T(8,128)(2,1)} %get-tuple-element.331.refs_1_, f32[768,768]{1,0:T(8,128)} %get-tuple-element.363.refs_2_.refs_3_, ...), custom_call_target="tpu_custom_call" | custom-call | flops 23000000512 | bytes 1048576 | tf_op jit(solution)/shard_map/pallas_call | solution.py:852
  209.5 11.3 %shard_map.418 = (f32[768,768]{1,0:T(8,128)}, bf16[4,4,80,384]{3,2,1,0:T(8,128)(2,1)}, bf16[4,4,80,384]{3,2,1,0:T(8,128)(2,1)}) custom-call(s32[2]{0:T(128)} %pad_add_fusion.refs_0_.idx, bf16[4,1024,384]{2,1,0:T(8,128)(2,1)} %get-tuple-element.331.refs_1_, bf16[4,384,768]{2,1,0:T(8,128)(2,1)} %get-tuple-element.375.refs_2_, ...), custom_call_target="tpu_custom_call" | custom-call | flops 12000000000 | bytes 1048576 | tf_op jit(solution)/shard_map/pallas_call | solution.py:852
  230.4 21.7 %shard_map.420 = (f32[768,768]{1,0:T(8,128)}, bf16[4,4,176,384]{3,2,1,0:T(8,128)(2,1)}, bf16[4,4,176,384]{3,2,1,0:T(8,128)(2,1)}, f32[4,16,192]{2,1,0:T(8,128)}) custom-call(s32[2]{0:T(128)} %pad_add_fusion.refs_0_.idx, bf16[4,1408,384]{2,1,0:T(8,128)(2,1)} %get-tuple-element.393.refs_1_, f32[768,768]{1,0:T(8,128)} %get-tuple-element.403.refs_2_, ...), custom_call_target="tpu_custom_call" | custom-call | flops 27000000512 | bytes 1048576 | tf_op jit(solution)/shard_map/pallas_call | solution.py:852
  261.0 5.4 %all-to-all-start.4 = ((bf16[4,304,384]{2,1,0:T(8,128)(2,1)}), bf16[4,304,384]{2,1,0:T(8,128)(2,1)S(1)}, u32[]{:S(2)}, u32[]{:S(2)}) async-start(bf16[4,304,384]{2,1,0:T(8,128)(2,1)} %pad_maximum_fusion.5), calls=%async_computation.4 | async-start | bytes 1867776 | tf_op jit(solution)/shard_map/all_to_all | solution.py:944
  270.0 18.4 %shard_map.421 = (bf16[4,384,768]{2,1,0:T(8,128)(2,1)}, bf16[4,4,48,384]{3,2,1,0:T(8,128)(2,1)}, bf16[4,4,48,384]{3,2,1,0:T(8,128)(2,1)}) custom-call(s32[2]{0:T(128)} %pad_add_fusion.refs_0_.idx, bf16[4,1024,384]{2,1,0:T(8,128)(2,1)} %get-tuple-element.392.refs_1_, f32[768,768]{1,0:T(8,128)} %get-tuple-element.419.refs_2_.refs_3_, ...), custom_call_target="tpu_custom_call" | custom-call | flops 23000000512 | bytes 1048576 | tf_op jit(solution)/shard_map/pallas_call | solution.py:852
  299.9 4.8 %all-to-all-start.5 = ((bf16[4,176,384]{2,1,0:T(8,128)(2,1)}), bf16[4,176,384]{2,1,0:T(8,128)(2,1)S(1)}, u32[]{:S(2)}, u32[]{:S(2)}) async-start(bf16[4,176,384]{2,1,0:T(8,128)(2,1)} %pad_maximum_fusion.9), calls=%async_computation.5 | async-start | bytes 1081344 | tf_op jit(solution)/shard_map/all_to_all | solution.py:944
  304.7 11.4 %shard_map.422 = (bf16[4,192,768]{2,1,0:T(8,128)(2,1)}, bf16[4,4,80,384]{3,2,1,0:T(8,128)(2,1)}, bf16[4,4,80,384]{3,2,1,0:T(8,128)(2,1)}) custom-call(s32[2]{0:T(128)} %pad_add_fusion.refs_0_.idx, bf16[4,1024,384]{2,1,0:T(8,128)(2,1)} %get-tuple-element.392.refs_1_, bf16[4,384,768]{2,1,0:T(8,128)(2,1)} %get-tuple-element.444.refs_2_, ...), custom_call_target="tpu_custom_call" | custom-call | flops 12000000000 | bytes 1048576 | tf_op jit(solution)/shard_map/pallas_call | solution.py:852
  330.8 4.7 %shard_map.423 = (f32[2,288,128]{2,1,0:T(8,128)}, f32[2,2304,128]{2,1,0:T(8,128)}, f32[2,1152,128]{2,1,0:T(8,128)}, f32[2,288,128]{2,1,0:T(8,128)}, f32[2,576,12...) custom-call(s32[2]{0:T(128)} %pad_add_fusion.refs_0_.idx, ...), custom_call_target="tpu_custom_call" | custom-call | flops 4000000000 | bytes 1048576 | tf_op jit(solution)/shard_map/pallas_call | solution.py:1166
  335.5 10.8 %collective-permute-done.45.refs_3_ = bf16[192,768]{1,0:T(8,128)(2,1)S(1)} collective-permute-done((bf16[192,768]{1,0:T(8,128)(2,1)S(1)}, bf16[192,768]{1,0:T(8,128)(2,1)S(1)}, u32[]{:S(2)}, u32[]{:S(2)}) %collective-permute-start.45) | collective-permute-done | bytes 294944 | tf_op jit(solution)/shard_map/ppermute | solution.py:885
  362.0 3.5 collective-permute-start.56
  367.5 3.9 %shard_map.424 = (f32[2,288,128]{2,1,0:T(8,128)}, f32[2,2304,128]{2,1,0:T(8,128)}, f32[2,1152,128]{2,1,0:T(8,128)}, f32[2,288,128]{2,1,0:T(8,128)}) custom-call(s32[2]{0:T(128)} %pad_add_fusion.refs_0_.idx, bf16[4,176,384]{2,1,0:T(8,128)(2,1)} %copy-done.22, ...), custom_call_target="tpu_custom_call", output_to_operand_aliasing={{0}: (3, {}), {1}: (4, {}), {2}: (5, {}), {3}: (6, {})} | custom-call | flops 4000000000 | bytes 1048576 | tf_op jit(solution)/shard_map/pallas_call | solution.py:1166
  375.9 3.7 shard_map.426
  (329 shorter events, 147.1 us)
Async XLA Ops:
  2.8 25.7 %collective-permute-start = (bf16[192,768]{1,0:T(8,128)(2,1)S(1)}, bf16[192,768]{1,0:T(8,128)(2,1)}, u32[]{:S(2)}, u32[]{:S(2)}) collective-permute-start(bf16[192,768]{1,0:T(8,128)(2,1)S(1)} %get-tuple-element.623), channel_id=1, source_target_pairs={{0,1},{1,2},{2,3},{3,0},{4,5},{5,6},{6,7},{7,4},{8,9},{9,10},{10,1... | collective-permute-start | bytes 884744 | tf_op jit(solution)/shard_map/ppermute | solution.py:885
  5.9 26.1 %collective-permute-start.1 = (bf16[192,768]{1,0:T(8,128)(2,1)S(1)}, bf16[192,768]{1,0:T(8,128)(2,1)}, u32[]{:S(2)}, u32[]{:S(2)}) collective-permute-start(bf16[192,768]{1,0:T(8,128)(2,1)S(1)} %get-tuple-element.622), channel_id=1, source_target_pairs={{0,2},{1,3},{2,0},{3,1},{4,6},{5,7},{6,4},{7,5},{8,10},{9,11},{10,... | collective-permute-start | bytes 884744 | tf_op jit(solution)/shard_map/ppermute | solution.py:885
  38.2 20.2 %all-to-all-start.1 = ((bf16[4,176,384]{2,1,0:T(8,128)(2,1)}), bf16[4,176,384]{2,1,0:T(8,128)(2,1)S(1)}, u32[]{:S(2)}, u32[]{:S(2)}) async-start(bf16[4,176,384]{2,1,0:T(8,128)(2,1)} %stack.239), calls=%async_computation.1 | async-start | bytes 1081344 | tf_op jit(solution)/shard_map/all_to_all | solution.py:909
  63.5 28.9 %collective-permute-start.7 = (bf16[3,176,384]{2,1,0:T(8,128)(2,1)S(1)}, bf16[3,176,384]{2,1,0:T(8,128)(2,1)S(1)}, u32[]{:S(2)}, u32[]{:S(2)}) collective-permute-start(bf16[3,176,384]{2,1,0:T(8,128)(2,1)S(1)} %pad_maximum_fusion.13), channel_id=1, source_target_pairs={{0,8},{4,12},{8,0},{12,4},{16,24},{20,28},{24,16},{28,20},{1,9},{5... | collective-permute-start | bytes 1216520 | tf_op jit(solution)/shard_map/ppermute | solution.py:880
  65.0 27.5 %collective-permute-start.8 = (bf16[3,176,384]{2,1,0:T(8,128)(2,1)S(1)}, bf16[3,176,384]{2,1,0:T(8,128)(2,1)}, u32[]{:S(2)}, u32[]{:S(2)}) collective-permute-start(bf16[3,176,384]{2,1,0:T(8,128)(2,1)S(1)} %pad_maximum_fusion.13), channel_id=1, source_target_pairs={{0,16},{4,20},{8,24},{12,28},{16,0},{20,4},{24,8},{28,12},{1,17},{... | collective-permute-start | bytes 1216520 | tf_op jit(solution)/shard_map/ppermute | solution.py:880
  66.5 25.9 %collective-permute-start.9 = (bf16[3,176,384]{2,1,0:T(8,128)(2,1)S(1)}, bf16[3,176,384]{2,1,0:T(8,128)(2,1)}, u32[]{:S(2)}, u32[]{:S(2)}) collective-permute-start(bf16[3,176,384]{2,1,0:T(8,128)(2,1)S(1)} %pad_maximum_fusion.13), channel_id=1, source_target_pairs={{0,24},{4,28},{8,16},{12,20},{16,8},{20,12},{24,0},{28,4},{1,25},{... | collective-permute-start | bytes 1216520 | tf_op jit(solution)/shard_map/ppermute | solution.py:880
  67.4 30.0 %all-to-all-start.2 = ((bf16[4,304,384]{2,1,0:T(8,128)(2,1)}), bf16[4,304,384]{2,1,0:T(8,128)(2,1)S(1)}, u32[]{:S(2)}, u32[]{:S(2)}) async-start(bf16[4,304,384]{2,1,0:T(8,128)(2,1)} %stack.241), calls=%async_computation.2 | async-start | bytes 1867776 | tf_op jit(solution)/shard_map/all_to_all | solution.py:909
  181.3 24.1 %collective-permute-start.22 = (bf16[4,4,176,384]{3,2,1,0:T(8,128)(2,1)}, bf16[4,4,176,384]{3,2,1,0:T(8,128)(2,1)S(1)}, u32[]{:S(2)}, u32[]{:S(2)}) collective-permute-start(bf16[4,4,176,384]{3,2,1,0:T(8,128)(2,1)} %get-tuple-element.374), channel_id=1, source_target_pairs={{0,4},{4,0},{8,12},{12,8},{16,20},{20,16},{24,28},{28,24},{1,5},{5... | collective-permute-start | bytes 6488072 | tf_op jit(solution)/shard_map/ppermute | solution.py:880
  182.1 38.9 %all-to-all-start.3 = ((bf16[4,192,768]{2,1,0:T(8,128)(2,1)}), bf16[4,192,768]{2,1,0:T(8,128)(2,1)}, u32[]{:S(2)}, u32[]{:S(2)}) async-start(bf16[4,192,768]{2,1,0:T(8,128)(2,1)} %get-tuple-element.387), calls=%async_computation.3 | async-start | bytes 2359296 | tf_op jit(solution)/shard_map/all_to_all | solution.py:1188
  222.2 29.9 %collective-permute-start.30 = (bf16[4,176,384]{2,1,0:T(8,128)(2,1)}, bf16[4,176,384]{2,1,0:T(8,128)(2,1)S(1)}, u32[]{:S(2)}, u32[]{:S(2)}) collective-permute-start(bf16[4,176,384]{2,1,0:T(8,128)(2,1)} %get-tuple-element.418), channel_id=1, source_target_pairs={{0,24},{4,28},{8,16},{12,20},{16,8},{20,12},{24,0},{28,4},{1,25},{... | collective-permute-start | bytes 1622024 | tf_op jit(solution)/shard_map/ppermute | solution.py:880
  226.8 25.2 %collective-permute-start.27 = (bf16[4,128,384]{2,1,0:T(8,128)(2,1)S(1)}, bf16[4,128,384]{2,1,0:T(8,128)(2,1)S(1)}, u32[]{:S(2)}, u32[]{:S(2)}) collective-permute-start(bf16[4,128,384]{2,1,0:T(8,128)(2,1)S(1)} %pad_maximum_fusion.15), channel_id=1, source_target_pairs={{0,8},{4,12},{8,0},{12,4},{16,24},{20,28},{24,16},{28,20},{1,9},{5... | collective-permute-start | bytes 1179656 | tf_op jit(solution)/shard_map/ppermute | solution.py:880
  228.0 24.1 %collective-permute-start.28 = (bf16[4,128,384]{2,1,0:T(8,128)(2,1)S(1)}, bf16[4,128,384]{2,1,0:T(8,128)(2,1)}, u32[]{:S(2)}, u32[]{:S(2)}) collective-permute-start(bf16[4,128,384]{2,1,0:T(8,128)(2,1)S(1)} %pad_maximum_fusion.16), channel_id=1, source_target_pairs={{0,16},{4,20},{8,24},{12,28},{16,0},{20,4},{24,8},{28,12},{1,17},{... | collective-permute-start | bytes 1179656 | tf_op jit(solution)/shard_map/ppermute | solution.py:880
  228.6 26.4 %collective-permute-start.29 = (bf16[4,128,384]{2,1,0:T(8,128)(2,1)S(1)}, bf16[4,128,384]{2,1,0:T(8,128)(2,1)}, u32[]{:S(2)}, u32[]{:S(2)}) collective-permute-start(bf16[4,128,384]{2,1,0:T(8,128)(2,1)S(1)} %pad_maximum_fusion.17), channel_id=1, source_target_pairs={{0,24},{4,28},{8,16},{12,20},{16,8},{20,12},{24,0},{28,4},{1,25},{... | collective-permute-start | bytes 1179656 | tf_op jit(solution)/shard_map/ppermute | solution.py:880
  261.0 28.7 %all-to-all-start.4 = ((bf16[4,304,384]{2,1,0:T(8,128)(2,1)}), bf16[4,304,384]{2,1,0:T(8,128)(2,1)S(1)}, u32[]{:S(2)}, u32[]{:S(2)}) async-start(bf16[4,304,384]{2,1,0:T(8,128)(2,1)} %pad_maximum_fusion.5), calls=%async_computation.4 | async-start | bytes 1867776 | tf_op jit(solution)/shard_map/all_to_all | solution.py:944
  266.4 23.4 %collective-permute-start.32 = (bf16[4,176,384]{2,1,0:T(8,128)(2,1)}, bf16[4,176,384]{2,1,0:T(8,128)(2,1)}, u32[]{:S(2)}, u32[]{:S(2)}) collective-permute-start(bf16[4,176,384]{2,1,0:T(8,128)(2,1)} %get-tuple-element.437.refs_18_), channel_id=1, source_target_pairs={{0,8},{4,12},{8,0},{12,4},{16,24},{20,28},{24,16},{28,20},{1,9},{5... | collective-permute-start | bytes 1622024 | tf_op jit(solution)/shard_map/ppermute | solution.py:880
  267.6 24.2 %collective-permute-start.33 = (bf16[4,176,384]{2,1,0:T(8,128)(2,1)S(1)}, bf16[4,176,384]{2,1,0:T(8,128)(2,1)}, u32[]{:S(2)}, u32[]{:S(2)}) collective-permute-start(bf16[4,176,384]{2,1,0:T(8,128)(2,1)S(1)} %get-tuple-element.438.refs_19_), channel_id=1, source_target_pairs={{0,16},{4,20},{8,24},{12,28},{16,0},{20,4},{24,8},{28,12},{1,17},{... | collective-permute-start | bytes 1622024 | tf_op jit(solution)/shard_map/ppermute | solution.py:880
  268.8 24.5 %collective-permute-start.34 = (bf16[4,176,384]{2,1,0:T(8,128)(2,1)S(1)}, bf16[4,176,384]{2,1,0:T(8,128)(2,1)}, u32[]{:S(2)}, u32[]{:S(2)}) collective-permute-start(bf16[4,176,384]{2,1,0:T(8,128)(2,1)S(1)} %get-tuple-element.439.refs_20_), channel_id=1, source_target_pairs={{0,24},{4,28},{8,16},{12,20},{16,8},{20,12},{24,0},{28,4},{1,25},{... | collective-permute-start | bytes 1622024 | tf_op jit(solution)/shard_map/ppermute | solution.py:880
  293.5 22.6 %collective-permute-start.35 = (bf16[304,384]{1,0:T(8,128)(2,1)S(1)}, bf16[304,384]{1,0:T(8,128)(2,1)S(1)}, u32[]{:S(2)}, u32[]{:S(2)}) collective-permute-start(bf16[304,384]{1,0:T(8,128)(2,1)S(1)} %add_convert_fusion.16), channel_id=1, source_target_pairs={{0,8},{4,12},{8,0},{12,4},{16,24},{20,28},{24,16},{28,20},{1,9},{5... | collective-permute-start | bytes 700424 | tf_op jit(solution)/shard_map/ppermute | solution.py:880
  294.5 21.6 %collective-permute-start.36 = (bf16[304,384]{1,0:T(8,128)(2,1)S(1)}, bf16[304,384]{1,0:T(8,128)(2,1)S(1)}, u32[]{:S(2)}, u32[]{:S(2)}) collective-permute-start(bf16[304,384]{1,0:T(8,128)(2,1)S(1)} %add_convert_fusion.16), channel_id=1, source_target_pairs={{0,16},{4,20},{8,24},{12,28},{16,0},{20,4},{24,8},{28,12},{1,17},{... | collective-permute-start | bytes 700424 | tf_op jit(solution)/shard_map/ppermute | solution.py:880
  295.7 20.5 %collective-permute-start.37 = (bf16[304,384]{1,0:T(8,128)(2,1)S(1)}, bf16[304,384]{1,0:T(8,128)(2,1)S(1)}, u32[]{:S(2)}, u32[]{:S(2)}) collective-permute-start(bf16[304,384]{1,0:T(8,128)(2,1)S(1)} %add_convert_fusion.16), channel_id=1, source_target_pairs={{0,24},{4,28},{8,16},{12,20},{16,8},{20,12},{24,0},{28,4},{1,25},{... | collective-permute-start | bytes 700424 | tf_op jit(solution)/shard_map/ppermute | solution.py:880
  297.0 20.2 %collective-permute-start.39 = (bf16[4,4,48,384]{3,2,1,0:T(8,128)(2,1)}, bf16[4,4,48,384]{3,2,1,0:T(8,128)(2,1)S(1)}, u32[]{:S(2)}, u32[]{:S(2)}) collective-permute-start(bf16[4,4,48,384]{3,2,1,0:T(8,128)(2,1)} %get-tuple-element.463), channel_id=1, source_target_pairs={{0,4},{4,0},{8,12},{12,8},{16,20},{20,16},{24,28},{28,24},{1,5},{5... | collective-permute-start | bytes 1769480 | tf_op jit(solution)/shard_map/ppermute | solution.py:880
  299.9 20.3 %all-to-all-start.5 = ((bf16[4,176,384]{2,1,0:T(8,128)(2,1)}), bf16[4,176,384]{2,1,0:T(8,128)(2,1)S(1)}, u32[]{:S(2)}, u32[]{:S(2)}) async-start(bf16[4,176,384]{2,1,0:T(8,128)(2,1)} %pad_maximum_fusion.9), calls=%async_computation.5 | async-start | bytes 1081344 | tf_op jit(solution)/shard_map/all_to_all | solution.py:944
  324.5 21.9 %collective-permute-start.42 = (bf16[4,128,384]{2,1,0:T(8,128)(2,1)S(1)}, bf16[4,128,384]{2,1,0:T(8,128)(2,1)S(1)}, u32[]{:S(2)}, u32[]{:S(2)}) collective-permute-start(bf16[4,128,384]{2,1,0:T(8,128)(2,1)S(1)} %pad_maximum_fusion.21), channel_id=1, source_target_pairs={{0,24},{4,28},{8,16},{12,20},{16,8},{20,12},{24,0},{28,4},{1,25},{... | collective-permute-start | bytes 1179656 | tf_op jit(solution)/shard_map/ppermute | solution.py:880
  326.2 20.2 %collective-permute-start.41 = (bf16[4,128,384]{2,1,0:T(8,128)(2,1)S(1)}, bf16[4,128,384]{2,1,0:T(8,128)(2,1)S(1)}, u32[]{:S(2)}, u32[]{:S(2)}) collective-permute-start(bf16[4,128,384]{2,1,0:T(8,128)(2,1)S(1)} %pad_maximum_fusion.20), channel_id=1, source_target_pairs={{0,16},{4,20},{8,24},{12,28},{16,0},{20,4},{24,8},{28,12},{1,17},{... | collective-permute-start | bytes 1179656 | tf_op jit(solution)/shard_map/ppermute | solution.py:880
  (106 other events, 810.6 us)
